TPU v7x, 256 devices: a whole 4x4x8 slice. The times are simulated.
256 devices in a mesh: outer: 16 (over y_lo, x, core), inner: 16 (over z, y_hi).
Axes of the slice: x: 4, y: 4 (y_hi: 2, y_lo: 2; y = y_hi * 2 + y_lo), z: 8, core: 2. Of those that a mesh axis runs over, the one named last changes fastest.
Arguments:
- queries: bfloat16 [65536, 1536], P(('outer', 'inner')), may hold values from -6 to 6
- key_rows: bfloat16 [65536, 1536], P(('outer', 'inner')), may hold values from -6 to 6
- values: bfloat16 [65536, 1536], P(('outer', 'inner')), may hold values from -6 to 6
- out_grads: bfloat16 [65536, 1536], P(('outer', 'inner')), may hold values from -96 to 96
- offsets: int32 [8], replicated, may hold values from 0 to 127, as said below
Outputs:
- grad_queries: bfloat16 [65536, 1536], P(('outer', 'inner'))
- grad_keys: bfloat16 [65536, 1536], P(('outer', 'inner'))
- grad_values: bfloat16 [65536, 1536], P(('outer', 'inner'))
Inputs may be any that keep to these rules, and one draw needn't show every extreme that they name: offsets[j] is below 4 for j < 5 and below 128 for the others.
All inputs are finite; a program needn't handle non-finite values.
Results may differ from a plain program's by a relative error of at most 0.0057.
The roundings to bfloat16 on the way count: a program that leaves them out, or rounds other values in their place, can miss the bound.
Values may be sent and summed in bfloat16 or wider, within the bound.
No kernel may reach another device: no remote copies, remote signals or barrier semaphores. Data moves between devices by JAX's collectives and lax.ppermute only.
A program may use at most 64 MiB of HBM per device.

v0:
```python
import math

import jax
import jax.numpy as jnp
from jax import lax
from jax.sharding import PartitionSpec as P

HEAD_DIM = 128
H_NEAR = 4
H_MID = 5
R_MID = 4
R_WIDE = 128


def select_rows(block, head_offsets, stride):
    row_number, columns = block.shape
    head_count = head_offsets.shape[0]
    shaped = block.reshape(row_number // stride, stride, head_count, columns // head_count)
    chosen = jnp.arange(stride, dtype=jnp.int32)[:, None] == head_offsets[None, :]
    masked = jnp.where(chosen[None, :, :, None], shaped, jnp.zeros((), block.dtype))
    return jnp.sum(masked, axis=1)


def spread_rows(picked, head_offsets, stride):
    picked_rows, head_count, head_depth = picked.shape
    chosen = jnp.arange(stride, dtype=jnp.int32)[:, None] == head_offsets[None, :]
    placed = jnp.where(chosen[None, :, :, None], picked[:, None], jnp.zeros((), picked.dtype))
    return placed.reshape(picked_rows * stride, head_count * head_depth)


def score_block(query_row_block, key_tile_block):
    score_scale = 1.0 / math.sqrt(query_row_block.shape[-1])
    return (
        jnp.einsum(
            "agk,igk->gai", query_row_block, key_tile_block, preferred_element_type=jnp.float32
        )
        * score_scale
    )


def score_gradients(weights, product_gradients, row_dots, score_scale):
    weights_bfloat = weights.astype(jnp.bfloat16)
    gradients_bfloat = (weights * (product_gradients - row_dots) * score_scale).astype(jnp.bfloat16)
    return (weights_bfloat, gradients_bfloat)


def rows_with_stats(query_row_block, key_tile_block, value_tile_block, gradient_rows):
    score_scale = 1.0 / math.sqrt(query_row_block.shape[-1])
    logit_scores = score_block(query_row_block, key_tile_block)
    row_max = jnp.max(logit_scores, axis=2, keepdims=True)
    exponent = jnp.exp(logit_scores - row_max)
    row_total = jnp.sum(exponent, axis=2, keepdims=True)
    weights = exponent / row_total
    product_gradients = jnp.einsum(
        "agk,igk->gai", gradient_rows, value_tile_block, preferred_element_type=jnp.float32
    )
    row_dots = jnp.sum(weights * product_gradients, axis=2, keepdims=True)
    weights_bfloat, gradients_bfloat = score_gradients(
        weights, product_gradients, row_dots, score_scale
    )
    return (
        weights_bfloat,
        gradients_bfloat,
        (row_max[:, :, 0], row_total[:, :, 0], row_dots[:, :, 0]),
    )


def whole_rows(query_row_block, key_tile_block, value_tile_block, gradient_rows):
    weights_bfloat, gradients_bfloat, unused = rows_with_stats(
        query_row_block, key_tile_block, value_tile_block, gradient_rows
    )
    return (weights_bfloat, gradients_bfloat)


def query_grad(gradients_bfloat, key_tile_block):
    return jnp.einsum(
        "ywr,ryu->wyu", gradients_bfloat, key_tile_block, preferred_element_type=jnp.float32
    )


def key_grad(gradients_bfloat, query_row_block):
    return jnp.einsum(
        "wfl,fwp->lwp", gradients_bfloat, query_row_block, preferred_element_type=jnp.float32
    )


def body(queries, key_rows, values, out_grads, offsets):
    tokens_here = queries.shape[0]
    near_end = H_NEAR * HEAD_DIM
    mid_end = near_end + H_MID * HEAD_DIM
    mid_offsets = offsets[:H_MID]
    wide_offsets = offsets[H_MID:]
    mid_query = select_rows(queries[:, near_end:mid_end], mid_offsets, R_MID)
    mid_key = select_rows(key_rows[:, near_end:mid_end], mid_offsets, R_MID)
    mid_value = select_rows(values[:, near_end:mid_end], mid_offsets, R_MID)
    mid_grad = select_rows(out_grads[:, near_end:mid_end], mid_offsets, R_MID)
    wide_query = select_rows(queries[:, mid_end:], wide_offsets, R_WIDE)
    wide_key = select_rows(key_rows[:, mid_end:], wide_offsets, R_WIDE)
    wide_value = select_rows(values[:, mid_end:], wide_offsets, R_WIDE)
    wide_grad = select_rows(out_grads[:, mid_end:], wide_offsets, R_WIDE)
    wide_keys_all, wide_values_all = (
        lax.all_gather(wide_key, ("outer", "inner"), axis=0, tiled=True),
        lax.all_gather(wide_value, ("outer", "inner"), axis=0, tiled=True),
    )
    all_keys, all_values = (
        lax.all_gather(mid_key, "inner", axis=0, tiled=True),
        lax.all_gather(mid_value, "inner", axis=0, tiled=True),
    )
    mid_weights, mid_sgrad = whole_rows(mid_query, all_keys, all_values, mid_grad)
    sgrad_part = mid_sgrad
    weight_part = mid_weights
    summed = lax.psum_scatter(
        jnp.stack([key_grad(sgrad_part, mid_query), key_grad(weight_part, mid_grad)], axis=1),
        "inner",
        scatter_dimension=0,
        tiled=True,
    )
    mid_result = [query_grad(mid_sgrad, all_keys), summed[:, 0], summed[:, 1]]
    near_query = queries[:, :near_end].reshape(tokens_here, H_NEAR, HEAD_DIM)
    near_key = key_rows[:, :near_end].reshape(tokens_here, H_NEAR, HEAD_DIM)
    near_value = values[:, :near_end].reshape(tokens_here, H_NEAR, HEAD_DIM)
    near_grad = out_grads[:, :near_end].reshape(tokens_here, H_NEAR, HEAD_DIM)
    near_weights, near_sgrad = whole_rows(near_query, near_key, near_value, near_grad)
    near_result = [
        query_grad(near_sgrad, near_key),
        key_grad(near_sgrad, near_query),
        key_grad(near_weights, near_grad),
    ]
    wide_weights, wide_sgrad = whole_rows(wide_query, wide_keys_all, wide_values_all, wide_grad)
    sgrad_part = wide_sgrad
    weight_part = wide_weights
    wide_summed = lax.psum_scatter(
        jnp.stack([key_grad(sgrad_part, wide_query), key_grad(weight_part, wide_grad)], axis=1),
        ("outer", "inner"),
        scatter_dimension=0,
        tiled=True,
    )
    wide_result = [query_grad(wide_sgrad, wide_keys_all), wide_summed[:, 0], wide_summed[:, 1]]
    joined = []
    for which in range(3):
        near_part = near_result[which].reshape(tokens_here, near_end)
        mid_part = spread_rows(mid_result[which], mid_offsets, R_MID)
        wide_part = spread_rows(wide_result[which], wide_offsets, R_WIDE)
        joined.append(
            jnp.concatenate([near_part, mid_part, wide_part], axis=1).astype(jnp.bfloat16)
        )
    return (joined[0], joined[1], joined[2])


def solution(mesh):
    return jax.shard_map(
        body,
        mesh=mesh,
        in_specs=(
            P(("outer", "inner"), None),
            P(("outer", "inner"), None),
            P(("outer", "inner"), None),
            P(("outer", "inner"), None),
            P(),
        ),
        out_specs=(
            P(("outer", "inner"), None),
            P(("outer", "inner"), None),
            P(("outer", "inner"), None),
        ),
        check_vma=False,
    )
```

profile of v0, /device:TPU:2, one launch (start us, length us, event | category | flops | bytes accessed | tf_op | source)
XLA Modules:
  0.0 1635.6 jit_solution(5643052252950914727)
XLA Ops:
  7.2 0.7 iota_compare_fusion.1
  7.9 1.0 slice.60
  8.9 0.4 reshape.149
  9.3 0.4 reshape.148
  9.7 0.2 slice-done.3
  9.9 0.4 reshape.151
  10.3 0.4 reshape.150
  10.7 1.4 select_reduce_fusion.2
  12.2 0.6 copy.99
  12.9 0.6 copy.101
  13.7 0.1 copy.106
  14.0 0.1 copy.104
  14.2 0.4 slice-done.4
  14.6 0.1 copy.110
  14.8 0.1 copy.109
  15.0 2.0 fusion.48
  17.3 579.2 %all_gather.14 = bf16[512,3,128]{2,1,0:T(4,128)(2,1)S(1)} all-gather(bf16[2,3,128]{2,1,0:T(4,128)(2,1)S(1)} %copy.105), channel_id=1, replica_groups=mesh['outer'=16,'inner'=16] {'outer','inner'}, dimensions={0}, use_global_device_ids=true | all-gather | bytes 394752 | tf_op jit(solution)/shard_map/all_gather | solution.py:102
  596.4 622.6 %all_gather.15 = bf16[512,3,128]{2,1,0:T(4,128)(2,1)S(1)} all-gather(bf16[2,3,128]{2,1,0:T(4,128)(2,1)S(1)} %copy.111), channel_id=1, replica_groups=mesh['outer'=16,'inner'=16] {'outer','inner'}, dimensions={0}, use_global_device_ids=true | all-gather | bytes 394752 | tf_op jit(solution)/shard_map/all_gather | solution.py:103
  1219.1 0.4 fusion.77
  1219.5 0.2 fusion.43
  1219.7 0.3 convolution_bitcast_fusion.4
  1220.0 0.4 convolution_bitcast_fusion.3
  1220.5 0.3 convolution_bitcast_fusion.2
  1220.8 0.2 pad_maximum_fusion.1
  1221.0 1.2 copy.126
  1222.1 130.5 %all-reduce.4 = bf16[512,2,3,128]{3,1,2,0:T(2,128)(2,1)S(1)} all-reduce(f32[512,2,3,128]{3,1,2,0:T(2,128)S(1)} %copy.126), channel_id=3, replica_groups=mesh['outer'=16,'inner'=16] {'outer','inner'}, use_global_device_ids=true, to_apply=%region_18.19.clone | all-reduce | flops 393216 | bytes 2359296
  1352.7 0.6 copy-done.8
  1353.3 0.6 dynamic-slice
  1354.1 0.1 copy.149
  1354.2 0.1 copy.152
  1354.4 0.1 copy.151
  1354.5 0.2 copy.115
  1354.7 0.2 copy.135
  1354.9 0.2 copy.128
  1355.1 1.5 select_convert_fusion.3
  1356.7 0.8 copy.137
  1357.5 0.8 copy.117
  1358.4 0.8 copy.130
  1359.2 0.3 fusion.82
  1359.5 0.5 fusion.79
  1360.1 0.5 convolution_convert_fusion
  1360.5 0.5 copy-done.9
  1361.1 0.1 copy.116
  1361.2 2.0 convolution_convert_fusion.2
  1363.2 0.1 copy.129
  1363.4 0.8 convolution_convert_fusion.1
  1364.1 0.1 copy.136
  1365.0 1.9 convolution_multiply_fusion
  1366.9 1.0 fusion.78
  1367.9 3.3 convolution_bitcast_fusion
  1371.2 2.0 fusion.52
  1373.2 1.1 copy-done.2
  1374.2 3.1 convolution_bitcast_fusion.1
  1377.3 5.3 fusion.24
  1382.6 0.9 copy.103
  1383.5 4.7 pad_maximum_fusion
  1388.2 8.8 copy.121
  1397.0 227.3 %all-reduce.5 = bf16[1024,2,5,128]{3,1,2,0:T(2,128)(2,1)S(1)} all-reduce(f32[1024,2,5,128]{3,1,2,0:T(2,128)} %copy.121), channel_id=2, replica_groups=mesh['outer'=16,'inner'=16] {'inner'}, use_global_device_ids=true, to_apply=%region_17.18.clone | all-reduce | flops 1310720 | bytes 7864320
  1624.3 0.3 constant_dynamic-slice_fusion.3
  1624.6 0.4 select_convert_fusion
  1625.2 0.7 copy-done.3
  1625.9 0.9 pad_maximum_fusion.4
  1626.9 0.9 pad_maximum_fusion.2
  1627.8 0.9 pad_maximum_fusion.3
  (60 shorter events, 1.3 us)
Async XLA Ops:
  7.2 2.2 slice-start
  7.2 1357.8 %all-gather.3.cloned.1.call-start = ((), (), s32[]{:S(2)}) async-start(), calls=%async_computation | async-start | bytes 1392640 | tf_op jit(solution)/shard_map/all_gather | solution.py:106
  8.9 1.0 slice-start.3
  9.3 1.0 slice-start.6
  10.7 2.9 copy-start.7
  12.2 1.6 slice-start.9
  12.8 1358.4 %all-gather.5.cloned.1.call-start = ((), (), s32[]{:S(2)}) async-start(), calls=%async_computation.1 | async-start | bytes 1392640 | tf_op jit(solution)/shard_map/all_gather | solution.py:107
  12.9 1.1 slice-start.1
  13.7 1.0 slice-start.4
  13.7 1.2 slice-start.7
  1352.6 0.7 copy-start.8
  1352.6 1.3 slice-start.10
  1352.7 1.4 slice-start.2
  1352.7 1.5 slice-start.5
  1352.7 1.7 slice-start.8
  1360.1 1.0 copy-start.9
  1363.4 1.6 copy-start.6
  1367.9 5.3 copy-start.1
  1373.1 1.1 copy-start.2
  1377.3 6.2 copy-start
  1625.0 0.9 copy-start.3
  1625.1 1.7 copy-start.4
  1625.9 1.9 copy-start.5
Sparse Core Ops, SparseCore 0:
  12.9 83.5 all-gather.2
  99.2 77.3 all-gather.4
where the time goes:
time: 1640 us
  blocking collectives  1560 us (95%)
  local copies, waits for them, and re-layouts  24.6 us (2%)
  matrix products  21.3 us (1%)
    all_gather x1, blocking collectives, body(): lax.all_gather(wide_value, ('outer', 'inner'), axis=0, tiled=True)  623 us
    all_gather x1, blocking collectives, body(): lax.all_gather(wide_key, ('outer', 'inner'), axis=0, tiled=True)  579 us
    unnamed x2, blocking collectives  358 us
  transfers between devices with their start and end apart: 2, of which 0 were waited for; matrix products, arithmetic and copies ran while one was open for 1% of the time, Pallas kernels for 0%

commit v1 on v0

v1 whole, which is shorter than its diff:
```python
import math

import jax
import jax.numpy as jnp
from jax import lax
from jax.experimental import pallas as pl
from jax.experimental.pallas import tpu as pltpu
from jax.sharding import PartitionSpec as P

HEAD_DIM = 128
H_NEAR = 4
H_MID = 5
H_WIDE = 3
R_MID = 4
R_WIDE = 128
TOK = 256
NEAR_END = H_NEAR * HEAD_DIM
MID_END = NEAR_END + H_MID * HEAD_DIM
HIDDEN = MID_END + H_WIDE * HEAD_DIM
MEMBERS = 16
OUTERS = 16
MID_ROWS = TOK // R_MID
SPLIT = 3
PART = 24
WIDE_SPLIT = 4
SCALE = 1.0 / math.sqrt(HEAD_DIM)
BF16 = jnp.bfloat16
F32 = jnp.float32
VMEM_LIMIT = 48 * 1024 * 1024


def dot(a, b):
    return lax.dot_general(a, b, (((1,), (0,)), ((), ())), preferred_element_type=F32)


def dot_nt(a, b):
    return lax.dot_general(a, b, (((1,), (1,)), ((), ())), preferred_element_type=F32)


def dot_tn(a, b):
    return lax.dot_general(a, b, (((0,), (0,)), ((), ())), preferred_element_type=F32)


def iota2(rows, columns):
    shape = (rows, columns)
    return (
        lax.broadcasted_iota(jnp.int32, shape, 0),
        lax.broadcasted_iota(jnp.int32, shape, 1),
    )


def one_hot(condition):
    return jnp.where(condition, 1.0, 0.0).astype(BF16)


def pair(left_ref, right_ref, start):
    columns = slice(start, start + HEAD_DIM)
    return jnp.concatenate([left_ref[:, columns], right_ref[:, columns]], axis=1)


def attention_transposed(query, key, value, gradient):
    scores = dot_nt(key, query) * SCALE
    exponent = jnp.exp(scores - jnp.max(scores, axis=0, keepdims=True))
    weights = exponent * (1.0 / jnp.sum(exponent, axis=0, keepdims=True))
    products = dot_nt(value, gradient)
    row_dots = jnp.sum(weights * products, axis=0, keepdims=True)
    score_gradients = (weights * (products - row_dots) * SCALE).astype(BF16)
    return weights.astype(BF16), score_gradients


def pack_kernel(off_ref, q_ref, k_ref, v_ref, g_ref, out_ref):
    row8, column8 = iota2(8, TOK)
    wide_rows = []
    for head in range(H_WIDE):
        start = MID_END + head * HEAD_DIM
        offset = off_ref[H_MID + head]
        pick_kv = one_hot((row8 < 2) & (column8 == offset + R_WIDE * row8))
        pick_qg = one_hot((row8 >= 2) & (row8 < 4) & (column8 == offset + R_WIDE * (row8 - 2)))
        wide_rows.append(
            dot(pick_kv, pair(k_ref, v_ref, start)) + dot(pick_qg, pair(q_ref, g_ref, start))
        )
    row_kv, column_kv = iota2(MID_ROWS, TOK)
    row_qg, column_qg = iota2(SPLIT * PART, TOK)
    for head in range(H_MID):
        start = NEAR_END + head * HEAD_DIM
        offset = off_ref[head]
        pick_kv = one_hot(column_kv == offset + R_MID * row_kv)
        pick_qg = one_hot(column_qg == offset + R_MID * row_qg)
        kv = dot(pick_kv, pair(k_ref, v_ref, start)).astype(BF16)
        qg = dot(pick_qg, pair(q_ref, g_ref, start))
        for part in range(SPLIT):
            worker = head * SPLIT + part
            wide_head = min(worker // WIDE_SPLIT, H_WIDE - 1)
            tail = jnp.concatenate([qg[part * PART : (part + 1) * PART], wide_rows[wide_head]], axis=0)
            out_ref[worker, 0:64, :] = kv
            out_ref[worker, 64:96, :] = tail.astype(BF16)
    out_ref[MEMBERS - 1] = jnp.zeros((96, 2 * HEAD_DIM), BF16)


def near_kernel(q_ref, k_ref, v_ref, g_ref, dq_ref, dk_ref, dv_ref):
    for head in range(H_NEAR):
        columns = slice(head * HEAD_DIM, (head + 1) * HEAD_DIM)
        query, key, value, gradient = (
            q_ref[:, columns],
            k_ref[:, columns],
            v_ref[:, columns],
            g_ref[:, columns],
        )
        weights, score_gradients = attention_transposed(query, key, value, gradient)
        dq_ref[:, columns] = dot_tn(score_gradients, key).astype(BF16)
        dk_ref[:, columns] = dot(score_gradients, query).astype(BF16)
        dv_ref[:, columns] = dot(weights, gradient).astype(BF16)


def forward_kernel(got_ref, out_ref):
    fourth = lax.rem(lax.axis_index("inner"), WIDE_SPLIT)
    rows = got_ref[:, 80:96, :].reshape(MEMBERS * 16, 2 * HEAD_DIM)
    row, column = iota2(48, MEMBERS * 16)
    source_kv = 16 * (row // 2) + 8 + row % 2
    query_row = row - 32
    source_qg = 16 * (WIDE_SPLIT * fourth + query_row // 2) + 10 + row % 2
    source = jnp.where(row < 32, source_kv, source_qg)
    picked = dot(one_hot((column == source) & (row < 40)), rows).astype(BF16)
    for target in range(OUTERS):
        out_ref[target] = picked


def worker_kernel(mid_ref, wide_ref, out_ref, dk_ref, dv_ref, dq_ref):
    outer = lax.axis_index("outer")
    fourth = lax.rem(lax.axis_index("inner"), WIDE_SPLIT)
    kv = wide_ref[:, 0:32, :].reshape(OUTERS * 32, 2 * HEAD_DIM)
    qg = wide_ref[:, 32:48, :].astype(F32)[:, 0:8, :].reshape(OUTERS * 8, 2 * HEAD_DIM).astype(BF16)
    key, value = kv[:, :HEAD_DIM], kv[:, HEAD_DIM:]
    query, gradient = qg[:, :HEAD_DIM], qg[:, HEAD_DIM:]
    weights, score_gradients = attention_transposed(query, key, value, gradient)
    dk_ref[...] = dot(score_gradients, query)
    dv_ref[...] = dot(weights, gradient)
    dq_ref[...] = dot_tn(score_gradients, key)
    own_keys = pl.ds(pl.multiple_of(outer * 32, 32), 32)
    own_queries = pl.ds(pl.multiple_of(outer * 8, 8), 8)
    dk, dv = dk_ref[own_keys, :].astype(BF16), dv_ref[own_keys, :].astype(BF16)
    dq = dq_ref[own_queries, :].astype(BF16)
    row, column = iota2(MEMBERS * 8, 32)
    member, place = row // 8, row % 8
    wide_out = dot(one_hot((column == 2 * member + place - 2) & (place >= 2) & (place < 4)), dk)
    wide_out += dot(one_hot((column == 2 * member + place - 4) & (place >= 4) & (place < 6)), dv)
    row, column = iota2(MEMBERS * 8, 8)
    member, place = row // 8, row % 8
    wide_out += dot(
        one_hot((column == 2 * (member - WIDE_SPLIT * fourth) + place) & (place < 2)), dq
    )
    key = mid_ref[:, 0:64, :HEAD_DIM].reshape(MEMBERS * 64, HEAD_DIM)
    value = mid_ref[:, 0:64, HEAD_DIM:].reshape(MEMBERS * 64, HEAD_DIM)
    qg = mid_ref[:, 64:96, :].astype(F32)[:, 0:PART, :].reshape(MEMBERS * PART, 2 * HEAD_DIM)
    qg = qg.astype(BF16)
    query, gradient = qg[:, :HEAD_DIM], qg[:, HEAD_DIM:]
    weights, score_gradients = attention_transposed(query, key, value, gradient)
    out_ref[:, 0:64, :] = dot(score_gradients, query).astype(BF16).reshape(MEMBERS, 64, HEAD_DIM)
    out_ref[:, 64:128, :] = dot(weights, gradient).astype(BF16).reshape(MEMBERS, 64, HEAD_DIM)
    dq = dot_tn(key, score_gradients).T.reshape(MEMBERS, PART, HEAD_DIM)
    tail = jnp.concatenate([dq, wide_out.reshape(MEMBERS, 8, HEAD_DIM)], axis=1)
    out_ref[:, 128:160, :] = tail.astype(BF16)


def assemble_kernel(off_ref, got_ref, nq_ref, nk_ref, nv_ref, dq_ref, dk_ref, dv_ref):
    inner = lax.axis_index("inner")
    for near_ref, out_ref in ((nq_ref, dq_ref), (nk_ref, dk_ref), (nv_ref, dv_ref)):
        out_ref[:, :NEAR_END] = near_ref[...]
    row, column = iota2(TOK, SPLIT * PART)
    row64, column64 = iota2(TOK, MID_ROWS)
    for head in range(H_MID):
        columns = slice(NEAR_END + head * HEAD_DIM, NEAR_END + (head + 1) * HEAD_DIM)
        offset = off_ref[head]
        workers = range(head * SPLIT, (head + 1) * SPLIT)
        dq = jnp.concatenate(
            [got_ref[worker, 128:160, :].astype(F32)[0:PART] for worker in workers], axis=0
        ).astype(BF16)
        dk = sum(got_ref[worker, 0:64, :].astype(F32) for worker in workers).astype(BF16)
        dv = sum(got_ref[worker, 64:128, :].astype(F32) for worker in workers).astype(BF16)
        place = one_hot(row64 == offset + R_MID * column64)
        dq_ref[:, columns] = dot(one_hot(row == offset + R_MID * column), dq).astype(BF16)
        dk_ref[:, columns] = dot(place, dk).astype(BF16)
        dv_ref[:, columns] = dot(place, dv).astype(BF16)
    row, unused = iota2(TOK, HEAD_DIM)
    for head in range(H_WIDE):
        columns = slice(MID_END + head * HEAD_DIM, MID_END + (head + 1) * HEAD_DIM)
        offset = off_ref[H_MID + head]
        workers = range(head * WIDE_SPLIT, (head + 1) * WIDE_SPLIT)
        sums = sum(got_ref[worker, 144:160, :].astype(F32) for worker in workers)
        owner = head * WIDE_SPLIT + lax.div(inner, WIDE_SPLIT)
        queries = got_ref[owner, 144:160, :].astype(F32)
        first, second = row == offset, row == offset + R_WIDE
        for out_ref, rows, at in ((dq_ref, queries, 8), (dk_ref, sums, 10), (dv_ref, sums, 12)):
            spread = jnp.where(first, rows[at : at + 1], 0.0)
            spread = jnp.where(second, rows[at + 1 : at + 2], spread)
            out_ref[:, columns] = spread.astype(BF16)


def call(kernel, out_shapes, in_smem, scratch=()):
    spaces = {True: pltpu.SMEM, False: pltpu.VMEM}
    outs = [jax.ShapeDtypeStruct(shape, BF16) for shape in out_shapes]
    specs = [pl.BlockSpec(memory_space=pltpu.VMEM) for unused in outs]
    return pl.pallas_call(
        kernel,
        out_shape=outs if len(outs) > 1 else outs[0],
        in_specs=[pl.BlockSpec(memory_space=spaces[smem]) for smem in in_smem],
        out_specs=specs if len(outs) > 1 else specs[0],
        scratch_shapes=list(scratch),
        compiler_params=pltpu.CompilerParams(vmem_limit_bytes=VMEM_LIMIT),
    )


def body(queries, key_rows, values, out_grads, offsets):
    arrays = (queries, key_rows, values, out_grads)
    packed = call(pack_kernel, [(MEMBERS, 96, 256)], [True] + [False] * 4)(offsets, *arrays)
    near_block = pl.BlockSpec((TOK, NEAR_END), lambda step: (0, 0))
    near = pl.pallas_call(
        near_kernel,
        grid=(1,),
        out_shape=[jax.ShapeDtypeStruct((TOK, NEAR_END), BF16)] * 3,
        in_specs=[near_block] * 4,
        out_specs=[near_block] * 3,
        compiler_params=pltpu.CompilerParams(vmem_limit_bytes=VMEM_LIMIT),
    )(*arrays)
    mid_got = lax.all_to_all(packed, "inner", 0, 0)
    wide_send = call(forward_kernel, [(OUTERS, 48, 256)], [False])(mid_got)
    wide_got = lax.all_to_all(wide_send, "outer", 0, 0)
    results = call(
        worker_kernel,
        [(MEMBERS, 160, HEAD_DIM)],
        [False] * 2,
        [pltpu.VMEM((512, 128), F32), pltpu.VMEM((512, 128), F32), pltpu.VMEM((128, 128), F32)],
    )(mid_got, wide_got)
    returned = lax.all_to_all(results, "inner", 0, 0)
    return tuple(
        call(assemble_kernel, [(TOK, HIDDEN)] * 3, [True] + [False] * 4)(offsets, returned, *near)
    )


def solution(mesh):
    spec = P(("outer", "inner"), None)
    return jax.shard_map(
        body,
        mesh=mesh,
        in_specs=(spec, spec, spec, spec, P()),
        out_specs=(spec, spec, spec),
        check_vma=False,
    )
```

time: 1640 us -> 91.9 us (0.06)
  blocking collectives: 1560 us -> 47.1 us
  matrix products: 21.3 us -> 0 us
  waiting for transfers between devices: 0.07 us -> 19.8 us
    all_gather x2 -> x0, blocking collectives: 1200 us -> none  [the longest x1 623 us: body(): lax.all_gather(wide_value, ('outer', 'inner'), axis=0, tiled=True)]
    unnamed x2 -> x0, blocking collectives: 358 us -> none
    all_to_all x0 -> x2, blocking collectives: none -> 47.1 us  [the longest x1 35.9 us: body(): mid_got = lax.all_to_all(packed, 'inner', 0, 0)]
    dot_general x13 -> x0, matrix products: 20.3 us -> none  [the longest x6 9.85 us: key_grad(): jnp.einsum('wfl,fwp->lwp', gradients_bfloat, query_row_block, preferred_e...]
    all_to_all x0 -> x1, waiting for transfers between devices: none -> 19.8 us  [body(): returned = lax.all_to_all(results, 'inner', 0, 0)]
  transfers between devices with their start and end apart: 2 -> 1, of which waited for: 0 -> 1; matrix products, arithmetic and copies ran while one was open for 1% -> 0% of each run, Pallas kernels for 0% -> 2%
where the time goes in v1:
time: 91.9 us; the launch traced here: 90.5 us
  blocking collectives  47.1 us (51%)
  waiting for transfers between devices  19.8 us (22%)
  local copies, waits for them, and re-layouts  9.98 us (11%)
  Pallas kernels  8.5 us (9%)
  starting transfers between devices  4.39 us (5%)
    all_to_all x1, blocking collectives, body(): mid_got = lax.all_to_all(packed, 'inner', 0, 0)  35.9 us
    all_to_all x1, waiting for transfers between devices, body(): returned = lax.all_to_all(results, 'inner', 0, 0)  19.8 us
    all_to_all x1, blocking collectives, body(): wide_got = lax.all_to_all(wide_send, 'outer', 0, 0)  11.2 us
    unnamed x30, local copies, waits for them, and re-layouts  9.98 us
    all_to_all x1, starting transfers between devices, body(): returned = lax.all_to_all(results, 'inner', 0, 0)  4.39 us
    pallas_call x1, Pallas kernels, body(): call(assemble_kernel, [(TOK, HIDDEN)] * 3, [True] + [False] * 4)  3.01 us
    pallas_call x1, Pallas kernels, body(): call(worker_kernel, [(MEMBERS, 160, HEAD_DIM)], [False] * 2, [pltpu.VMEM(...  2.45 us
    pallas_call x1, Pallas kernels, body(): pl.pallas_call(near_kernel, grid=(1,), out_shape=[jax.ShapeDtypeStruct((T...  1.87 us
  transfers between devices with their start and end apart: 1, of which 1 were waited for; matrix products, arithmetic and copies ran while one was open for 0% of the time, Pallas kernels for 2%

profile of v1, /device:TPU:2, one launch (start us, length us, event | category | flops | bytes accessed | tf_op | source)
XLA Modules:
  0.0 90.5 jit_solution(5913614310274307153)
XLA Ops:
  0.6 0.0 copy-start
  0.6 1.1 %copy-done = bf16[256,1536]{1,0:T(8,128)(2,1)S(1)} copy-done((bf16[256,1536]{1,0:T(8,128)(2,1)S(1)}, bf16[256,1536]{1,0:T(8,128)(2,1)}, u32[]{:S(2)}) %copy-start) | copy-done | bytes 786456
  1.8 0.0 copy-start.2
  1.8 1.1 %copy-done.2 = bf16[256,1536]{1,0:T(8,128)(2,1)S(1)} copy-done((bf16[256,1536]{1,0:T(8,128)(2,1)S(1)}, bf16[256,1536]{1,0:T(8,128)(2,1)}, u32[]{:S(2)}) %copy-start.2) | copy-done | bytes 786456
  2.9 0.0 copy-start.4
  2.9 1.1 %copy-done.4 = bf16[256,1536]{1,0:T(8,128)(2,1)S(1)} copy-done((bf16[256,1536]{1,0:T(8,128)(2,1)S(1)}, bf16[256,1536]{1,0:T(8,128)(2,1)}, u32[]{:S(2)}) %copy-start.4) | copy-done | bytes 786456
  4.0 0.0 copy-start.6
  4.0 1.1 %copy-done.6 = bf16[256,1536]{1,0:T(8,128)(2,1)S(1)} copy-done((bf16[256,1536]{1,0:T(8,128)(2,1)S(1)}, bf16[256,1536]{1,0:T(8,128)(2,1)}, u32[]{:S(2)}) %copy-start.6) | copy-done | bytes 786456
  5.2 0.0 copy-start.13
  5.2 0.7 copy-done.13
  5.8 1.0 %shard_map.76 = bf16[16,96,256]{2,1,0:T(8,128)(2,1)S(1)} custom-call(s32[8]{0:T(128)S(1)} %copy-done.13, bf16[256,1536]{1,0:T(8,128)(2,1)S(1)} %copy-done, bf16[256,1536]{1,0:T(8,128)(2,1)S(1)} %copy-done.2, bf16[256,1536]{1,0:T(8,128)(2,1)S(1)} %copy-done.4, bf16[256,1536]{1,0:T(8,128)(2,1)S(1)} %copy-done.6), custom_call_target="tpu_custom_call" | custom-call | tf_op jit(solution)/shard_map/pallas_call | solution.py:215
  6.8 35.9 %all_to_all.15.got_ref.mid_ref = bf16[16,96,256]{2,1,0:T(8,128)(2,1)S(1)} all-to-all(bf16[16,96,256]{2,1,0:T(8,128)(2,1)S(1)} %shard_map.76), channel_id=1, replica_groups=mesh['outer'=16,'inner'=16] {'inner'}, dimensions={0} | all-to-all | bytes 1572864 | tf_op jit(solution)/shard_map/all_to_all | solution.py:225
  42.7 0.2 shard_map.77
  42.9 11.2 %all_to_all.16.wide_ref = bf16[16,48,256]{2,1,0:T(8,128)(2,1)S(1)} all-to-all(bf16[16,48,256]{2,1,0:T(8,128)(2,1)S(1)} %shard_map.77), channel_id=1, replica_groups=mesh['outer'=16,'inner'=16] {'outer'}, dimensions={0} | all-to-all | bytes 786432 | tf_op jit(solution)/shard_map/all_to_all | solution.py:227
  54.1 0.0 copy-start.3
  54.1 0.0 copy-start.5
  54.1 0.0 copy-start.7
  54.1 2.4 %shard_map.78 = bf16[16,160,128]{2,1,0:T(8,128)(2,1)S(1)} custom-call(bf16[16,96,256]{2,1,0:T(8,128)(2,1)S(1)} %all_to_all.15.got_ref.mid_ref, bf16[16,48,256]{2,1,0:T(8,128)(2,1)S(1)} %all_to_all.16.wide_ref), custom_call_target="tpu_custom_call" | custom-call | tf_op jit(solution)/shard_map/pallas_call | solution.py:228
  56.6 0.0 copy-start.8
  56.6 0.8 copy-done.8
  57.4 0.0 copy-start.1
  57.4 4.4 %all-to-all-start.2 = ((bf16[16,160,128]{2,1,0:T(8,128)(2,1)}), bf16[16,160,128]{2,1,0:T(8,128)(2,1)}, u32[]{:S(2)}, u32[]{:S(2)}) async-start(bf16[16,160,128]{2,1,0:T(8,128)(2,1)} %copy-done.8), calls=%async_computation.2 | async-start | bytes 1310720 | tf_op jit(solution)/shard_map/all_to_all | solution.py:234
  61.8 0.0 copy-done.3
  61.8 0.0 copy-done.5
  61.8 0.0 copy-done.7
  61.8 0.0 copy-done.1
  61.8 1.9 %shard_map.79 = (bf16[256,512]{1,0:T(8,128)(2,1)S(1)}, bf16[256,512]{1,0:T(8,128)(2,1)S(1)}, bf16[256,512]{1,0:T(8,128)(2,1)S(1)}) custom-call(bf16[256,1536]{1,0:T(8,128)(2,1)S(1)} %copy-done.1, bf16[256,1536]{1,0:T(8,128)(2,1)S(1)} %copy-done.3, bf16[256,1536]{1,0:T(8,128)(2,1)S(1)} %copy-done.5, bf16[256,1536]{1,0:T(8,128)(2,1)S(1)} %copy-done.7), custom_call_target="tpu_custom_call" | custom-call | tf_op jit(solution)/shard_map/pallas_call | solution.py:217
  63.7 0.0 copy-start.9
  63.7 0.7 copy-done.9
  64.4 0.0 copy-start.11
  64.4 0.7 copy-done.11
  65.1 19.8 %all-to-all-done.2.got_ref = bf16[16,160,128]{2,1,0:T(8,128)(2,1)} async-done(((bf16[16,160,128]{2,1,0:T(8,128)(2,1)}), bf16[16,160,128]{2,1,0:T(8,128)(2,1)}, u32[]{:S(2)}, u32[]{:S(2)}) %all-to-all-start.2) | async-done | bytes 655392 | tf_op jit(solution)/shard_map/all_to_all | solution.py:234
  84.9 0.0 copy-start.14
  84.9 0.7 copy-done.14
  85.6 0.0 copy-start.10
  85.6 0.9 %copy-done.10 = bf16[256,512]{1,0:T(8,128)(2,1)S(1)} copy-done((bf16[256,512]{1,0:T(8,128)(2,1)S(1)}, bf16[256,512]{1,0:T(8,128)(2,1)}, u32[]{:S(2)}) %copy-start.10) | copy-done | bytes 262168
  86.5 0.0 copy-start.12
  86.5 0.9 %copy-done.12 = bf16[256,512]{1,0:T(8,128)(2,1)S(1)} copy-done((bf16[256,512]{1,0:T(8,128)(2,1)S(1)}, bf16[256,512]{1,0:T(8,128)(2,1)}, u32[]{:S(2)}) %copy-start.12) | copy-done | bytes 262168
  87.5 3.0 %shard_map.80 = (bf16[256,1536]{1,0:T(8,128)(2,1)}, bf16[256,1536]{1,0:T(8,128)(2,1)}, bf16[256,1536]{1,0:T(8,128)(2,1)}) custom-call(s32[8]{0:T(128)S(1)} %copy-done.14, bf16[16,160,128]{2,1,0:T(8,128)(2,1)} %all-to-all-done.2.got_ref, bf16[256,512]{1,0:T(8,128)(2,1)S(1)} %get-tuple-element.6.nq_ref, bf16[256,512]{1,0:T(8,128)(2,1)S(1)} %copy-done.10, ...), custom_call_target="tpu_custom_call" | custom-call | tf_op jit(solution)/shard_map/pallas_call | solution.py:236
Async XLA Ops:
  0.6 1.1 %copy-start = (bf16[256,1536]{1,0:T(8,128)(2,1)S(1)}, bf16[256,1536]{1,0:T(8,128)(2,1)}, u32[]{:S(2)}) copy-start(bf16[256,1536]{1,0:T(8,128)(2,1)} %q_ref.3) | copy-start | bytes 2359300
  1.8 1.1 %copy-start.2 = (bf16[256,1536]{1,0:T(8,128)(2,1)S(1)}, bf16[256,1536]{1,0:T(8,128)(2,1)}, u32[]{:S(2)}) copy-start(bf16[256,1536]{1,0:T(8,128)(2,1)} %k_ref.3) | copy-start | bytes 2359300
  2.9 1.1 %copy-start.4 = (bf16[256,1536]{1,0:T(8,128)(2,1)S(1)}, bf16[256,1536]{1,0:T(8,128)(2,1)}, u32[]{:S(2)}) copy-start(bf16[256,1536]{1,0:T(8,128)(2,1)} %v_ref.3) | copy-start | bytes 2359300
  4.0 1.1 %copy-start.6 = (bf16[256,1536]{1,0:T(8,128)(2,1)S(1)}, bf16[256,1536]{1,0:T(8,128)(2,1)}, u32[]{:S(2)}) copy-start(bf16[256,1536]{1,0:T(8,128)(2,1)} %g_ref.3) | copy-start | bytes 2359300
  5.2 0.7 copy-start.13
  54.1 7.7 %copy-start.3 = (bf16[256,1536]{1,0:T(8,128)(2,1)S(1)}, bf16[256,1536]{1,0:T(8,128)(2,1)}, u32[]{:S(2)}) copy-start(bf16[256,1536]{1,0:T(8,128)(2,1)} %k_ref.3) | copy-start | bytes 2359300
  54.1 7.7 %copy-start.5 = (bf16[256,1536]{1,0:T(8,128)(2,1)S(1)}, bf16[256,1536]{1,0:T(8,128)(2,1)}, u32[]{:S(2)}) copy-start(bf16[256,1536]{1,0:T(8,128)(2,1)} %v_ref.3) | copy-start | bytes 2359300
  54.1 7.7 %copy-start.7 = (bf16[256,1536]{1,0:T(8,128)(2,1)S(1)}, bf16[256,1536]{1,0:T(8,128)(2,1)}, u32[]{:S(2)}) copy-start(bf16[256,1536]{1,0:T(8,128)(2,1)} %g_ref.3) | copy-start | bytes 2359300
  56.6 0.8 copy-start.8
  57.4 4.4 %copy-start.1 = (bf16[256,1536]{1,0:T(8,128)(2,1)S(1)}, bf16[256,1536]{1,0:T(8,128)(2,1)}, u32[]{:S(2)}) copy-start(bf16[256,1536]{1,0:T(8,128)(2,1)} %q_ref.3) | copy-start | bytes 2359300
  57.4 27.5 %all-to-all-start.2 = ((bf16[16,160,128]{2,1,0:T(8,128)(2,1)}), bf16[16,160,128]{2,1,0:T(8,128)(2,1)}, u32[]{:S(2)}, u32[]{:S(2)}) async-start(bf16[16,160,128]{2,1,0:T(8,128)(2,1)} %copy-done.8), calls=%async_computation.2 | async-start | bytes 1310720 | tf_op jit(solution)/shard_map/all_to_all | solution.py:234
  63.7 0.7 copy-start.9
  64.4 0.7 copy-start.11
  84.9 0.7 copy-start.14
  85.6 0.9 %copy-start.10 = (bf16[256,512]{1,0:T(8,128)(2,1)S(1)}, bf16[256,512]{1,0:T(8,128)(2,1)}, u32[]{:S(2)}) copy-start(bf16[256,512]{1,0:T(8,128)(2,1)} %copy-done.9) | copy-start | bytes 786436
  86.5 0.9 %copy-start.12 = (bf16[256,512]{1,0:T(8,128)(2,1)S(1)}, bf16[256,512]{1,0:T(8,128)(2,1)}, u32[]{:S(2)}) copy-start(bf16[256,512]{1,0:T(8,128)(2,1)} %copy-done.11) | copy-start | bytes 786436

commit v2 on v1

v2 whole, which is shorter than its diff:
```python
import math

import jax
import jax.numpy as jnp
from jax import lax
from jax.experimental import pallas as pl
from jax.experimental.pallas import tpu as pltpu
from jax.sharding import PartitionSpec as P

HEAD_DIM = 128
H_NEAR = 4
H_MID = 5
H_WIDE = 3
R_MID = 4
R_WIDE = 128
TOK = 256
NEAR_END = H_NEAR * HEAD_DIM
MID_END = NEAR_END + H_MID * HEAD_DIM
HIDDEN = MID_END + H_WIDE * HEAD_DIM
MEMBERS = 16
OUTERS = 16
MID_ROWS = TOK // R_MID
SPLIT = 3
PART = 24
WIDE_SPLIT = 4
SCALE = 1.0 / math.sqrt(HEAD_DIM)
BF16 = jnp.bfloat16
F32 = jnp.float32


def dot(a, b):
    return lax.dot_general(a, b, (((1,), (0,)), ((), ())), preferred_element_type=F32)


def dot_nt(a, b):
    return lax.dot_general(a, b, (((1,), (1,)), ((), ())), preferred_element_type=F32)


def dot_tn(a, b):
    return lax.dot_general(a, b, (((0,), (0,)), ((), ())), preferred_element_type=F32)


def iota2(rows, columns):
    shape = (rows, columns)
    return (
        lax.broadcasted_iota(jnp.int32, shape, 0),
        lax.broadcasted_iota(jnp.int32, shape, 1),
    )


def one_hot(condition):
    return jnp.where(condition, 1.0, 0.0).astype(BF16)


def attention_transposed(query, key, value, gradient):
    scores = dot_nt(key, query) * SCALE
    exponent = jnp.exp(scores - jnp.max(scores, axis=0, keepdims=True))
    weights = exponent * (1.0 / jnp.sum(exponent, axis=0, keepdims=True))
    products = dot_nt(value, gradient)
    row_dots = jnp.sum(weights * products, axis=0, keepdims=True)
    score_gradients = (weights * (products - row_dots) * SCALE).astype(BF16)
    return weights.astype(BF16), score_gradients


def pack_kernel(off_hbm, q_hbm, k_hbm, v_hbm, g_hbm, out_ref, off_out, off_ref, held, off_sem, sems):
    off_copy = pltpu.make_async_copy(off_hbm, off_ref, off_sem)
    off_copy.start()
    order = list(range(H_MID, H_MID + H_WIDE)) + list(range(H_MID))
    copies = {}
    for head in order:
        for which, source in enumerate((q_hbm, k_hbm, v_hbm, g_hbm)):
            copies[head, which] = pltpu.make_async_copy(
                source.at[:, pl.ds(NEAR_END + head * HEAD_DIM, HEAD_DIM)],
                held.at[which, head],
                sems.at[which, head],
            )
            copies[head, which].start()
    off_copy.wait()
    for head in range(H_MID + H_WIDE):
        off_out[head : head + 1, :] = jnp.full((1, HEAD_DIM), off_ref[head], jnp.int32)
    row8, column8 = iota2(8, TOK)
    wide_rows = []
    for head in range(H_MID, H_MID + H_WIDE):
        offset = off_ref[head]
        pick_kv = one_hot((row8 < 2) & (column8 == offset + R_WIDE * row8))
        pick_qg = one_hot((row8 >= 2) & (row8 < 4) & (column8 == offset + R_WIDE * (row8 - 2)))
        for which in range(4):
            copies[head, which].wait()
        kv = jnp.concatenate([held[1, head], held[2, head]], axis=1)
        qg = jnp.concatenate([held[0, head], held[3, head]], axis=1)
        wide_rows.append(dot(pick_kv, kv) + dot(pick_qg, qg))
    row_kv, column_kv = iota2(MID_ROWS, TOK)
    row_qg, column_qg = iota2(SPLIT * PART, TOK)
    for head in range(H_MID):
        offset = off_ref[head]
        pick_kv = one_hot(column_kv == offset + R_MID * row_kv)
        pick_qg = one_hot(column_qg == offset + R_MID * row_qg)
        for which in range(4):
            copies[head, which].wait()
        kv = dot(pick_kv, jnp.concatenate([held[1, head], held[2, head]], axis=1)).astype(BF16)
        qg = dot(pick_qg, jnp.concatenate([held[0, head], held[3, head]], axis=1))
        for part in range(SPLIT):
            worker = head * SPLIT + part
            wide_head = min(worker // WIDE_SPLIT, H_WIDE - 1)
            tail = jnp.concatenate([qg[part * PART : (part + 1) * PART], wide_rows[wide_head]], axis=0)
            out_ref[worker, 0:64, :] = kv
            out_ref[worker, 64:96, :] = tail.astype(BF16)
    out_ref[MEMBERS - 1] = jnp.zeros((96, 2 * HEAD_DIM), BF16)


def near_kernel(q_ref, k_ref, v_ref, g_ref, dq_ref, dk_ref, dv_ref):
    query, key, value, gradient = q_ref[...], k_ref[...], v_ref[...], g_ref[...]
    weights, score_gradients = attention_transposed(query, key, value, gradient)
    dq_ref[...] = dot_tn(score_gradients, key).astype(BF16)
    dk_ref[...] = dot(score_gradients, query).astype(BF16)
    dv_ref[...] = dot(weights, gradient).astype(BF16)


def forward_kernel(got_ref, out_ref):
    fourth = lax.rem(lax.axis_index("inner"), WIDE_SPLIT)
    rows = got_ref[:, 80:96, :].reshape(MEMBERS * 16, 2 * HEAD_DIM)
    row, column = iota2(48, MEMBERS * 16)
    source_kv = 16 * (row // 2) + 8 + row % 2
    query_row = row - 32
    source_qg = 16 * (WIDE_SPLIT * fourth + query_row // 2) + 10 + row % 2
    source = jnp.where(row < 32, source_kv, source_qg)
    picked = dot(one_hot((column == source) & (row < 40)), rows).astype(BF16)
    for target in range(OUTERS):
        out_ref[target] = picked


def worker_kernel(mid_ref, wide_ref, out_ref, dk_ref, dv_ref, dq_ref):
    outer = lax.axis_index("outer")
    fourth = lax.rem(lax.axis_index("inner"), WIDE_SPLIT)
    kv = wide_ref[:, 0:32, :].reshape(OUTERS * 32, 2 * HEAD_DIM)
    qg = wide_ref[:, 32:48, :].astype(F32)[:, 0:8, :].reshape(OUTERS * 8, 2 * HEAD_DIM).astype(BF16)
    key, value = kv[:, :HEAD_DIM], kv[:, HEAD_DIM:]
    query, gradient = qg[:, :HEAD_DIM], qg[:, HEAD_DIM:]
    weights, score_gradients = attention_transposed(query, key, value, gradient)
    dk_ref[...] = dot(score_gradients, query)
    dv_ref[...] = dot(weights, gradient)
    dq_ref[...] = dot_tn(score_gradients, key)
    own_keys = pl.ds(pl.multiple_of(outer * 32, 32), 32)
    own_queries = pl.ds(pl.multiple_of(outer * 8, 8), 8)
    dk, dv = dk_ref[own_keys, :].astype(BF16), dv_ref[own_keys, :].astype(BF16)
    dq = dq_ref[own_queries, :].astype(BF16)
    row, column = iota2(MEMBERS * 8, 32)
    member, place = row // 8, row % 8
    wide_out = dot(one_hot((column == 2 * member + place - 2) & (place >= 2) & (place < 4)), dk)
    wide_out += dot(one_hot((column == 2 * member + place - 4) & (place >= 4) & (place < 6)), dv)
    row, column = iota2(MEMBERS * 8, 8)
    member, place = row // 8, row % 8
    wide_out += dot(
        one_hot((column == 2 * (member - WIDE_SPLIT * fourth) + place) & (place < 2)), dq
    )
    key = mid_ref[:, 0:64, :HEAD_DIM].reshape(MEMBERS * 64, HEAD_DIM)
    value = mid_ref[:, 0:64, HEAD_DIM:].reshape(MEMBERS * 64, HEAD_DIM)
    qg = mid_ref[:, 64:96, :].astype(F32)[:, 0:PART, :].reshape(MEMBERS * PART, 2 * HEAD_DIM)
    qg = qg.astype(BF16)
    query, gradient = qg[:, :HEAD_DIM], qg[:, HEAD_DIM:]
    weights, score_gradients = attention_transposed(query, key, value, gradient)
    out_ref[:, 0:64, :] = dot(score_gradients, query).astype(BF16).reshape(MEMBERS, 64, HEAD_DIM)
    out_ref[:, 64:128, :] = dot(weights, gradient).astype(BF16).reshape(MEMBERS, 64, HEAD_DIM)
    dq = dot_tn(key, score_gradients).T.reshape(MEMBERS, PART, HEAD_DIM)
    tail = jnp.concatenate([dq, wide_out.reshape(MEMBERS, 8, HEAD_DIM)], axis=1)
    out_ref[:, 128:160, :] = tail.astype(BF16)


def assemble_kernel(off_ref, got_ref, nq, nk, nv, dq_hbm, dk_hbm, dv_hbm, held, sems):
    inner = lax.axis_index("inner")
    copies = []

    def send(which, head, block):
        held[which, head] = block.astype(BF16)
        target = (dq_hbm, dk_hbm, dv_hbm)[which]
        copy = pltpu.make_async_copy(
            held.at[which, head],
            target.at[:, pl.ds(NEAR_END + head * HEAD_DIM, HEAD_DIM)],
            sems.at[which, head],
        )
        copy.start()
        copies.append(copy)

    row, unused = iota2(TOK, HEAD_DIM)
    for wide_head in range(H_WIDE):
        head = H_MID + wide_head
        offset = off_ref[head : head + 1, :]
        workers = range(wide_head * WIDE_SPLIT, (wide_head + 1) * WIDE_SPLIT)
        sums = sum(got_ref[worker, 144:160, :].astype(F32) for worker in workers)
        owner = wide_head * WIDE_SPLIT + lax.div(inner, WIDE_SPLIT)
        queries = got_ref[owner, 144:160, :].astype(F32)
        first, second = row == offset, row == offset + R_WIDE
        for which, rows, at in ((0, queries, 8), (1, sums, 10), (2, sums, 12)):
            spread = jnp.where(first, rows[at : at + 1], 0.0)
            send(which, head, jnp.where(second, rows[at + 1 : at + 2], spread))
    row, column = iota2(TOK, SPLIT * PART)
    row64, column64 = iota2(TOK, MID_ROWS)
    for head in range(H_MID):
        offset = off_ref[head : head + 1, :1]
        workers = range(head * SPLIT, (head + 1) * SPLIT)
        dq = jnp.concatenate(
            [got_ref[worker, 128:160, :].astype(F32)[0:PART] for worker in workers], axis=0
        ).astype(BF16)
        dk = sum(got_ref[worker, 0:64, :].astype(F32) for worker in workers).astype(BF16)
        dv = sum(got_ref[worker, 64:128, :].astype(F32) for worker in workers).astype(BF16)
        place = one_hot(row64 - R_MID * column64 == offset)
        send(0, head, dot(one_hot(row - R_MID * column == offset), dq))
        send(1, head, dot(place, dk))
        send(2, head, dot(place, dv))
    for copy in copies:
        copy.wait()


def spec(space):
    return pl.BlockSpec(memory_space=space)


def in_hbm(array):
    return pltpu.with_memory_space_constraint(array, pltpu.HBM)


def params(mebibytes):
    return pltpu.CompilerParams(vmem_limit_bytes=mebibytes * 1024 * 1024)


def shape(*sizes, kind=BF16):
    return jax.ShapeDtypeStruct(sizes, kind)


def body(queries, key_rows, values, out_grads, offsets):
    arrays = [in_hbm(array) for array in (queries, key_rows, values, out_grads)]
    heads = H_MID + H_WIDE
    packed, offset_rows = pl.pallas_call(
        pack_kernel,
        out_shape=[shape(MEMBERS, 96, 256), shape(heads, HEAD_DIM, kind=jnp.int32)],
        in_specs=[spec(pltpu.HBM)] * 5,
        out_specs=[spec(pltpu.VMEM)] * 2,
        scratch_shapes=[
            pltpu.SMEM((heads,), jnp.int32),
            pltpu.VMEM((4, heads, TOK, HEAD_DIM), BF16),
            pltpu.SemaphoreType.DMA,
            pltpu.SemaphoreType.DMA((4, heads)),
        ],
        compiler_params=params(16),
    )(in_hbm(offsets), *arrays)
    near_block = pl.BlockSpec((TOK, HEAD_DIM), lambda head: (0, head))
    near = pl.pallas_call(
        near_kernel,
        grid=(H_NEAR,),
        out_shape=[shape(TOK, HIDDEN)] * 3,
        in_specs=[near_block] * 4,
        out_specs=[near_block] * 3,
        cost_estimate=pl.CostEstimate(
            flops=10 * H_NEAR * TOK * TOK * HEAD_DIM,
            bytes_accessed=14 * TOK * NEAR_END,
            transcendentals=H_NEAR * TOK * TOK,
        ),
        compiler_params=params(16),
    )(*arrays)
    mid_got = lax.all_to_all(packed, "inner", 0, 0)
    wide_send = pl.pallas_call(
        forward_kernel,
        out_shape=shape(OUTERS, 48, 256),
        in_specs=[spec(pltpu.VMEM)],
        out_specs=spec(pltpu.VMEM),
        compiler_params=params(16),
    )(mid_got)
    wide_got = lax.all_to_all(wide_send, "outer", 0, 0)
    results = pl.pallas_call(
        worker_kernel,
        out_shape=shape(MEMBERS, 160, HEAD_DIM),
        in_specs=[spec(pltpu.VMEM)] * 2,
        out_specs=spec(pltpu.VMEM),
        scratch_shapes=[
            pltpu.VMEM((512, HEAD_DIM), F32),
            pltpu.VMEM((512, HEAD_DIM), F32),
            pltpu.VMEM((HEAD_DIM, HEAD_DIM), F32),
        ],
        compiler_params=params(32),
    )(mid_got, wide_got)
    returned = lax.all_to_all(results, "inner", 0, 0)
    return tuple(
        pl.pallas_call(
            assemble_kernel,
            out_shape=[shape(TOK, HIDDEN)] * 3,
            in_specs=[spec(pltpu.VMEM)] * 2 + [spec(pltpu.HBM)] * 3,
            out_specs=[spec(pltpu.HBM)] * 3,
            scratch_shapes=[
                pltpu.VMEM((3, heads, TOK, HEAD_DIM), BF16),
                pltpu.SemaphoreType.DMA((3, heads)),
            ],
            input_output_aliases={2: 0, 3: 1, 4: 2},
            compiler_params=params(16),
        )(offset_rows, returned, *near)
    )


def solution(mesh):
    rows = P(("outer", "inner"), None)
    return jax.shard_map(
        body,
        mesh=mesh,
        in_specs=(rows, rows, rows, rows, P()),
        out_specs=(rows, rows, rows),
        check_vma=False,
    )
```

time: 91.9 us -> 83.5 us (0.909)
  local copies, waits for them, and re-layouts: 9.98 us -> 0 us
  Pallas kernels: 8.5 us -> 12.3 us
  waiting for transfers between devices: 19.8 us -> 18.5 us
    unnamed x30 -> x0, local copies, waits for them, and re-layouts: 9.98 us -> none
    pallas_call x5, Pallas kernels: 8.5 us -> 12.3 us  [the longest x1 4.55 us: body(): pl.pallas_call(near_kernel, grid=(H_NEAR,), out_shape=[shape(TOK, HIDDEN)...]
    all_to_all x1, waiting for transfers between devices: 19.8 us -> 18.5 us  [body(): returned = lax.all_to_all(results, 'inner', 0, 0)]
  transfers between devices with their start and end apart: 1 -> 1, of which waited for: 1 -> 1; matrix products, arithmetic and copies ran while one was open for 0% -> 0% of each run, Pallas kernels for 2% -> 6%
where the time goes in v2:
time: 83.5 us; the launch traced here: 82.1 us
  blocking collectives  47.1 us (56%)
  waiting for transfers between devices  18.5 us (22%)
  Pallas kernels  12.3 us (15%)
  starting transfers between devices  3.59 us (4%)
    all_to_all x1, blocking collectives, body(): mid_got = lax.all_to_all(packed, 'inner', 0, 0)  35.9 us
    all_to_all x1, waiting for transfers between devices, body(): returned = lax.all_to_all(results, 'inner', 0, 0)  18.5 us
    all_to_all x1, blocking collectives, body(): wide_got = lax.all_to_all(wide_send, 'outer', 0, 0)  11.2 us
    pallas_call x1, Pallas kernels, body(): pl.pallas_call(near_kernel, grid=(H_NEAR,), out_shape=[shape(TOK, HIDDEN)...  4.55 us
    all_to_all x1, starting transfers between devices, body(): returned = lax.all_to_all(results, 'inner', 0, 0)  3.59 us
    pallas_call x1, Pallas kernels, body(): pl.pallas_call(worker_kernel, out_shape=shape(MEMBERS, 160, HEAD_DIM), in...  3.29 us
    pallas_call x1, Pallas kernels, body(): pl.pallas_call(pack_kernel, out_shape=[shape(MEMBERS, 96, 256), shape(hea...  2.74 us
  transfers between devices with their start and end apart: 1, of which 1 were waited for; matrix products, arithmetic and copies ran while one was open for 0% of the time, Pallas kernels for 6%

profile of v2, /device:TPU:2, one launch (start us, length us, event | category | flops | bytes accessed | tf_op | source)
XLA Modules:
  0.0 82.1 jit_solution(14283884414378039035)
XLA Ops:
  0.6 2.7 %shard_map.76 = (bf16[16,96,256]{2,1,0:T(8,128)(2,1)S(1)}, s32[8,128]{1,0:T(8,128)S(1)}) custom-call(s32[8]{0:T(128)} %off_hbm.1, bf16[256,1536]{1,0:T(8,128)(2,1)} %q_ref.1, bf16[256,1536]{1,0:T(8,128)(2,1)} %k_ref.1, bf16[256,1536]{1,0:T(8,128)(2,1)} %v_ref.1, bf16[256,1536]{1,0:T(8,128)(2,1)} %g_ref.1), custom_call_target="tpu_custom_call" | custom-call | tf_op jit(solution)/shard_map/pallas_call | solution.py:233
  3.4 35.9 %all_to_all.15.got_ref.mid_ref = bf16[16,96,256]{2,1,0:T(8,128)(2,1)S(1)} all-to-all(bf16[16,96,256]{2,1,0:T(8,128)(2,1)S(1)} %get-tuple-element.9), channel_id=1, replica_groups=mesh['outer'=16,'inner'=16] {'inner'}, dimensions={0} | all-to-all | bytes 1572864 | tf_op jit(solution)/shard_map/all_to_all | solution.py:260
  39.2 0.2 shard_map.77
  39.4 11.2 %all_to_all.16.wide_ref = bf16[16,48,256]{2,1,0:T(8,128)(2,1)S(1)} all-to-all(bf16[16,48,256]{2,1,0:T(8,128)(2,1)S(1)} %shard_map.77), channel_id=1, replica_groups=mesh['outer'=16,'inner'=16] {'outer'}, dimensions={0} | all-to-all | bytes 786432 | tf_op jit(solution)/shard_map/all_to_all | solution.py:268
  50.7 3.3 %shard_map.78 = bf16[16,160,128]{2,1,0:T(8,128)(2,1)} custom-call(bf16[16,96,256]{2,1,0:T(8,128)(2,1)S(1)} %all_to_all.15.got_ref.mid_ref, bf16[16,48,256]{2,1,0:T(8,128)(2,1)S(1)} %all_to_all.16.wide_ref), custom_call_target="tpu_custom_call" | custom-call | tf_op jit(solution)/shard_map/pallas_call | solution.py:269
  54.0 3.6 %all-to-all-start.2 = ((bf16[16,160,128]{2,1,0:T(8,128)(2,1)}), bf16[16,160,128]{2,1,0:T(8,128)(2,1)S(1)}, u32[]{:S(2)}, u32[]{:S(2)}) async-start(bf16[16,160,128]{2,1,0:T(8,128)(2,1)} %shard_map.78), calls=%async_computation.2 | async-start | bytes 1310720 | tf_op jit(solution)/shard_map/all_to_all | solution.py:281
  57.6 4.6 %shard_map.79 = (bf16[256,1536]{1,0:T(8,128)(2,1)}, bf16[256,1536]{1,0:T(8,128)(2,1)}, bf16[256,1536]{1,0:T(8,128)(2,1)}) custom-call(bf16[256,1536]{1,0:T(8,128)(2,1)} %q_ref.1, bf16[256,1536]{1,0:T(8,128)(2,1)} %k_ref.1, bf16[256,1536]{1,0:T(8,128)(2,1)} %v_ref.1, bf16[256,1536]{1,0:T(8,128)(2,1)} %g_ref.1), custom_call_target="tpu_custom_call" | custom-call | flops 335544320 | bytes 1835008 | tf_op jit(solution)/shard_map/pallas_call | solution.py:247
  62.1 18.5 %all-to-all-done.2.got_ref = bf16[16,160,128]{2,1,0:T(8,128)(2,1)S(1)} async-done(((bf16[16,160,128]{2,1,0:T(8,128)(2,1)}), bf16[16,160,128]{2,1,0:T(8,128)(2,1)S(1)}, u32[]{:S(2)}, u32[]{:S(2)}) %all-to-all-start.2) | async-done | bytes 655392 | tf_op jit(solution)/shard_map/all_to_all | solution.py:281
  80.6 1.5 %shard_map.80 = (bf16[256,1536]{1,0:T(8,128)(2,1)}, bf16[256,1536]{1,0:T(8,128)(2,1)}, bf16[256,1536]{1,0:T(8,128)(2,1)}) custom-call(s32[8,128]{1,0:T(8,128)S(1)} %get-tuple-element.8.off_ref, bf16[16,160,128]{2,1,0:T(8,128)(2,1)S(1)} %all-to-all-done.2.got_ref, ...), custom_call_target="tpu_custom_call", output_to_operand_aliasing={{0}: (2, {}), {1}: (3, {}), {2}: (4, {})} | custom-call | tf_op jit(solution)/shard_map/pallas_call | solution.py:283
Async XLA Ops:
  54.0 26.6 %all-to-all-start.2 = ((bf16[16,160,128]{2,1,0:T(8,128)(2,1)}), bf16[16,160,128]{2,1,0:T(8,128)(2,1)S(1)}, u32[]{:S(2)}, u32[]{:S(2)}) async-start(bf16[16,160,128]{2,1,0:T(8,128)(2,1)} %shard_map.78), calls=%async_computation.2 | async-start | bytes 1310720 | tf_op jit(solution)/shard_map/all_to_all | solution.py:281

commit v3 on v2

v3 whole, which is shorter than its diff:
```python
import math

import jax
import jax.numpy as jnp
from jax import lax
from jax.experimental import pallas as pl
from jax.experimental.pallas import tpu as pltpu
from jax.sharding import PartitionSpec as P

HEAD_DIM = 128
H_NEAR = 4
H_MID = 5
H_WIDE = 3
R_MID = 4
R_WIDE = 128
TOK = 256
NEAR_END = H_NEAR * HEAD_DIM
MID_END = NEAR_END + H_MID * HEAD_DIM
HIDDEN = MID_END + H_WIDE * HEAD_DIM
OUTERS = 16
MID_ROWS = TOK // R_MID
SLOTS = 8
HALVES = 2
HALF_KEYS = SLOTS * MID_ROWS
QUERY_BLOCK = 256
ALONG_Z = [[HALVES * z + half for z in range(SLOTS)] for half in range(HALVES)]
ACROSS_Y = [(member, member ^ 1) for member in range(HALVES * SLOTS)]
SCALE = 1.0 / math.sqrt(HEAD_DIM)
BF16 = jnp.bfloat16
F32 = jnp.float32


def dot(a, b):
    return lax.dot_general(a, b, (((1,), (0,)), ((), ())), preferred_element_type=F32)


def dot_nt(a, b):
    return lax.dot_general(a, b, (((1,), (1,)), ((), ())), preferred_element_type=F32)


def dot_tn(a, b):
    return lax.dot_general(a, b, (((0,), (0,)), ((), ())), preferred_element_type=F32)


def iota2(rows, columns):
    shape = (rows, columns)
    return (
        lax.broadcasted_iota(jnp.int32, shape, 0),
        lax.broadcasted_iota(jnp.int32, shape, 1),
    )


def one_hot(condition):
    return jnp.where(condition, 1.0, 0.0).astype(BF16)


def attention_transposed(query, key, value, gradient):
    scores = dot_nt(key, query) * SCALE
    exponent = jnp.exp(scores - jnp.max(scores, axis=0, keepdims=True))
    weights = exponent * (1.0 / jnp.sum(exponent, axis=0, keepdims=True))
    products = dot_nt(value, gradient)
    row_dots = jnp.sum(weights * products, axis=0, keepdims=True)
    score_gradients = (weights * (products - row_dots) * SCALE).astype(BF16)
    return weights.astype(BF16), score_gradients


def pack_kernel(off_hbm, q_hbm, k_hbm, v_hbm, g_hbm, out_ref, off_out, off_ref, held, off_sem, sems):
    off_copy = pltpu.make_async_copy(off_hbm, off_ref, off_sem)
    off_copy.start()
    order = list(range(H_MID, H_MID + H_WIDE)) + list(range(H_MID))
    copies = {}
    for head in order:
        for which, source in enumerate((q_hbm, k_hbm, v_hbm, g_hbm)):
            copies[head, which] = pltpu.make_async_copy(
                source.at[:, pl.ds(NEAR_END + head * HEAD_DIM, HEAD_DIM)],
                held.at[which, head],
                sems.at[which, head],
            )
            copies[head, which].start()
    off_copy.wait()
    for head in range(H_MID + H_WIDE):
        off_out[head : head + 1, :] = jnp.full((1, HEAD_DIM), off_ref[head], jnp.int32)
    row, column = iota2(16, TOK)
    for head in range(H_MID, H_MID + H_WIDE):
        offset = off_ref[head]
        pick_kv = one_hot((row < 2) & (column == offset + R_WIDE * row))
        pick_qg = one_hot((row >= 2) & (row < 4) & (column == offset + R_WIDE * (row - 2)))
        for which in range(4):
            copies[head, which].wait()
        kv = jnp.concatenate([held[1, head], held[2, head]], axis=1)
        qg = jnp.concatenate([held[0, head], held[3, head]], axis=1)
        out_ref[head, 0:16, :] = (dot(pick_kv, kv) + dot(pick_qg, qg)).astype(BF16)
        out_ref[head, 16:128, :] = jnp.zeros((112, 2 * HEAD_DIM), BF16)
    row, column = iota2(MID_ROWS, TOK)
    for head in range(H_MID):
        pick = one_hot(column == off_ref[head] + R_MID * row)
        for which in range(4):
            copies[head, which].wait()
        kv = jnp.concatenate([held[1, head], held[2, head]], axis=1)
        qg = jnp.concatenate([held[0, head], held[3, head]], axis=1)
        out_ref[head, 0:64, :] = dot(pick, kv).astype(BF16)
        out_ref[head, 64:128, :] = dot(pick, qg).astype(BF16)


def near_kernel(q_ref, k_ref, v_ref, g_ref, dq_ref, dk_ref, dv_ref):
    query, key, value, gradient = q_ref[...], k_ref[...], v_ref[...], g_ref[...]
    weights, score_gradients = attention_transposed(query, key, value, gradient)
    dq_ref[...] = dot_tn(score_gradients, key).astype(BF16)
    dk_ref[...] = dot(score_gradients, query).astype(BF16)
    dv_ref[...] = dot(weights, gradient).astype(BF16)


def slot():
    return lax.div(lax.axis_index("inner"), HALVES)


def mid_kernel(own_ref, other_ref, dq_ref, own_out, other_out, wide_out, dkv_ref):
    @pl.when(slot() >= H_MID)
    def forward_wide():
        rows = jnp.concatenate([own_ref[:, 0:16, :], other_ref[:, 0:16, :]], axis=0)
        rows = rows.reshape(2 * SLOTS * 16, 2 * HEAD_DIM)
        row, column = iota2(64, 2 * SLOTS * 16)
        place = row % 2 + jnp.where(row < 32, 0, 2)
        picked = dot(one_hot(column == 16 * ((row % 32) // 2) + place), rows).astype(BF16)
        for target in range(OUTERS):
            wide_out[target] = picked

    @pl.when(slot() < H_MID)
    def attend():
        kv = [ref[:, 0:64, :].reshape(HALF_KEYS, 2 * HEAD_DIM) for ref in (own_ref, other_ref)]
        kv = jnp.concatenate(kv, axis=0)
        key, value = kv[:, :HEAD_DIM], kv[:, HEAD_DIM:]
        qg = own_ref[:, 64:128, :].reshape(HALF_KEYS, 2 * HEAD_DIM)
        for start in range(0, HALF_KEYS, QUERY_BLOCK):
            query = qg[start : start + QUERY_BLOCK, :HEAD_DIM]
            gradient = qg[start : start + QUERY_BLOCK, HEAD_DIM:]
            weights, score_gradients = attention_transposed(query, key, value, gradient)
            dk, dv = dot(score_gradients, query), dot(weights, gradient)
            if start == 0:
                dkv_ref[:, :HEAD_DIM] = dk
                dkv_ref[:, HEAD_DIM:] = dv
            else:
                dkv_ref[:, :HEAD_DIM] += dk
                dkv_ref[:, HEAD_DIM:] += dv
            dq = dot_tn(key, score_gradients).T.astype(BF16)
            blocks = slice(start // MID_ROWS, (start + QUERY_BLOCK) // MID_ROWS)
            dq_ref[blocks] = dq.reshape(QUERY_BLOCK // MID_ROWS, MID_ROWS, HEAD_DIM)
        own_out[...] = dkv_ref[:HALF_KEYS, :]
        other = dkv_ref[HALF_KEYS:, :].astype(BF16)
        other_out[...] = other.reshape(SLOTS, MID_ROWS, 2 * HEAD_DIM)


def return_kernel(wide_ref, dq_ref, own_ref, back_ref, out_ref):
    @pl.when(slot() < H_MID)
    def add_halves():
        out_ref[:, 0:64, :] = dq_ref[...]
        back = back_ref[...].reshape(HALF_KEYS, 2 * HEAD_DIM).astype(F32)
        dkv = (own_ref[...] + back).astype(BF16)
        out_ref[:, 64:128, :] = dkv[:, :HEAD_DIM].reshape(SLOTS, MID_ROWS, HEAD_DIM)
        out_ref[:, 128:192, :] = dkv[:, HEAD_DIM:].reshape(SLOTS, MID_ROWS, HEAD_DIM)

    @pl.when(slot() >= H_MID)
    def attend_wide():
        kv = wide_ref[:, 0:32, :].reshape(OUTERS * 32, 2 * HEAD_DIM)
        qg = wide_ref[:, 32:64, :].reshape(OUTERS * 32, 2 * HEAD_DIM)
        key, value = kv[:, :HEAD_DIM], kv[:, HEAD_DIM:]
        query, gradient = qg[:, :HEAD_DIM], qg[:, HEAD_DIM:]
        scores = dot_nt(key, query) * SCALE
        top = jnp.max(scores, axis=0, keepdims=True)
        exponent = jnp.exp(scores - top)
        inverse = 1.0 / jnp.sum(exponent, axis=0, keepdims=True)
        products = dot_nt(value, gradient)
        row_dots = jnp.sum(exponent * inverse * products, axis=0, keepdims=True)
        outer = lax.axis_index("outer")
        own_kv, own_qg = wide_ref[outer, 0:16, :], wide_ref[outer, 32:48, :]
        own_key, own_value = own_kv[:, :HEAD_DIM], own_kv[:, HEAD_DIM:]
        own_query, own_gradient = own_qg[:, :HEAD_DIM], own_qg[:, HEAD_DIM:]
        weights = jnp.exp(dot_nt(own_key, query) * SCALE - top) * inverse
        score_gradients = weights * (dot_nt(own_value, gradient) - row_dots) * SCALE
        dk = dot(score_gradients.astype(BF16), query).astype(BF16)
        dv = dot(weights.astype(BF16), gradient).astype(BF16)
        scores = dot_nt(own_query, key) * SCALE
        exponent = jnp.exp(scores - jnp.max(scores, axis=1, keepdims=True))
        weights = exponent * (1.0 / jnp.sum(exponent, axis=1, keepdims=True))
        products = dot_nt(own_gradient, value)
        row_dots = jnp.sum(weights * products, axis=1, keepdims=True)
        score_gradients = weights * (products - row_dots) * SCALE
        dq = dot(score_gradients.astype(BF16), key).astype(BF16)
        row, column = iota2(SLOTS * 16, 16)
        member, place = row // 16, row % 16
        spread = 0.0
        for which, rows in enumerate((dq, dk, dv)):
            mine = (place >= 2 * which) & (place < 2 * which + 2)
            spread += dot(one_hot(mine & (column == 2 * member + place - 2 * which)), rows)
        out_ref[:, 0:16, :] = spread.astype(BF16).reshape(SLOTS, 16, HEAD_DIM)


def assemble_kernel(off_ref, got_ref, nq, nk, nv, dq_hbm, dk_hbm, dv_hbm, held, sems):
    copies = []

    def send(which, head, block):
        held[which, head] = block.astype(BF16)
        target = (dq_hbm, dk_hbm, dv_hbm)[which]
        copy = pltpu.make_async_copy(
            held.at[which, head],
            target.at[:, pl.ds(NEAR_END + head * HEAD_DIM, HEAD_DIM)],
            sems.at[which, head],
        )
        copy.start()
        copies.append(copy)

    row, unused = iota2(TOK, HEAD_DIM)
    for head in range(H_MID, H_MID + H_WIDE):
        offset = off_ref[head : head + 1, :]
        rows = got_ref[head, 0:16, :].astype(F32)
        first, second = row == offset, row == offset + R_WIDE
        for which in range(3):
            spread = jnp.where(first, rows[2 * which : 2 * which + 1], 0.0)
            send(which, head, jnp.where(second, rows[2 * which + 1 : 2 * which + 2], spread))
    row, column = iota2(TOK, MID_ROWS)
    for head in range(H_MID):
        place = one_hot(row - R_MID * column == off_ref[head : head + 1, :1])
        for which in range(3):
            send(which, head, dot(place, got_ref[head, 64 * which : 64 * which + 64, :]))
    for copy in copies:
        copy.wait()


def spec(space):
    return pl.BlockSpec(memory_space=space)


def in_hbm(array):
    return pltpu.with_memory_space_constraint(array, pltpu.HBM)


def params(mebibytes):
    return pltpu.CompilerParams(vmem_limit_bytes=mebibytes * 1024 * 1024)


def shape(*sizes, kind=BF16):
    return jax.ShapeDtypeStruct(sizes, kind)


def body(queries, key_rows, values, out_grads, offsets):
    arrays = [in_hbm(array) for array in (queries, key_rows, values, out_grads)]
    heads = H_MID + H_WIDE
    packed, offset_rows = pl.pallas_call(
        pack_kernel,
        out_shape=[shape(SLOTS, 128, 256), shape(heads, HEAD_DIM, kind=jnp.int32)],
        in_specs=[spec(pltpu.HBM)] * 5,
        out_specs=[spec(pltpu.VMEM)] * 2,
        scratch_shapes=[
            pltpu.SMEM((heads,), jnp.int32),
            pltpu.VMEM((4, heads, TOK, HEAD_DIM), BF16),
            pltpu.SemaphoreType.DMA,
            pltpu.SemaphoreType.DMA((4, heads)),
        ],
        compiler_params=params(16),
    )(in_hbm(offsets), *arrays)
    near_block = pl.BlockSpec((TOK, HEAD_DIM), lambda head: (0, head))
    near = pl.pallas_call(
        near_kernel,
        grid=(H_NEAR,),
        out_shape=[shape(TOK, HIDDEN)] * 3,
        in_specs=[near_block] * 4,
        out_specs=[near_block] * 3,
        cost_estimate=pl.CostEstimate(
            flops=10 * H_NEAR * TOK * TOK * HEAD_DIM,
            bytes_accessed=14 * TOK * NEAR_END,
            transcendentals=H_NEAR * TOK * TOK,
        ),
        compiler_params=params(16),
    )(*arrays)
    own = lax.all_to_all(packed, "inner", 0, 0, axis_index_groups=ALONG_Z)
    other = lax.ppermute(own[:, 0:64, :], "inner", ACROSS_Y)
    dq, own_sums, other_sums, wide_send = pl.pallas_call(
        mid_kernel,
        out_shape=[
            shape(SLOTS, MID_ROWS, HEAD_DIM),
            shape(HALF_KEYS, 256, kind=F32),
            shape(SLOTS, MID_ROWS, 256),
            shape(OUTERS, 64, 256),
        ],
        in_specs=[spec(pltpu.VMEM)] * 2,
        out_specs=[spec(pltpu.VMEM)] * 4,
        scratch_shapes=[pltpu.VMEM((HALVES * HALF_KEYS, 256), F32)],
        compiler_params=params(32),
    )(own, other)
    back = lax.ppermute(other_sums, "inner", ACROSS_Y)
    wide_got = lax.all_to_all(wide_send, "outer", 0, 0)
    results = pl.pallas_call(
        return_kernel,
        out_shape=shape(SLOTS, 192, HEAD_DIM),
        in_specs=[spec(pltpu.VMEM)] * 4,
        out_specs=spec(pltpu.VMEM),
        compiler_params=params(32),
    )(wide_got, dq, own_sums, back)
    returned = lax.all_to_all(results, "inner", 0, 0, axis_index_groups=ALONG_Z)
    return tuple(
        pl.pallas_call(
            assemble_kernel,
            out_shape=[shape(TOK, HIDDEN)] * 3,
            in_specs=[spec(pltpu.VMEM)] * 2 + [spec(pltpu.HBM)] * 3,
            out_specs=[spec(pltpu.HBM)] * 3,
            scratch_shapes=[
                pltpu.VMEM((3, heads, TOK, HEAD_DIM), BF16),
                pltpu.SemaphoreType.DMA((3, heads)),
            ],
            input_output_aliases={2: 0, 3: 1, 4: 2},
            compiler_params=params(16),
        )(offset_rows, returned, *near)
    )


def solution(mesh):
    rows = P(("outer", "inner"), None)
    return jax.shard_map(
        body,
        mesh=mesh,
        in_specs=(rows, rows, rows, rows, P()),
        out_specs=(rows, rows, rows),
        check_vma=False,
    )
```

time: 83.5 us -> 83.7 us (level)
  blocking collectives: 47.1 us -> 25.8 us
  starting transfers between devices: 3.59 us -> 15.5 us
  waiting for transfers between devices: 18.5 us -> 27.4 us
    all_to_all x2 -> x1, blocking collectives: 47.1 us -> 25.8 us  [body(): own = lax.all_to_all(packed, 'inner', 0, 0, axis_index_groups=ALONG_Z)]
    ppermute x0 -> x2, waiting for transfers between devices: none -> 17.1 us  [the longest x1 12.4 us: body(): back = lax.ppermute(other_sums, 'inner', ACROSS_Y)]
    all_to_all x1 -> x2, waiting for transfers between devices: 18.5 us -> 10.3 us  [the longest x1 10.3 us: body(): returned = lax.all_to_all(results, 'inner', 0, 0, axis_index_groups=ALONG_Z)]
    ppermute x0 -> x2, starting transfers between devices: none -> 6.18 us  [the longest x1 3.28 us: body(): other = lax.ppermute(own[:, 0:64, :], 'inner', ACROSS_Y)]
    all_to_all x1 -> x2, starting transfers between devices: 3.59 us -> 9.31 us  [the longest x1 5.86 us: body(): wide_got = lax.all_to_all(wide_send, 'outer', 0, 0)]
  transfers between devices with their start and end apart: 1 -> 4, of which waited for: 1 -> 3; matrix products, arithmetic and copies ran while one was open for 0% -> 0% of each run, Pallas kernels for 6% -> 6%
where the time goes in v3:
time: 83.7 us; the launch traced here: 82.1 us
  waiting for transfers between devices  27.4 us (33%)
  blocking collectives  25.8 us (31%)
  starting transfers between devices  15.5 us (19%)
  Pallas kernels  12.8 us (15%)
    all_to_all x1, blocking collectives, body(): own = lax.all_to_all(packed, 'inner', 0, 0, axis_index_groups=ALONG_Z)  25.8 us
    ppermute x1, waiting for transfers between devices, body(): back = lax.ppermute(other_sums, 'inner', ACROSS_Y)  12.4 us
    all_to_all x1, waiting for transfers between devices, body(): returned = lax.all_to_all(results, 'inner', 0, 0, axis_index_groups=ALONG_Z)  10.3 us
    all_to_all x1, starting transfers between devices, body(): wide_got = lax.all_to_all(wide_send, 'outer', 0, 0)  5.86 us
    ppermute x1, waiting for transfers between devices, body(): other = lax.ppermute(own[:, 0:64, :], 'inner', ACROSS_Y)  4.68 us
    pallas_call x1, Pallas kernels, body(): pl.pallas_call(near_kernel, grid=(H_NEAR,), out_shape=[shape(TOK, HIDDEN)...  4.54 us
    all_to_all x1, starting transfers between devices, body(): returned = lax.all_to_all(results, 'inner', 0, 0, axis_index_groups=ALONG_Z)  3.45 us
    ppermute x1, starting transfers between devices, body(): other = lax.ppermute(own[:, 0:64, :], 'inner', ACROSS_Y)  3.28 us
  transfers between devices with their start and end apart: 4, of which 3 were waited for; matrix products, arithmetic and copies ran while one was open for 0% of the time, Pallas kernels for 6%

profile of v3, /device:TPU:2, one launch (start us, length us, event | category | flops | bytes accessed | tf_op | source)
XLA Modules:
  0.0 82.1 jit_solution(18416043231226674455)
XLA Ops:
  0.6 2.7 %shard_map.76 = (bf16[8,128,256]{2,1,0:T(8,128)(2,1)S(1)}, s32[8,128]{1,0:T(8,128)S(1)}) custom-call(s32[8]{0:T(128)} %off_hbm.1, bf16[256,1536]{1,0:T(8,128)(2,1)} %q_ref.1, bf16[256,1536]{1,0:T(8,128)(2,1)} %k_ref.1, bf16[256,1536]{1,0:T(8,128)(2,1)} %v_ref.1, bf16[256,1536]{1,0:T(8,128)(2,1)} %g_ref.1), custom_call_target="tpu_custom_call" | custom-call | tf_op jit(solution)/shard_map/pallas_call | solution.py:248
  3.4 25.8 %all_to_all.15.own_ref = bf16[8,128,256]{2,1,0:T(8,128)(2,1)S(1)} all-to-all(bf16[8,128,256]{2,1,0:T(8,128)(2,1)S(1)} %get-tuple-element.13), channel_id=1, replica_groups={{0,2,4,6,8,10,12,14},{1,3,5,7,9,11,13,15},{16,18,20,22,24,26,28,30},{17..., dimensions={0} | all-to-all | bytes 1048576 | tf_op jit(solution)/shard_map/all_to_all | solution.py:275
  29.2 3.3 %collective-permute-start = (bf16[8,64,256]{2,1,0:T(8,128)(2,1)S(1)}, bf16[8,64,256]{2,1,0:T(8,128)(2,1)S(1)}, u32[]{:S(2)}, u32[]{:S(2)}) collective-permute-start(bf16[8,64,256]{2,1,0:T(8,128)(2,1)S(1)} %slice.4), channel_id=1, source_target_pairs={{0,1},{1,0},{2,3},{3,2},{4,5},{5,4},{6,7},{7,6},{8,9},{9,8},{10,11... | collective-permute-start | bytes 786440 | tf_op jit(solution)/shard_map/ppermute | solution.py:276
  32.4 4.7 %collective-permute-done.other_ref = bf16[8,64,256]{2,1,0:T(8,128)(2,1)S(1)} collective-permute-done((bf16[8,64,256]{2,1,0:T(8,128)(2,1)S(1)}, bf16[8,64,256]{2,1,0:T(8,128)(2,1)S(1)}, u32[]{:S(2)}, u32[]{:S(2)}) %collective-permute-start) | collective-permute-done | bytes 262176 | tf_op jit(solution)/shard_map/ppermute | solution.py:276
  37.1 3.2 %shard_map.77 = (bf16[8,64,128]{2,1,0:T(8,128)(2,1)S(1)}, f32[512,256]{1,0:T(8,128)S(1)}, bf16[8,64,256]{2,1,0:T(8,128)(2,1)S(1)}, bf16[16,64,256]{2,1,0:T(8,128)(2,1)}) custom-call(bf16[8,128,256]{2,1,0:T(8,128)(2,1)S(1)} %all_to_all.15.own_ref, bf16[8,64,256]{2,1,0:T(8,128)(2,1)S(1)} %collective-permute-done.other_ref), custom_call_target="tpu_custom_call" | custom-call | tf_op jit(solution)/shard_map/pallas_call | solution.py:277
  40.4 5.9 %all-to-all-start.1 = ((bf16[16,64,256]{2,1,0:T(8,128)(2,1)}), bf16[16,64,256]{2,1,0:T(8,128)(2,1)S(1)}, u32[]{:S(2)}, u32[]{:S(2)}) async-start(bf16[16,64,256]{2,1,0:T(8,128)(2,1)} %get-tuple-element.14), calls=%async_computation.1 | async-start | bytes 1048576 | tf_op jit(solution)/shard_map/all_to_all | solution.py:291
  46.2 2.9 %collective-permute-start.1 = (bf16[8,64,256]{2,1,0:T(8,128)(2,1)S(1)}, bf16[8,64,256]{2,1,0:T(8,128)(2,1)S(1)}, u32[]{:S(2)}, u32[]{:S(2)}) collective-permute-start(bf16[8,64,256]{2,1,0:T(8,128)(2,1)S(1)} %get-tuple-element.17), channel_id=1, source_target_pairs={{0,1},{1,0},{2,3},{3,2},{4,5},{5,4},{6,7},{7,6},{8,9},{9,8},{10,11... | collective-permute-start | bytes 786440 | tf_op jit(solution)/shard_map/ppermute | solution.py:290
  49.1 12.4 %collective-permute-done.1.back_ref = bf16[8,64,256]{2,1,0:T(8,128)(2,1)S(1)} collective-permute-done((bf16[8,64,256]{2,1,0:T(8,128)(2,1)S(1)}, bf16[8,64,256]{2,1,0:T(8,128)(2,1)S(1)}, u32[]{:S(2)}, u32[]{:S(2)}) %collective-permute-start.1) | collective-permute-done | bytes 262176 | tf_op jit(solution)/shard_map/ppermute | solution.py:290
  61.6 0.0 all-to-all-done.1.wide_ref
  61.6 0.8 shard_map.78
  62.4 3.5 %all-to-all-start.2 = ((bf16[8,192,128]{2,1,0:T(8,128)(2,1)}), bf16[8,192,128]{2,1,0:T(8,128)(2,1)S(1)}, u32[]{:S(2)}, u32[]{:S(2)}) async-start(bf16[8,192,128]{2,1,0:T(8,128)(2,1)} %shard_map.78), calls=%async_computation.2 | async-start | bytes 786432 | tf_op jit(solution)/shard_map/all_to_all | solution.py:299
  65.8 4.5 %shard_map.79 = (bf16[256,1536]{1,0:T(8,128)(2,1)}, bf16[256,1536]{1,0:T(8,128)(2,1)}, bf16[256,1536]{1,0:T(8,128)(2,1)}) custom-call(bf16[256,1536]{1,0:T(8,128)(2,1)} %q_ref.1, bf16[256,1536]{1,0:T(8,128)(2,1)} %k_ref.1, bf16[256,1536]{1,0:T(8,128)(2,1)} %v_ref.1, bf16[256,1536]{1,0:T(8,128)(2,1)} %g_ref.1), custom_call_target="tpu_custom_call" | custom-call | flops 335544320 | bytes 1835008 | tf_op jit(solution)/shard_map/pallas_call | solution.py:262
  70.4 10.3 %all-to-all-done.2.got_ref = bf16[8,192,128]{2,1,0:T(8,128)(2,1)S(1)} async-done(((bf16[8,192,128]{2,1,0:T(8,128)(2,1)}), bf16[8,192,128]{2,1,0:T(8,128)(2,1)S(1)}, u32[]{:S(2)}, u32[]{:S(2)}) %all-to-all-start.2) | async-done | bytes 393248 | tf_op jit(solution)/shard_map/all_to_all | solution.py:299
  80.6 1.5 %shard_map.80 = (bf16[256,1536]{1,0:T(8,128)(2,1)}, bf16[256,1536]{1,0:T(8,128)(2,1)}, bf16[256,1536]{1,0:T(8,128)(2,1)}) custom-call(s32[8,128]{1,0:T(8,128)S(1)} %get-tuple-element.12.off_ref, bf16[8,192,128]{2,1,0:T(8,128)(2,1)S(1)} %all-to-all-done.2.got_ref, ...), custom_call_target="tpu_custom_call", output_to_operand_aliasing={{0}: (2, {}), {1}: (3, {}), {2}: (4, {})} | custom-call | tf_op jit(solution)/shard_map/pallas_call | solution.py:301
  (1 shorter events, 0.0 us)
Async XLA Ops:
  29.2 8.0 %collective-permute-start = (bf16[8,64,256]{2,1,0:T(8,128)(2,1)S(1)}, bf16[8,64,256]{2,1,0:T(8,128)(2,1)S(1)}, u32[]{:S(2)}, u32[]{:S(2)}) collective-permute-start(bf16[8,64,256]{2,1,0:T(8,128)(2,1)S(1)} %slice.4), channel_id=1, source_target_pairs={{0,1},{1,0},{2,3},{3,2},{4,5},{5,4},{6,7},{7,6},{8,9},{9,8},{10,11... | collective-permute-start | bytes 786440 | tf_op jit(solution)/shard_map/ppermute | solution.py:276
  40.4 21.2 %all-to-all-start.1 = ((bf16[16,64,256]{2,1,0:T(8,128)(2,1)}), bf16[16,64,256]{2,1,0:T(8,128)(2,1)S(1)}, u32[]{:S(2)}, u32[]{:S(2)}) async-start(bf16[16,64,256]{2,1,0:T(8,128)(2,1)} %get-tuple-element.14), calls=%async_computation.1 | async-start | bytes 1048576 | tf_op jit(solution)/shard_map/all_to_all | solution.py:291
  46.2 15.3 %collective-permute-start.1 = (bf16[8,64,256]{2,1,0:T(8,128)(2,1)S(1)}, bf16[8,64,256]{2,1,0:T(8,128)(2,1)S(1)}, u32[]{:S(2)}, u32[]{:S(2)}) collective-permute-start(bf16[8,64,256]{2,1,0:T(8,128)(2,1)S(1)} %get-tuple-element.17), channel_id=1, source_target_pairs={{0,1},{1,0},{2,3},{3,2},{4,5},{5,4},{6,7},{7,6},{8,9},{9,8},{10,11... | collective-permute-start | bytes 786440 | tf_op jit(solution)/shard_map/ppermute | solution.py:290
  62.4 18.3 %all-to-all-start.2 = ((bf16[8,192,128]{2,1,0:T(8,128)(2,1)}), bf16[8,192,128]{2,1,0:T(8,128)(2,1)S(1)}, u32[]{:S(2)}, u32[]{:S(2)}) async-start(bf16[8,192,128]{2,1,0:T(8,128)(2,1)} %shard_map.78), calls=%async_computation.2 | async-start | bytes 786432 | tf_op jit(solution)/shard_map/all_to_all | solution.py:299

commit v4 on v3

v4 whole, which is shorter than its diff:
```python
import math

import jax
import jax.numpy as jnp
from jax import lax
from jax.experimental import pallas as pl
from jax.experimental.pallas import tpu as pltpu
from jax.sharding import PartitionSpec as P

HEAD_DIM = 128
H_NEAR = 4
H_MID = 5
H_WIDE = 3
R_MID = 4
R_WIDE = 128
TOK = 256
NEAR_END = H_NEAR * HEAD_DIM
MID_END = NEAR_END + H_MID * HEAD_DIM
HIDDEN = MID_END + H_WIDE * HEAD_DIM
OUTERS = 16
MID_ROWS = TOK // R_MID
SLOTS = 8
HALVES = 2
HALF_KEYS = SLOTS * MID_ROWS
QUERY_BLOCK = 256
ALONG_Z = [[HALVES * z + half for z in range(SLOTS)] for half in range(HALVES)]
ACROSS_Y = [(member, member ^ 1) for member in range(HALVES * SLOTS)]
SCALE = 1.0 / math.sqrt(HEAD_DIM)
BF16 = jnp.bfloat16
F32 = jnp.float32


def dot(a, b):
    return lax.dot_general(a, b, (((1,), (0,)), ((), ())), preferred_element_type=F32)


def dot_nt(a, b):
    return lax.dot_general(a, b, (((1,), (1,)), ((), ())), preferred_element_type=F32)


def dot_tn(a, b):
    return lax.dot_general(a, b, (((0,), (0,)), ((), ())), preferred_element_type=F32)


def iota2(rows, columns):
    shape = (rows, columns)
    return (
        lax.broadcasted_iota(jnp.int32, shape, 0),
        lax.broadcasted_iota(jnp.int32, shape, 1),
    )


def one_hot(condition):
    return jnp.where(condition, 1.0, 0.0).astype(BF16)


def attention_transposed(query, key, value, gradient):
    scores = dot_nt(key, query) * SCALE
    exponent = jnp.exp(scores - jnp.max(scores, axis=0, keepdims=True))
    weights = exponent * (1.0 / jnp.sum(exponent, axis=0, keepdims=True))
    products = dot_nt(value, gradient)
    row_dots = jnp.sum(weights * products, axis=0, keepdims=True)
    score_gradients = (weights * (products - row_dots) * SCALE).astype(BF16)
    return weights.astype(BF16), score_gradients


def fetch(sources, held, sems, heads):
    copies = {}
    for at, head in enumerate(heads):
        for which, source in enumerate(sources):
            copies[head, which] = pltpu.make_async_copy(
                source.at[:, pl.ds(NEAR_END + head * HEAD_DIM, HEAD_DIM)],
                held.at[which, at],
                sems.at[which, at],
            )
            copies[head, which].start()
    return copies


def pairs(copies, held, head, at):
    for which in range(4):
        copies[head, which].wait()
    kv = jnp.concatenate([held[1, at], held[2, at]], axis=1)
    qg = jnp.concatenate([held[0, at], held[3, at]], axis=1)
    return kv, qg


def wide_kernel(off_hbm, q_hbm, k_hbm, v_hbm, g_hbm, out_ref, off_out, off_ref, held, off_sem, sems):
    off_copy = pltpu.make_async_copy(off_hbm, off_ref, off_sem)
    off_copy.start()
    heads = range(H_MID, H_MID + H_WIDE)
    copies = fetch((q_hbm, k_hbm, v_hbm, g_hbm), held, sems, heads)
    off_copy.wait()
    for head in range(H_MID + H_WIDE):
        off_out[head : head + 1, :] = jnp.full((1, TOK), off_ref[head], jnp.int32)
    row, column = iota2(16, TOK)
    rows = 0.0
    for at, head in enumerate(heads):
        kv, qg = pairs(copies, held, head, at)
        offset = off_ref[head]
        for start, block in ((2 * at, kv), (6 + 2 * at, qg)):
            mine = (row >= start) & (row < start + 2)
            rows += dot(one_hot(mine & (column == offset + R_WIDE * (row - start))), block)
    rows = rows.astype(BF16)
    for target in range(OUTERS):
        out_ref[target] = rows


def mid_pack_kernel(off_ref, q_hbm, k_hbm, v_hbm, g_hbm, out_ref, held, sems):
    copies = fetch((q_hbm, k_hbm, v_hbm, g_hbm), held, sems, range(H_MID))
    row, column = iota2(MID_ROWS, TOK)
    for head in range(H_MID):
        pick = one_hot(column - R_MID * row == off_ref[head : head + 1, :])
        kv, qg = pairs(copies, held, head, head)
        out_ref[head, 0:64, :] = dot(pick, kv).astype(BF16)
        out_ref[head, 64:128, :] = dot(pick, qg).astype(BF16)
    for head in range(H_MID, SLOTS):
        out_ref[head, 64:128, :] = jnp.zeros((64, 2 * HEAD_DIM), BF16)


def wide_pack_kernel(got_ref, packed, out, held, sems):
    rows = got_ref[...].reshape(OUTERS * 16, 2 * HEAD_DIM)
    row, column = iota2(64, OUTERS * 16)
    base = 16 * ((row % 32) // 2) + row % 2 + jnp.where(row < 32, 0, 6)
    copies = []
    for head in range(H_WIDE):
        held[head] = dot(one_hot(column == base + 2 * head), rows).astype(BF16)
        copy = pltpu.make_async_copy(
            held.at[head], out.at[H_MID + head, pl.ds(0, 64)], sems.at[head]
        )
        copy.start()
        copies.append(copy)
    for copy in copies:
        copy.wait()


def near_kernel(after, q_ref, k_ref, v_ref, g_ref, dq_ref, dk_ref, dv_ref):
    query, key, value, gradient = q_ref[...], k_ref[...], v_ref[...], g_ref[...]
    weights, score_gradients = attention_transposed(query, key, value, gradient)
    dq_ref[...] = dot_tn(score_gradients, key).astype(BF16)
    dk_ref[...] = dot(score_gradients, query).astype(BF16)
    dv_ref[...] = dot(weights, gradient).astype(BF16)


def slot():
    return lax.div(lax.axis_index("inner"), HALVES)


def attend_wide(own_ref, other_ref, out_ref):
    wide_rows = SLOTS * 32
    kv = [ref[:, 0:32, :].reshape(wide_rows, 2 * HEAD_DIM) for ref in (own_ref, other_ref)]
    qg = [ref[:, 32:64, :].reshape(wide_rows, 2 * HEAD_DIM) for ref in (own_ref, other_ref)]
    row, column = iota2(16, wide_rows)
    source = 32 * (row // 2) + 2 * lax.axis_index("outer") + row % 2
    pick = one_hot(column == source)
    own_kv, own_qg = dot(pick, kv[0]).astype(BF16), dot(pick, qg[0]).astype(BF16)
    kv, qg = jnp.concatenate(kv, axis=0), jnp.concatenate(qg, axis=0)
    key, value = kv[:, :HEAD_DIM], kv[:, HEAD_DIM:]
    query, gradient = qg[:, :HEAD_DIM], qg[:, HEAD_DIM:]
    scores = dot_nt(key, query) * SCALE
    top = jnp.max(scores, axis=0, keepdims=True)
    exponent = jnp.exp(scores - top)
    inverse = 1.0 / jnp.sum(exponent, axis=0, keepdims=True)
    products = dot_nt(value, gradient)
    row_dots = jnp.sum(exponent * inverse * products, axis=0, keepdims=True)
    own_key, own_value = own_kv[:, :HEAD_DIM], own_kv[:, HEAD_DIM:]
    own_query, own_gradient = own_qg[:, :HEAD_DIM], own_qg[:, HEAD_DIM:]
    weights = jnp.exp(dot_nt(own_key, query) * SCALE - top) * inverse
    score_gradients = weights * (dot_nt(own_value, gradient) - row_dots) * SCALE
    dk = dot(score_gradients.astype(BF16), query).astype(BF16)
    dv = dot(weights.astype(BF16), gradient).astype(BF16)
    scores = dot_nt(own_query, key) * SCALE
    exponent = jnp.exp(scores - jnp.max(scores, axis=1, keepdims=True))
    weights = exponent * (1.0 / jnp.sum(exponent, axis=1, keepdims=True))
    products = dot_nt(own_gradient, value)
    row_dots = jnp.sum(weights * products, axis=1, keepdims=True)
    score_gradients = weights * (products - row_dots) * SCALE
    dq = dot(score_gradients.astype(BF16), key).astype(BF16)
    row, column = iota2(SLOTS * 16, 16)
    member, place = row // 16, row % 16
    spread = 0.0
    for which, rows in enumerate((dq, dk, dv)):
        mine = (place >= 2 * which) & (place < 2 * which + 2)
        spread += dot(one_hot(mine & (column == 2 * member + place - 2 * which)), rows)
    out_ref[...] = spread.astype(BF16).reshape(SLOTS, 16, HEAD_DIM)


def work_kernel(own_ref, other_ref, dq_ref, own_out, wide_out, other_out, dkv_ref):
    @pl.when(slot() >= H_MID)
    def wide():
        attend_wide(own_ref, other_ref, wide_out)

    @pl.when(slot() < H_MID)
    def attend():
        kv = [ref[:, 0:64, :].reshape(HALF_KEYS, 2 * HEAD_DIM) for ref in (own_ref, other_ref)]
        kv = jnp.concatenate(kv, axis=0)
        key, value = kv[:, :HEAD_DIM], kv[:, HEAD_DIM:]
        qg = own_ref[:, 64:128, :].reshape(HALF_KEYS, 2 * HEAD_DIM)
        for start in range(0, HALF_KEYS, QUERY_BLOCK):
            query = qg[start : start + QUERY_BLOCK, :HEAD_DIM]
            gradient = qg[start : start + QUERY_BLOCK, HEAD_DIM:]
            weights, score_gradients = attention_transposed(query, key, value, gradient)
            dk, dv = dot(score_gradients, query), dot(weights, gradient)
            if start == 0:
                dkv_ref[:, :HEAD_DIM] = dk
                dkv_ref[:, HEAD_DIM:] = dv
            else:
                dkv_ref[:, :HEAD_DIM] += dk
                dkv_ref[:, HEAD_DIM:] += dv
            dq = dot_tn(key, score_gradients).T.astype(BF16)
            blocks = slice(start // MID_ROWS, (start + QUERY_BLOCK) // MID_ROWS)
            dq_ref[blocks] = dq.reshape(QUERY_BLOCK // MID_ROWS, MID_ROWS, HEAD_DIM)
        own_out[...] = dkv_ref[:HALF_KEYS, :]
        other = dkv_ref[HALF_KEYS:, :].astype(BF16)
        other_out[...] = other.reshape(SLOTS, MID_ROWS, 2 * HEAD_DIM)


def return_kernel(dq_ref, own_ref, wide_ref, back_ref, out_ref):
    @pl.when(slot() < H_MID)
    def add_halves():
        out_ref[:, 0:64, :] = dq_ref[...]
        back = back_ref[...].reshape(HALF_KEYS, 2 * HEAD_DIM).astype(F32)
        dkv = (own_ref[...] + back).astype(BF16)
        out_ref[:, 64:128, :] = dkv[:, :HEAD_DIM].reshape(SLOTS, MID_ROWS, HEAD_DIM)
        out_ref[:, 128:192, :] = dkv[:, HEAD_DIM:].reshape(SLOTS, MID_ROWS, HEAD_DIM)

    @pl.when(slot() >= H_MID)
    def wide():
        out_ref[:, 0:16, :] = wide_ref[...]


def assemble_kernel(off_ref, got_ref, nq, nk, nv, dq_hbm, dk_hbm, dv_hbm, held, sems):
    copies = []

    def send(which, head, block):
        held[which, head] = block.astype(BF16)
        target = (dq_hbm, dk_hbm, dv_hbm)[which]
        copy = pltpu.make_async_copy(
            held.at[which, head],
            target.at[:, pl.ds(NEAR_END + head * HEAD_DIM, HEAD_DIM)],
            sems.at[which, head],
        )
        copy.start()
        copies.append(copy)

    row, unused = iota2(TOK, HEAD_DIM)
    for head in range(H_MID, H_MID + H_WIDE):
        offset = off_ref[head : head + 1, :HEAD_DIM]
        rows = got_ref[head, 0:16, :].astype(F32)
        first, second = row == offset, row == offset + R_WIDE
        for which in range(3):
            spread = jnp.where(first, rows[2 * which : 2 * which + 1], 0.0)
            send(which, head, jnp.where(second, rows[2 * which + 1 : 2 * which + 2], spread))
    row, column = iota2(TOK, MID_ROWS)
    for head in range(H_MID):
        place = one_hot(row - R_MID * column == off_ref[head : head + 1, :1])
        for which in range(3):
            send(which, head, dot(place, got_ref[head, 64 * which : 64 * which + 64, :]))
    for copy in copies:
        copy.wait()


def spec(space):
    return pl.BlockSpec(memory_space=space)


def in_hbm(array):
    return pltpu.with_memory_space_constraint(array, pltpu.HBM)


def params(mebibytes):
    return pltpu.CompilerParams(vmem_limit_bytes=mebibytes * 1024 * 1024)


def shape(*sizes, kind=BF16):
    return jax.ShapeDtypeStruct(sizes, kind)


def body(queries, key_rows, values, out_grads, offsets):
    arrays = [in_hbm(array) for array in (queries, key_rows, values, out_grads)]
    heads = H_MID + H_WIDE
    wide_send, offset_rows = pl.pallas_call(
        wide_kernel,
        out_shape=[shape(OUTERS, 16, 256), shape(heads, TOK, kind=jnp.int32)],
        in_specs=[spec(pltpu.HBM)] * 5,
        out_specs=[spec(pltpu.VMEM)] * 2,
        scratch_shapes=[
            pltpu.SMEM((heads,), jnp.int32),
            pltpu.VMEM((4, H_WIDE, TOK, HEAD_DIM), BF16),
            pltpu.SemaphoreType.DMA,
            pltpu.SemaphoreType.DMA((4, H_WIDE)),
        ],
        compiler_params=params(8),
    )(in_hbm(offsets), *arrays)
    wide_got = lax.all_to_all(wide_send, "outer", 0, 0)
    packed = pl.pallas_call(
        mid_pack_kernel,
        out_shape=shape(SLOTS, 128, 256),
        in_specs=[spec(pltpu.VMEM)] + [spec(pltpu.HBM)] * 4,
        out_specs=spec(pltpu.VMEM),
        scratch_shapes=[
            pltpu.VMEM((4, H_MID, TOK, HEAD_DIM), BF16),
            pltpu.SemaphoreType.DMA((4, H_MID)),
        ],
        cost_estimate=pl.CostEstimate(
            flops=8 * H_MID * MID_ROWS * TOK * HEAD_DIM,
            bytes_accessed=8 * H_MID * TOK * HEAD_DIM,
            transcendentals=0,
        ),
        compiler_params=params(8),
    )(offset_rows, *arrays)
    packed = pl.pallas_call(
        wide_pack_kernel,
        out_shape=shape(SLOTS, 128, 256),
        in_specs=[spec(pltpu.VMEM), spec(pl.ANY)],
        out_specs=spec(pl.ANY),
        scratch_shapes=[
            pltpu.VMEM((H_WIDE, 64, 256), BF16),
            pltpu.SemaphoreType.DMA((H_WIDE,)),
        ],
        input_output_aliases={1: 0},
        compiler_params=params(8),
    )(wide_got, packed)
    own = lax.all_to_all(packed, "inner", 0, 0, axis_index_groups=ALONG_Z)
    other = lax.ppermute(own[:, 0:64, :], "inner", ACROSS_Y)
    dq, own_sums, wide_rows, other_sums = pl.pallas_call(
        work_kernel,
        out_shape=[
            shape(SLOTS, MID_ROWS, HEAD_DIM),
            shape(HALF_KEYS, 256, kind=F32),
            shape(SLOTS, 16, HEAD_DIM),
            shape(SLOTS, MID_ROWS, 256),
        ],
        in_specs=[spec(pltpu.VMEM)] * 2,
        out_specs=[spec(pltpu.VMEM)] * 4,
        scratch_shapes=[pltpu.VMEM((HALVES * HALF_KEYS, 256), F32)],
        compiler_params=params(32),
    )(own, other)
    back = lax.ppermute(other_sums, "inner", ACROSS_Y)
    near_block = pl.BlockSpec((TOK, HEAD_DIM), lambda head: (0, head))
    near = pl.pallas_call(
        near_kernel,
        grid=(H_NEAR,),
        out_shape=[shape(TOK, HIDDEN)] * 3,
        in_specs=[spec(pl.ANY)] + [near_block] * 4,
        out_specs=[near_block] * 3,
        cost_estimate=pl.CostEstimate(
            flops=10 * H_NEAR * TOK * TOK * HEAD_DIM,
            bytes_accessed=14 * TOK * NEAR_END,
            transcendentals=H_NEAR * TOK * TOK,
        ),
        compiler_params=params(16),
    )(other_sums, *arrays)
    results = pl.pallas_call(
        return_kernel,
        out_shape=shape(SLOTS, 192, HEAD_DIM),
        in_specs=[spec(pltpu.VMEM)] * 4,
        out_specs=spec(pltpu.VMEM),
        compiler_params=params(16),
    )(dq, own_sums, wide_rows, back)
    returned = lax.all_to_all(results, "inner", 0, 0, axis_index_groups=ALONG_Z)
    return tuple(
        pl.pallas_call(
            assemble_kernel,
            out_shape=[shape(TOK, HIDDEN)] * 3,
            in_specs=[spec(pltpu.VMEM)] * 2 + [spec(pltpu.HBM)] * 3,
            out_specs=[spec(pltpu.HBM)] * 3,
            scratch_shapes=[
                pltpu.VMEM((3, heads, TOK, HEAD_DIM), BF16),
                pltpu.SemaphoreType.DMA((3, heads)),
            ],
            input_output_aliases={2: 0, 3: 1, 4: 2},
            compiler_params=params(16),
        )(offset_rows, returned, *near)
    )


def solution(mesh):
    rows = P(("outer", "inner"), None)
    return jax.shard_map(
        body,
        mesh=mesh,
        in_specs=(rows, rows, rows, rows, P()),
        out_specs=(rows, rows, rows),
        check_vma=False,
    )
```

time: 83.7 us -> 80.9 us (0.967); the launches traced: 82.1 us -> 80.3 us
  waiting for transfers between devices: 27.4 us -> 24 us
  Pallas kernels: 12.8 us -> 14.1 us
    ppermute x1, waiting for transfers between devices: 12.4 us -> 5.85 us  [body(): back = lax.ppermute(other_sums, 'inner', ACROSS_Y)]
    all_to_all x1, waiting for transfers between devices: 0.01 us -> 2.81 us  [body(): wide_got = lax.all_to_all(wide_send, 'outer', 0, 0)]
    ppermute x1, waiting for transfers between devices: 4.68 us -> 6.71 us  [body(): other = lax.ppermute(own[:, 0:64, :], 'inner', ACROSS_Y)]
    all_to_all x1, waiting for transfers between devices: 10.3 us -> 8.61 us  [body(): returned = lax.all_to_all(results, 'inner', 0, 0, axis_index_groups=ALONG_Z)]
    pallas_call x2 -> x4, Pallas kernels: 5.98 us -> 7.26 us  [the longest x1 2.45 us: body(): pl.pallas_call(work_kernel, out_shape=[shape(SLOTS, MID_ROWS, HEAD_DIM),...]
  transfers between devices with their start and end apart: 4 -> 4, of which waited for: 3 -> 4; matrix products, arithmetic and copies ran while one was open for 0% -> 0% of each run, Pallas kernels for 6% -> 8%
where the time goes in v4:
time: 80.9 us; the launch traced here: 80.3 us
  blocking collectives  26.2 us (32%)
  waiting for transfers between devices  24 us (30%)
  starting transfers between devices  15.3 us (19%)
  Pallas kernels  14.1 us (17%)
    all_to_all x1, blocking collectives, body(): own = lax.all_to_all(packed, 'inner', 0, 0, axis_index_groups=ALONG_Z)  26.2 us
    all_to_all x1, waiting for transfers between devices, body(): returned = lax.all_to_all(results, 'inner', 0, 0, axis_index_groups=ALONG_Z)  8.61 us
    ppermute x1, waiting for transfers between devices, body(): other = lax.ppermute(own[:, 0:64, :], 'inner', ACROSS_Y)  6.71 us
    all_to_all x1, starting transfers between devices, body(): wide_got = lax.all_to_all(wide_send, 'outer', 0, 0)  5.87 us
    ppermute x1, waiting for transfers between devices, body(): back = lax.ppermute(other_sums, 'inner', ACROSS_Y)  5.85 us
    pallas_call x1, Pallas kernels, body(): pl.pallas_call(near_kernel, grid=(H_NEAR,), out_shape=[shape(TOK, HIDDEN)...  4.54 us
    all_to_all x1, starting transfers between devices, body(): returned = lax.all_to_all(results, 'inner', 0, 0, axis_index_groups=ALONG_Z)  3.45 us
    ppermute x1, starting transfers between devices, body(): other = lax.ppermute(own[:, 0:64, :], 'inner', ACROSS_Y)  2.99 us
  transfers between devices with their start and end apart: 4, of which 4 were waited for; matrix products, arithmetic and copies ran while one was open for 0% of the time, Pallas kernels for 8%

profile of v4, /device:TPU:2, one launch (start us, length us, event | category | flops | bytes accessed | tf_op | source)
XLA Modules:
  0.0 80.3 jit_solution(15571401779553994837)
XLA Ops:
  0.6 2.2 %shard_map.76 = (bf16[16,16,256]{2,1,0:T(8,128)(2,1)}, s32[8,256]{1,0:T(8,128)S(1)}) custom-call(s32[8]{0:T(128)} %off_hbm.1, bf16[256,1536]{1,0:T(8,128)(2,1)} %q_ref.1, bf16[256,1536]{1,0:T(8,128)(2,1)} %k_ref.1, bf16[256,1536]{1,0:T(8,128)(2,1)} %v_ref.1, bf16[256,1536]{1,0:T(8,128)(2,1)} %g_ref.1), custom_call_target="tpu_custom_call" | custom-call | tf_op jit(solution)/shard_map/pallas_call | solution.py:282
  2.8 5.9 %all-to-all-start = ((bf16[16,16,256]{2,1,0:T(8,128)(2,1)}), bf16[16,16,256]{2,1,0:T(8,128)(2,1)S(1)}, u32[]{:S(2)}, u32[]{:S(2)}) async-start(bf16[16,16,256]{2,1,0:T(8,128)(2,1)} %get-tuple-element.13), calls=%async_computation | async-start | bytes 262144 | tf_op jit(solution)/shard_map/all_to_all | solution.py:295
  8.7 2.0 %shard_map.77.packed = bf16[8,128,256]{2,1,0:T(8,128)(2,1)S(1)} custom-call(s32[8,256]{1,0:T(8,128)S(1)} %get-tuple-element.12.off_ref, bf16[256,1536]{1,0:T(8,128)(2,1)} %q_ref.1, bf16[256,1536]{1,0:T(8,128)(2,1)} %k_ref.1, bf16[256,1536]{1,0:T(8,128)(2,1)} %v_ref.1, bf16[256,1536]{1,0:T(8,128)(2,1)} %g_ref.1), custom_call_target="tpu_custom_call" | custom-call | flops 83886080 | bytes 1310720 | tf_op jit(solution)/shard_map/pallas_call | solution.py:296
  10.7 2.8 %all-to-all-done.got_ref = bf16[16,16,256]{2,1,0:T(8,128)(2,1)S(1)} async-done(((bf16[16,16,256]{2,1,0:T(8,128)(2,1)}), bf16[16,16,256]{2,1,0:T(8,128)(2,1)S(1)}, u32[]{:S(2)}, u32[]{:S(2)}) %all-to-all-start) | async-done | bytes 131104 | tf_op jit(solution)/shard_map/all_to_all | solution.py:295
  13.5 0.6 shard_map.78
  14.1 26.2 %all_to_all.15.own_ref = bf16[8,128,256]{2,1,0:T(8,128)(2,1)S(1)} all-to-all(bf16[8,128,256]{2,1,0:T(8,128)(2,1)S(1)} %shard_map.78), channel_id=1, replica_groups={{0,2,4,6,8,10,12,14},{1,3,5,7,9,11,13,15},{16,18,20,22,24,26,28,30},{17..., dimensions={0} | all-to-all | bytes 1048576 | tf_op jit(solution)/shard_map/all_to_all | solution.py:324
  40.4 3.0 %collective-permute-start = (bf16[8,64,256]{2,1,0:T(8,128)(2,1)S(1)}, bf16[8,64,256]{2,1,0:T(8,128)(2,1)S(1)}, u32[]{:S(2)}, u32[]{:S(2)}) collective-permute-start(bf16[8,64,256]{2,1,0:T(8,128)(2,1)S(1)} %slice.4), channel_id=1, source_target_pairs={{0,1},{1,0},{2,3},{3,2},{4,5},{5,4},{6,7},{7,6},{8,9},{9,8},{10,11... | collective-permute-start | bytes 786440 | tf_op jit(solution)/shard_map/ppermute | solution.py:325
  43.4 6.7 %collective-permute-done.other_ref = bf16[8,64,256]{2,1,0:T(8,128)(2,1)S(1)} collective-permute-done((bf16[8,64,256]{2,1,0:T(8,128)(2,1)S(1)}, bf16[8,64,256]{2,1,0:T(8,128)(2,1)S(1)}, u32[]{:S(2)}, u32[]{:S(2)}) %collective-permute-start) | collective-permute-done | bytes 262176 | tf_op jit(solution)/shard_map/ppermute | solution.py:325
  50.1 2.4 %shard_map.79 = (bf16[8,64,128]{2,1,0:T(8,128)(2,1)S(1)}, f32[512,256]{1,0:T(8,128)S(1)}, bf16[8,16,128]{2,1,0:T(8,128)(2,1)S(1)}, bf16[8,64,256]{2,1,0:T(8,128)(2,1)S(1)}) custom-call(bf16[8,128,256]{2,1,0:T(8,128)(2,1)S(1)} %all_to_all.15.own_ref, bf16[8,64,256]{2,1,0:T(8,128)(2,1)S(1)} %collective-permute-done.other_ref), custom_call_target="tpu_custom_call" | custom-call | tf_op jit(solution)/shard_map/pallas_call | solution.py:326
  52.5 3.0 %collective-permute-start.1 = (bf16[8,64,256]{2,1,0:T(8,128)(2,1)S(1)}, bf16[8,64,256]{2,1,0:T(8,128)(2,1)S(1)}, u32[]{:S(2)}, u32[]{:S(2)}) collective-permute-start(bf16[8,64,256]{2,1,0:T(8,128)(2,1)S(1)} %get-tuple-element.17.after), channel_id=1, source_target_pairs={{0,1},{1,0},{2,3},{3,2},{4,5},{5,4},{6,7},{7,6},{8,9},{9,8},{10,11... | collective-permute-start | bytes 786440 | tf_op jit(solution)/shard_map/ppermute | solution.py:339
  55.5 5.8 %collective-permute-done.1.back_ref = bf16[8,64,256]{2,1,0:T(8,128)(2,1)S(1)} collective-permute-done((bf16[8,64,256]{2,1,0:T(8,128)(2,1)S(1)}, bf16[8,64,256]{2,1,0:T(8,128)(2,1)S(1)}, u32[]{:S(2)}, u32[]{:S(2)}) %collective-permute-start.1) | collective-permute-done | bytes 262176 | tf_op jit(solution)/shard_map/ppermute | solution.py:339
  61.4 0.8 shard_map.80
  62.2 3.5 %all-to-all-start.2 = ((bf16[8,192,128]{2,1,0:T(8,128)(2,1)}), bf16[8,192,128]{2,1,0:T(8,128)(2,1)S(1)}, u32[]{:S(2)}, u32[]{:S(2)}) async-start(bf16[8,192,128]{2,1,0:T(8,128)(2,1)} %shard_map.80), calls=%async_computation.2 | async-start | bytes 786432 | tf_op jit(solution)/shard_map/all_to_all | solution.py:361
  65.6 4.5 %shard_map.81 = (bf16[256,1536]{1,0:T(8,128)(2,1)}, bf16[256,1536]{1,0:T(8,128)(2,1)}, bf16[256,1536]{1,0:T(8,128)(2,1)}) custom-call(bf16[8,64,256]{2,1,0:T(8,128)(2,1)S(1)} %get-tuple-element.17.after, bf16[256,1536]{1,0:T(8,128)(2,1)} %q_ref.1, bf16[256,1536]{1,0:T(8,128)(2,1)} %k_ref.1, bf16[256,1536]{1,0:T(8,128)(2,1)} %v_ref.1, bf16[256,1536]{1,0:T(8,128)(2,1)} %g_ref.1), custom_call_target="tpu_custom_call" | custom-call | flops 335544320 | bytes 1835008 | tf_op jit(solution)/shard_map/pallas_call | solution.py:341
  70.2 8.6 %all-to-all-done.2.got_ref = bf16[8,192,128]{2,1,0:T(8,128)(2,1)S(1)} async-done(((bf16[8,192,128]{2,1,0:T(8,128)(2,1)}), bf16[8,192,128]{2,1,0:T(8,128)(2,1)S(1)}, u32[]{:S(2)}, u32[]{:S(2)}) %all-to-all-start.2) | async-done | bytes 393248 | tf_op jit(solution)/shard_map/all_to_all | solution.py:361
  78.8 1.5 %shard_map.82 = (bf16[256,1536]{1,0:T(8,128)(2,1)}, bf16[256,1536]{1,0:T(8,128)(2,1)}, bf16[256,1536]{1,0:T(8,128)(2,1)}) custom-call(s32[8,256]{1,0:T(8,128)S(1)} %get-tuple-element.12.off_ref, bf16[8,192,128]{2,1,0:T(8,128)(2,1)S(1)} %all-to-all-done.2.got_ref, ...), custom_call_target="tpu_custom_call", output_to_operand_aliasing={{0}: (2, {}), {1}: (3, {}), {2}: (4, {})} | custom-call | tf_op jit(solution)/shard_map/pallas_call | solution.py:363
  (1 shorter events, 0.0 us)
Async XLA Ops:
  2.8 10.7 %all-to-all-start = ((bf16[16,16,256]{2,1,0:T(8,128)(2,1)}), bf16[16,16,256]{2,1,0:T(8,128)(2,1)S(1)}, u32[]{:S(2)}, u32[]{:S(2)}) async-start(bf16[16,16,256]{2,1,0:T(8,128)(2,1)} %get-tuple-element.13), calls=%async_computation | async-start | bytes 262144 | tf_op jit(solution)/shard_map/all_to_all | solution.py:295
  40.4 9.7 %collective-permute-start = (bf16[8,64,256]{2,1,0:T(8,128)(2,1)S(1)}, bf16[8,64,256]{2,1,0:T(8,128)(2,1)S(1)}, u32[]{:S(2)}, u32[]{:S(2)}) collective-permute-start(bf16[8,64,256]{2,1,0:T(8,128)(2,1)S(1)} %slice.4), channel_id=1, source_target_pairs={{0,1},{1,0},{2,3},{3,2},{4,5},{5,4},{6,7},{7,6},{8,9},{9,8},{10,11... | collective-permute-start | bytes 786440 | tf_op jit(solution)/shard_map/ppermute | solution.py:325
  52.5 8.8 %collective-permute-start.1 = (bf16[8,64,256]{2,1,0:T(8,128)(2,1)S(1)}, bf16[8,64,256]{2,1,0:T(8,128)(2,1)S(1)}, u32[]{:S(2)}, u32[]{:S(2)}) collective-permute-start(bf16[8,64,256]{2,1,0:T(8,128)(2,1)S(1)} %get-tuple-element.17.after), channel_id=1, source_target_pairs={{0,1},{1,0},{2,3},{3,2},{4,5},{5,4},{6,7},{7,6},{8,9},{9,8},{10,11... | collective-permute-start | bytes 786440 | tf_op jit(solution)/shard_map/ppermute | solution.py:339
  62.2 16.6 %all-to-all-start.2 = ((bf16[8,192,128]{2,1,0:T(8,128)(2,1)}), bf16[8,192,128]{2,1,0:T(8,128)(2,1)S(1)}, u32[]{:S(2)}, u32[]{:S(2)}) async-start(bf16[8,192,128]{2,1,0:T(8,128)(2,1)} %shard_map.80), calls=%async_computation.2 | async-start | bytes 786432 | tf_op jit(solution)/shard_map/all_to_all | solution.py:361

commit v5 on v4

--- a/solution.py
+++ b/solution.py
@@ -1,3 +1,4 @@
+import functools
 import math
 
 import jax
@@ -64,12 +65,12 @@
     return weights.astype(BF16), score_gradients
 
 
-def fetch(sources, held, sems, heads):
+def fetch(sources, held, sems, heads, first=NEAR_END):
     copies = {}
     for at, head in enumerate(heads):
         for which, source in enumerate(sources):
             copies[head, which] = pltpu.make_async_copy(
-                source.at[:, pl.ds(NEAR_END + head * HEAD_DIM, HEAD_DIM)],
+                source.at[:, pl.ds(first + head * HEAD_DIM, HEAD_DIM)],
                 held.at[which, at],
                 sems.at[which, at],
             )
@@ -118,7 +119,7 @@
         out_ref[head, 64:128, :] = jnp.zeros((64, 2 * HEAD_DIM), BF16)
 
 
-def wide_pack_kernel(got_ref, packed, out, held, sems):
+def wide_pack_kernel(got_ref, packed, after, out, held, sems):
     rows = got_ref[...].reshape(OUTERS * 16, 2 * HEAD_DIM)
     row, column = iota2(64, OUTERS * 16)
     base = 16 * ((row % 32) // 2) + row % 2 + jnp.where(row < 32, 0, 6)
@@ -134,12 +135,53 @@
         copy.wait()
 
 
-def near_kernel(after, q_ref, k_ref, v_ref, g_ref, dq_ref, dk_ref, dv_ref):
-    query, key, value, gradient = q_ref[...], k_ref[...], v_ref[...], g_ref[...]
-    weights, score_gradients = attention_transposed(query, key, value, gradient)
-    dq_ref[...] = dot_tn(score_gradients, key).astype(BF16)
-    dk_ref[...] = dot(score_gradients, query).astype(BF16)
-    dv_ref[...] = dot(weights, gradient).astype(BF16)
+def near_kernel(core, after, q_hbm, k_hbm, v_hbm, g_hbm, *rest):
+    targets, (held, results, sems, out_sems) = rest[-7:-4], rest[-4:]
+
+    @pl.when(lax.rem(lax.axis_index("outer"), 2) == core)
+    def attend():
+        copies = fetch((q_hbm, k_hbm, v_hbm, g_hbm), held, sems, range(H_NEAR), 0)
+        sends = []
+        for head in range(H_NEAR):
+            for which in range(4):
+                copies[head, which].wait()
+            query, key, value, gradient = (held[which, head] for which in range(4))
+            weights, score_gradients = attention_transposed(query, key, value, gradient)
+            results[0, head] = dot_tn(score_gradients, key).astype(BF16)
+            results[1, head] = dot(score_gradients, query).astype(BF16)
+            results[2, head] = dot(weights, gradient).astype(BF16)
+            for which, target in enumerate(targets):
+                send = pltpu.make_async_copy(
+                    results.at[which, head],
+                    target.at[:, pl.ds(head * HEAD_DIM, HEAD_DIM)],
+                    out_sems.at[which, head],
+                )
+                send.start()
+                sends.append(send)
+        for send in sends:
+            send.wait()
+
+
+def near_heads(core, after, arrays, previous=()):
+    return pl.pallas_call(
+        functools.partial(near_kernel, core),
+        out_shape=[shape(TOK, HIDDEN)] * 3,
+        in_specs=[spec(pl.ANY)] + [spec(pltpu.HBM)] * (4 + len(previous)),
+        out_specs=[spec(pltpu.HBM)] * 3,
+        scratch_shapes=[
+            pltpu.VMEM((4, H_NEAR, TOK, HEAD_DIM), BF16),
+            pltpu.VMEM((3, H_NEAR, TOK, HEAD_DIM), BF16),
+            pltpu.SemaphoreType.DMA((4, H_NEAR)),
+            pltpu.SemaphoreType.DMA((3, H_NEAR)),
+        ],
+        input_output_aliases={5 + which: which for which in range(len(previous))},
+        cost_estimate=pl.CostEstimate(
+            flops=10 * H_NEAR * TOK * TOK * HEAD_DIM,
+            bytes_accessed=14 * TOK * NEAR_END,
+            transcendentals=H_NEAR * TOK * TOK,
+        ),
+        compiler_params=params(16),
+    )(after, *arrays, *previous)
 
 
 def slot():
@@ -215,7 +257,7 @@
         other_out[...] = other.reshape(SLOTS, MID_ROWS, 2 * HEAD_DIM)
 
 
-def return_kernel(dq_ref, own_ref, wide_ref, back_ref, out_ref):
+def return_kernel(dq_ref, own_ref, wide_ref, back_ref, after, out_ref):
     @pl.when(slot() < H_MID)
     def add_halves():
         out_ref[:, 0:64, :] = dq_ref[...]
@@ -309,10 +351,11 @@
         ),
         compiler_params=params(8),
     )(offset_rows, *arrays)
+    near = near_heads(0, wide_got, arrays)
     packed = pl.pallas_call(
         wide_pack_kernel,
         out_shape=shape(SLOTS, 128, 256),
-        in_specs=[spec(pltpu.VMEM), spec(pl.ANY)],
+        in_specs=[spec(pltpu.VMEM), spec(pl.ANY), spec(pl.ANY)],
         out_specs=spec(pl.ANY),
         scratch_shapes=[
             pltpu.VMEM((H_WIDE, 64, 256), BF16),
@@ -320,7 +363,7 @@
         ],
         input_output_aliases={1: 0},
         compiler_params=params(8),
-    )(wide_got, packed)
+    )(wide_got, packed, in_hbm(near[0]))
     own = lax.all_to_all(packed, "inner", 0, 0, axis_index_groups=ALONG_Z)
     other = lax.ppermute(own[:, 0:64, :], "inner", ACROSS_Y)
     dq, own_sums, wide_rows, other_sums = pl.pallas_call(
@@ -337,27 +380,14 @@
         compiler_params=params(32),
     )(own, other)
     back = lax.ppermute(other_sums, "inner", ACROSS_Y)
-    near_block = pl.BlockSpec((TOK, HEAD_DIM), lambda head: (0, head))
-    near = pl.pallas_call(
-        near_kernel,
-        grid=(H_NEAR,),
-        out_shape=[shape(TOK, HIDDEN)] * 3,
-        in_specs=[spec(pl.ANY)] + [near_block] * 4,
-        out_specs=[near_block] * 3,
-        cost_estimate=pl.CostEstimate(
-            flops=10 * H_NEAR * TOK * TOK * HEAD_DIM,
-            bytes_accessed=14 * TOK * NEAR_END,
-            transcendentals=H_NEAR * TOK * TOK,
-        ),
-        compiler_params=params(16),
-    )(other_sums, *arrays)
+    near = near_heads(1, other_sums, arrays, near)
     results = pl.pallas_call(
         return_kernel,
         out_shape=shape(SLOTS, 192, HEAD_DIM),
-        in_specs=[spec(pltpu.VMEM)] * 4,
+        in_specs=[spec(pltpu.VMEM)] * 4 + [spec(pl.ANY)],
         out_specs=spec(pltpu.VMEM),
         compiler_params=params(16),
-    )(dq, own_sums, wide_rows, back)
+    )(dq, own_sums, wide_rows, back, in_hbm(near[0]))
     returned = lax.all_to_all(results, "inner", 0, 0, axis_index_groups=ALONG_Z)
     return tuple(
         pl.pallas_call(

time: 80.9 us -> 76.6 us (0.947)
  waiting for transfers between devices: 24 us -> 12.5 us
  blocking collectives: 26.2 us -> 36.6 us
  starting transfers between devices: 15.3 us -> 11.8 us
    all_to_all x0 -> x1, blocking collectives: none -> 14.7 us  [body(): returned = lax.all_to_all(results, 'inner', 0, 0, axis_index_groups=ALONG_Z)]
    all_to_all x1 -> x0, waiting for transfers between devices: 8.61 us -> none  [body(): returned = lax.all_to_all(results, 'inner', 0, 0, axis_index_groups=ALONG_Z)]
    all_to_all x1, blocking collectives: 26.2 us -> 21.9 us  [body(): own = lax.all_to_all(packed, 'inner', 0, 0, axis_index_groups=ALONG_Z)]
    all_to_all x1 -> x0, starting transfers between devices: 3.45 us -> none  [body(): returned = lax.all_to_all(results, 'inner', 0, 0, axis_index_groups=ALONG_Z)]
    ppermute x1, waiting for transfers between devices: 6.71 us -> 4.98 us  [body(): other = lax.ppermute(own[:, 0:64, :], 'inner', ACROSS_Y)]
    ppermute x1, waiting for transfers between devices: 5.85 us -> 4.72 us  [body(): back = lax.ppermute(other_sums, 'inner', ACROSS_Y)]
    pallas_call x1 -> x2, Pallas kernels: 4.54 us -> 4.83 us  [near_heads(): pl.pallas_call(functools.partial(near_kernel, core), out_shape=[shape(TOK...]
  transfers between devices with their start and end apart: 4 -> 3, of which waited for: 4 -> 3; matrix products, arithmetic and copies ran while one was open for 0% -> 0% of each run, Pallas kernels for 8% -> 3%
where the time goes in v5:
time: 76.6 us; the launch traced here: 75.3 us
  blocking collectives  36.6 us (48%)
  Pallas kernels  13.7 us (18%)
  waiting for transfers between devices  12.5 us (16%)
  starting transfers between devices  11.8 us (15%)
    all_to_all x1, blocking collectives, body(): own = lax.all_to_all(packed, 'inner', 0, 0, axis_index_groups=ALONG_Z)  21.9 us
    all_to_all x1, blocking collectives, body(): returned = lax.all_to_all(results, 'inner', 0, 0, axis_index_groups=ALONG_Z)  14.7 us
    all_to_all x1, starting transfers between devices, body(): wide_got = lax.all_to_all(wide_send, 'outer', 0, 0)  5.87 us
    ppermute x1, waiting for transfers between devices, body(): other = lax.ppermute(own[:, 0:64, :], 'inner', ACROSS_Y)  4.98 us
    pallas_call x2, Pallas kernels, near_heads(): pl.pallas_call(functools.partial(near_kernel, core), out_shape=[shape(TOK...  4.83 us
    ppermute x1, waiting for transfers between devices, body(): back = lax.ppermute(other_sums, 'inner', ACROSS_Y)  4.72 us
    ppermute x1, starting transfers between devices, body(): back = lax.ppermute(other_sums, 'inner', ACROSS_Y)  2.99 us
    ppermute x1, starting transfers between devices, body(): other = lax.ppermute(own[:, 0:64, :], 'inner', ACROSS_Y)  2.99 us
  transfers between devices with their start and end apart: 3, of which 3 were waited for; matrix products, arithmetic and copies ran while one was open for 0% of the time, Pallas kernels for 3%

profile of v5, /device:TPU:2, one launch (start us, length us, event | category | flops | bytes accessed | tf_op | source)
XLA Modules:
  0.0 75.3 jit_solution(16017219182644341667)
XLA Ops:
  0.6 2.2 %shard_map.76 = (bf16[16,16,256]{2,1,0:T(8,128)(2,1)}, s32[8,256]{1,0:T(8,128)S(1)}) custom-call(s32[8]{0:T(128)} %off_hbm.1, bf16[256,1536]{1,0:T(8,128)(2,1)} %q_hbm.7, bf16[256,1536]{1,0:T(8,128)(2,1)} %k_hbm.7, bf16[256,1536]{1,0:T(8,128)(2,1)} %v_hbm.7, bf16[256,1536]{1,0:T(8,128)(2,1)} %g_hbm.7), custom_call_target="tpu_custom_call" | custom-call | tf_op jit(solution)/shard_map/pallas_call | solution.py:324
  2.8 5.9 %all-to-all-start = ((bf16[16,16,256]{2,1,0:T(8,128)(2,1)}), bf16[16,16,256]{2,1,0:T(8,128)(2,1)S(1)}, u32[]{:S(2)}, u32[]{:S(2)}) async-start(bf16[16,16,256]{2,1,0:T(8,128)(2,1)} %get-tuple-element.16), calls=%async_computation | async-start | bytes 262144 | tf_op jit(solution)/shard_map/all_to_all | solution.py:337
  8.7 2.0 %shard_map.77.packed = bf16[8,128,256]{2,1,0:T(8,128)(2,1)S(1)} custom-call(s32[8,256]{1,0:T(8,128)S(1)} %get-tuple-element.15.off_ref, bf16[256,1536]{1,0:T(8,128)(2,1)} %q_hbm.7, bf16[256,1536]{1,0:T(8,128)(2,1)} %k_hbm.7, bf16[256,1536]{1,0:T(8,128)(2,1)} %v_hbm.7, bf16[256,1536]{1,0:T(8,128)(2,1)} %g_hbm.7), custom_call_target="tpu_custom_call" | custom-call | flops 83886080 | bytes 1310720 | tf_op jit(solution)/shard_map/pallas_call | solution.py:338
  10.7 2.8 %all-to-all-done.after.got_ref = bf16[16,16,256]{2,1,0:T(8,128)(2,1)S(1)} async-done(((bf16[16,16,256]{2,1,0:T(8,128)(2,1)}), bf16[16,16,256]{2,1,0:T(8,128)(2,1)S(1)}, u32[]{:S(2)}, u32[]{:S(2)}) %all-to-all-start) | async-done | bytes 131104 | tf_op jit(solution)/shard_map/all_to_all | solution.py:337
  13.5 4.6 %shard_map.78 = (bf16[256,1536]{1,0:T(8,128)(2,1)}, bf16[256,1536]{1,0:T(8,128)(2,1)}, bf16[256,1536]{1,0:T(8,128)(2,1)}) custom-call(bf16[16,16,256]{2,1,0:T(8,128)(2,1)S(1)} %all-to-all-done.after.got_ref, bf16[256,1536]{1,0:T(8,128)(2,1)} %q_hbm.7, bf16[256,1536]{1,0:T(8,128)(2,1)} %k_hbm.7, bf16[256,1536]{1,0:T(8,128)(2,1)} %v_hbm.7, bf16[256,1536]{1,0:T(8,128)(2,1)} %g_hbm.7), custom_call_target="tpu_custom_call" | custom-call | flops 335544320 | bytes 1835008 | tf_op jit(solution)/shard_map/pallas_call | solution.py:166
  18.1 0.6 shard_map.79
  18.7 21.9 %all_to_all.15.own_ref = bf16[8,128,256]{2,1,0:T(8,128)(2,1)S(1)} all-to-all(bf16[8,128,256]{2,1,0:T(8,128)(2,1)S(1)} %shard_map.79), channel_id=1, replica_groups={{0,2,4,6,8,10,12,14},{1,3,5,7,9,11,13,15},{16,18,20,22,24,26,28,30},{17..., dimensions={0} | all-to-all | bytes 1048576 | tf_op jit(solution)/shard_map/all_to_all | solution.py:367
  40.7 3.0 %collective-permute-start = (bf16[8,64,256]{2,1,0:T(8,128)(2,1)S(1)}, bf16[8,64,256]{2,1,0:T(8,128)(2,1)S(1)}, u32[]{:S(2)}, u32[]{:S(2)}) collective-permute-start(bf16[8,64,256]{2,1,0:T(8,128)(2,1)S(1)} %slice.4), channel_id=1, source_target_pairs={{0,1},{1,0},{2,3},{3,2},{4,5},{5,4},{6,7},{7,6},{8,9},{9,8},{10,11... | collective-permute-start | bytes 786440 | tf_op jit(solution)/shard_map/ppermute | solution.py:368
  43.6 5.0 %collective-permute-done.other_ref = bf16[8,64,256]{2,1,0:T(8,128)(2,1)S(1)} collective-permute-done((bf16[8,64,256]{2,1,0:T(8,128)(2,1)S(1)}, bf16[8,64,256]{2,1,0:T(8,128)(2,1)S(1)}, u32[]{:S(2)}, u32[]{:S(2)}) %collective-permute-start) | collective-permute-done | bytes 262176 | tf_op jit(solution)/shard_map/ppermute | solution.py:368
  48.6 2.4 %shard_map.80 = (bf16[8,64,128]{2,1,0:T(8,128)(2,1)S(1)}, f32[512,256]{1,0:T(8,128)S(1)}, bf16[8,16,128]{2,1,0:T(8,128)(2,1)S(1)}, bf16[8,64,256]{2,1,0:T(8,128)(2,1)S(1)}) custom-call(bf16[8,128,256]{2,1,0:T(8,128)(2,1)S(1)} %all_to_all.15.own_ref, bf16[8,64,256]{2,1,0:T(8,128)(2,1)S(1)} %collective-permute-done.other_ref), custom_call_target="tpu_custom_call" | custom-call | tf_op jit(solution)/shard_map/pallas_call | solution.py:369
  51.1 3.0 %collective-permute-start.1 = (bf16[8,64,256]{2,1,0:T(8,128)(2,1)S(1)}, bf16[8,64,256]{2,1,0:T(8,128)(2,1)S(1)}, u32[]{:S(2)}, u32[]{:S(2)}) collective-permute-start(bf16[8,64,256]{2,1,0:T(8,128)(2,1)S(1)} %get-tuple-element.21.after), channel_id=1, source_target_pairs={{0,1},{1,0},{2,3},{3,2},{4,5},{5,4},{6,7},{7,6},{8,9},{9,8},{10,11... | collective-permute-start | bytes 786440 | tf_op jit(solution)/shard_map/ppermute | solution.py:382
  54.1 0.3 shard_map.81
  54.3 4.7 %collective-permute-done.1.back_ref = bf16[8,64,256]{2,1,0:T(8,128)(2,1)S(1)} collective-permute-done((bf16[8,64,256]{2,1,0:T(8,128)(2,1)S(1)}, bf16[8,64,256]{2,1,0:T(8,128)(2,1)S(1)}, u32[]{:S(2)}, u32[]{:S(2)}) %collective-permute-start.1) | collective-permute-done | bytes 262176 | tf_op jit(solution)/shard_map/ppermute | solution.py:382
  59.0 0.1 shard_map.82
  59.1 14.7 %all_to_all.16.got_ref = bf16[8,192,128]{2,1,0:T(8,128)(2,1)S(1)} all-to-all(bf16[8,192,128]{2,1,0:T(8,128)(2,1)S(1)} %shard_map.82), channel_id=1, replica_groups={{0,2,4,6,8,10,12,14},{1,3,5,7,9,11,13,15},{16,18,20,22,24,26,28,30},{17..., dimensions={0} | all-to-all | bytes 786432 | tf_op jit(solution)/shard_map/all_to_all | solution.py:391
  73.8 1.5 %shard_map.83 = (bf16[256,1536]{1,0:T(8,128)(2,1)}, bf16[256,1536]{1,0:T(8,128)(2,1)}, bf16[256,1536]{1,0:T(8,128)(2,1)}) custom-call(s32[8,256]{1,0:T(8,128)S(1)} %get-tuple-element.15.off_ref, bf16[8,192,128]{2,1,0:T(8,128)(2,1)S(1)} %all_to_all.16.got_ref, ...), custom_call_target="tpu_custom_call", output_to_operand_aliasing={{0}: (2, {}), {1}: (3, {}), {2}: (4, {})} | custom-call | tf_op jit(solution)/shard_map/pallas_call | solution.py:393
  (1 shorter events, 0.0 us)
Async XLA Ops:
  2.8 10.7 %all-to-all-start = ((bf16[16,16,256]{2,1,0:T(8,128)(2,1)}), bf16[16,16,256]{2,1,0:T(8,128)(2,1)S(1)}, u32[]{:S(2)}, u32[]{:S(2)}) async-start(bf16[16,16,256]{2,1,0:T(8,128)(2,1)} %get-tuple-element.16), calls=%async_computation | async-start | bytes 262144 | tf_op jit(solution)/shard_map/all_to_all | solution.py:337
  40.7 8.0 %collective-permute-start = (bf16[8,64,256]{2,1,0:T(8,128)(2,1)S(1)}, bf16[8,64,256]{2,1,0:T(8,128)(2,1)S(1)}, u32[]{:S(2)}, u32[]{:S(2)}) collective-permute-start(bf16[8,64,256]{2,1,0:T(8,128)(2,1)S(1)} %slice.4), channel_id=1, source_target_pairs={{0,1},{1,0},{2,3},{3,2},{4,5},{5,4},{6,7},{7,6},{8,9},{9,8},{10,11... | collective-permute-start | bytes 786440 | tf_op jit(solution)/shard_map/ppermute | solution.py:368
  51.1 8.0 %collective-permute-start.1 = (bf16[8,64,256]{2,1,0:T(8,128)(2,1)S(1)}, bf16[8,64,256]{2,1,0:T(8,128)(2,1)S(1)}, u32[]{:S(2)}, u32[]{:S(2)}) collective-permute-start(bf16[8,64,256]{2,1,0:T(8,128)(2,1)S(1)} %get-tuple-element.21.after), channel_id=1, source_target_pairs={{0,1},{1,0},{2,3},{3,2},{4,5},{5,4},{6,7},{7,6},{8,9},{9,8},{10,11... | collective-permute-start | bytes 786440 | tf_op jit(solution)/shard_map/ppermute | solution.py:382

commit v6 on v5

--- a/solution.py
+++ b/solution.py
@@ -27,6 +27,7 @@
 ALONG_Z = [[HALVES * z + half for z in range(SLOTS)] for half in range(HALVES)]
 ACROSS_Y = [(member, member ^ 1) for member in range(HALVES * SLOTS)]
 SCALE = 1.0 / math.sqrt(HEAD_DIM)
+EXP2_SCALE = SCALE * math.log2(math.e)
 BF16 = jnp.bfloat16
 F32 = jnp.float32
 
@@ -55,14 +56,22 @@
     return jnp.where(condition, 1.0, 0.0).astype(BF16)
 
 
+def scaled_weights(parts, query, gradient):
+    scores = [dot_nt(key, query) for key, unused in parts]
+    top = functools.reduce(jnp.maximum, [jnp.max(s, axis=0, keepdims=True) for s in scores])
+    exponents = [jnp.exp2((s - top) * EXP2_SCALE) for s in scores]
+    inverse = 1.0 / sum(jnp.sum(e, axis=0, keepdims=True) for e in exponents)
+    products = [dot_nt(value, gradient) for unused, value in parts]
+    row_dots = inverse * sum(
+        jnp.sum(e * p, axis=0, keepdims=True) for e, p in zip(exponents, products)
+    )
+    weights = exponents[0] * inverse
+    score_gradients = weights * (products[0] - row_dots) * SCALE
+    return weights.astype(BF16), score_gradients.astype(BF16)
+
+
 def attention_transposed(query, key, value, gradient):
-    scores = dot_nt(key, query) * SCALE
-    exponent = jnp.exp(scores - jnp.max(scores, axis=0, keepdims=True))
-    weights = exponent * (1.0 / jnp.sum(exponent, axis=0, keepdims=True))
-    products = dot_nt(value, gradient)
-    row_dots = jnp.sum(weights * products, axis=0, keepdims=True)
-    score_gradients = (weights * (products - row_dots) * SCALE).astype(BF16)
-    return weights.astype(BF16), score_gradients
+    return scaled_weights([(key, value)], query, gradient)
 
 
 def fetch(sources, held, sems, heads, first=NEAR_END):
@@ -227,22 +236,29 @@
     out_ref[...] = spread.astype(BF16).reshape(SLOTS, 16, HEAD_DIM)
 
 
-def work_kernel(own_ref, other_ref, dq_ref, own_out, wide_out, other_out, dkv_ref):
+def halves(ref, rows):
+    block = ref[:, rows, :].reshape(HALF_KEYS, 2 * HEAD_DIM)
+    return block[:, :HEAD_DIM], block[:, HEAD_DIM:]
+
+
+def own_work_kernel(own_ref, other_ref, after, dq_ref, dkv_ref, wide_out):
     @pl.when(slot() >= H_MID)
     def wide():
         attend_wide(own_ref, other_ref, wide_out)
 
     @pl.when(slot() < H_MID)
     def attend():
-        kv = [ref[:, 0:64, :].reshape(HALF_KEYS, 2 * HEAD_DIM) for ref in (own_ref, other_ref)]
-        kv = jnp.concatenate(kv, axis=0)
-        key, value = kv[:, :HEAD_DIM], kv[:, HEAD_DIM:]
-        qg = own_ref[:, 64:128, :].reshape(HALF_KEYS, 2 * HEAD_DIM)
+        own_key, own_value = halves(own_ref, slice(0, 64))
+        other_key, other_value = halves(other_ref, slice(0, 64))
+        key = jnp.concatenate([own_key, other_key], axis=0)
+        value = jnp.concatenate([own_value, other_value], axis=0)
+        queries, gradients = halves(own_ref, slice(64, 128))
         for start in range(0, HALF_KEYS, QUERY_BLOCK):
-            query = qg[start : start + QUERY_BLOCK, :HEAD_DIM]
-            gradient = qg[start : start + QUERY_BLOCK, HEAD_DIM:]
+            query = queries[start : start + QUERY_BLOCK]
+            gradient = gradients[start : start + QUERY_BLOCK]
             weights, score_gradients = attention_transposed(query, key, value, gradient)
-            dk, dv = dot(score_gradients, query), dot(weights, gradient)
+            dk = dot(score_gradients[:HALF_KEYS], query)
+            dv = dot(weights[:HALF_KEYS], gradient)
             if start == 0:
                 dkv_ref[:, :HEAD_DIM] = dk
                 dkv_ref[:, HEAD_DIM:] = dv
@@ -252,17 +268,22 @@
             dq = dot_tn(key, score_gradients).T.astype(BF16)
             blocks = slice(start // MID_ROWS, (start + QUERY_BLOCK) // MID_ROWS)
             dq_ref[blocks] = dq.reshape(QUERY_BLOCK // MID_ROWS, MID_ROWS, HEAD_DIM)
-        own_out[...] = dkv_ref[:HALF_KEYS, :]
-        other = dkv_ref[HALF_KEYS:, :].astype(BF16)
-        other_out[...] = other.reshape(SLOTS, MID_ROWS, 2 * HEAD_DIM)
-
-
-def return_kernel(dq_ref, own_ref, wide_ref, back_ref, after, out_ref):
+
+
+def other_work_kernel(own_ref, other_ref, query_ref, dq_ref, dkv_ref, wide_ref, out_ref, sum_ref):
     @pl.when(slot() < H_MID)
-    def add_halves():
+    def attend():
+        parts = [halves(own_ref, slice(0, 64)), halves(other_ref, slice(0, 64))]
+        queries, gradients = halves(query_ref, slice(0, 64))
+        for start in range(0, HALF_KEYS, QUERY_BLOCK):
+            query = queries[start : start + QUERY_BLOCK]
+            gradient = gradients[start : start + QUERY_BLOCK]
+            weights, score_gradients = scaled_weights(parts, query, gradient)
+            before = dkv_ref if start == 0 else sum_ref
+            sum_ref[:, :HEAD_DIM] = before[:, :HEAD_DIM] + dot(score_gradients, query)
+            sum_ref[:, HEAD_DIM:] = before[:, HEAD_DIM:] + dot(weights, gradient)
         out_ref[:, 0:64, :] = dq_ref[...]
-        back = back_ref[...].reshape(HALF_KEYS, 2 * HEAD_DIM).astype(F32)
-        dkv = (own_ref[...] + back).astype(BF16)
+        dkv = sum_ref[...].astype(BF16)
         out_ref[:, 64:128, :] = dkv[:, :HEAD_DIM].reshape(SLOTS, MID_ROWS, HEAD_DIM)
         out_ref[:, 128:192, :] = dkv[:, HEAD_DIM:].reshape(SLOTS, MID_ROWS, HEAD_DIM)
 
@@ -316,6 +337,14 @@
 
 def shape(*sizes, kind=BF16):
     return jax.ShapeDtypeStruct(sizes, kind)
+
+
+def work_cost(products):
+    return pl.CostEstimate(
+        flops=products * 4 * HALF_KEYS * HALF_KEYS * HEAD_DIM,
+        bytes_accessed=0,
+        transcendentals=2 * HALF_KEYS * HALF_KEYS,
+    )
 
 
 def body(queries, key_rows, values, out_grads, offsets):
@@ -366,28 +395,29 @@
     )(wide_got, packed, in_hbm(near[0]))
     own = lax.all_to_all(packed, "inner", 0, 0, axis_index_groups=ALONG_Z)
     other = lax.ppermute(own[:, 0:64, :], "inner", ACROSS_Y)
-    dq, own_sums, wide_rows, other_sums = pl.pallas_call(
-        work_kernel,
+    other_queries = lax.ppermute(own[:, 64:128, :], "inner", ACROSS_Y)
+    near = near_heads(1, own, arrays, near)
+    dq, own_sums, wide_rows = pl.pallas_call(
+        own_work_kernel,
         out_shape=[
             shape(SLOTS, MID_ROWS, HEAD_DIM),
             shape(HALF_KEYS, 256, kind=F32),
             shape(SLOTS, 16, HEAD_DIM),
-            shape(SLOTS, MID_ROWS, 256),
         ],
-        in_specs=[spec(pltpu.VMEM)] * 2,
-        out_specs=[spec(pltpu.VMEM)] * 4,
-        scratch_shapes=[pltpu.VMEM((HALVES * HALF_KEYS, 256), F32)],
-        compiler_params=params(32),
-    )(own, other)
-    back = lax.ppermute(other_sums, "inner", ACROSS_Y)
-    near = near_heads(1, other_sums, arrays, near)
+        in_specs=[spec(pltpu.VMEM)] * 2 + [spec(pl.ANY)],
+        out_specs=[spec(pltpu.VMEM)] * 3,
+        cost_estimate=work_cost(5),
+        compiler_params=params(24),
+    )(own, other, in_hbm(near[0]))
     results = pl.pallas_call(
-        return_kernel,
+        other_work_kernel,
         out_shape=shape(SLOTS, 192, HEAD_DIM),
-        in_specs=[spec(pltpu.VMEM)] * 4 + [spec(pl.ANY)],
+        in_specs=[spec(pltpu.VMEM)] * 6,
         out_specs=spec(pltpu.VMEM),
-        compiler_params=params(16),
-    )(dq, own_sums, wide_rows, back, in_hbm(near[0]))
+        scratch_shapes=[pltpu.VMEM((HALF_KEYS, 256), F32)],
+        cost_estimate=work_cost(4),
+        compiler_params=params(24),
+    )(own, other, other_queries, dq, own_sums, wide_rows)
     returned = lax.all_to_all(results, "inner", 0, 0, axis_index_groups=ALONG_Z)
     return tuple(
         pl.pallas_call(

time: 76.6 us -> 70 us (0.914)
  waiting for transfers between devices: 12.5 us -> 7.54 us
  starting transfers between devices: 11.8 us -> 9.49 us
  Pallas kernels: 13.7 us -> 15 us
    ppermute x1, waiting for transfers between devices: 4.72 us -> 0.65 us  [body(): other_queries = lax.ppermute(own[:, 64:128, :], 'inner', ACROSS_Y)]
    ppermute x1, starting transfers between devices: 2.99 us -> 0.63 us  [body(): other_queries = lax.ppermute(own[:, 64:128, :], 'inner', ACROSS_Y)]
    pallas_call x2, Pallas kernels: 2.5 us -> 3.96 us  [the longest x1 2.24 us: body(): pl.pallas_call(own_work_kernel, out_shape=[shape(SLOTS, MID_ROWS, HEAD_DI...]
    ppermute x1, waiting for transfers between devices: 4.98 us -> 4.09 us  [body(): other = lax.ppermute(own[:, 0:64, :], 'inner', ACROSS_Y)]
  transfers between devices with their start and end apart: 3 -> 3, of which waited for: 3 -> 3; matrix products, arithmetic and copies ran while one was open for 0% -> 0% of each run, Pallas kernels for 3% -> 7%
where the time goes in v6:
time: 70 us; the launch traced here: 69 us
  blocking collectives  36.3 us (52%)
  Pallas kernels  15 us (21%)
  starting transfers between devices  9.49 us (14%)
  waiting for transfers between devices  7.54 us (11%)
    all_to_all x1, blocking collectives, body(): own = lax.all_to_all(packed, 'inner', 0, 0, axis_index_groups=ALONG_Z)  22 us
    all_to_all x1, blocking collectives, body(): returned = lax.all_to_all(results, 'inner', 0, 0, axis_index_groups=ALONG_Z)  14.3 us
    all_to_all x1, starting transfers between devices, body(): wide_got = lax.all_to_all(wide_send, 'outer', 0, 0)  5.87 us
    pallas_call x2, Pallas kernels, near_heads(): pl.pallas_call(functools.partial(near_kernel, core), out_shape=[shape(TOK...  4.74 us
    ppermute x1, waiting for transfers between devices, body(): other = lax.ppermute(own[:, 0:64, :], 'inner', ACROSS_Y)  4.09 us
    ppermute x1, starting transfers between devices, body(): other = lax.ppermute(own[:, 0:64, :], 'inner', ACROSS_Y)  2.99 us
    all_to_all x1, waiting for transfers between devices, body(): wide_got = lax.all_to_all(wide_send, 'outer', 0, 0)  2.81 us
    pallas_call x1, Pallas kernels, body(): pl.pallas_call(own_work_kernel, out_shape=[shape(SLOTS, MID_ROWS, HEAD_DI...  2.24 us
  transfers between devices with their start and end apart: 3, of which 3 were waited for; matrix products, arithmetic and copies ran while one was open for 0% of the time, Pallas kernels for 7%

profile of v6, /device:TPU:2, one launch (start us, length us, event | category | flops | bytes accessed | tf_op | source)
XLA Modules:
  0.0 69.0 jit_solution(7070454764488565622)
XLA Ops:
  0.6 2.2 %shard_map.76 = (bf16[16,16,256]{2,1,0:T(8,128)(2,1)}, s32[8,256]{1,0:T(8,128)S(1)}) custom-call(s32[8]{0:T(128)} %off_hbm.1, bf16[256,1536]{1,0:T(8,128)(2,1)} %q_hbm.7, bf16[256,1536]{1,0:T(8,128)(2,1)} %k_hbm.7, bf16[256,1536]{1,0:T(8,128)(2,1)} %v_hbm.7, bf16[256,1536]{1,0:T(8,128)(2,1)} %g_hbm.7), custom_call_target="tpu_custom_call" | custom-call | tf_op jit(solution)/shard_map/pallas_call | solution.py:353
  2.8 5.9 %all-to-all-start = ((bf16[16,16,256]{2,1,0:T(8,128)(2,1)}), bf16[16,16,256]{2,1,0:T(8,128)(2,1)S(1)}, u32[]{:S(2)}, u32[]{:S(2)}) async-start(bf16[16,16,256]{2,1,0:T(8,128)(2,1)} %get-tuple-element.15), calls=%async_computation | async-start | bytes 262144 | tf_op jit(solution)/shard_map/all_to_all | solution.py:366
  8.7 2.0 %shard_map.77.packed = bf16[8,128,256]{2,1,0:T(8,128)(2,1)S(1)} custom-call(s32[8,256]{1,0:T(8,128)S(1)} %get-tuple-element.14.off_ref, bf16[256,1536]{1,0:T(8,128)(2,1)} %q_hbm.7, bf16[256,1536]{1,0:T(8,128)(2,1)} %k_hbm.7, bf16[256,1536]{1,0:T(8,128)(2,1)} %v_hbm.7, bf16[256,1536]{1,0:T(8,128)(2,1)} %g_hbm.7), custom_call_target="tpu_custom_call" | custom-call | flops 83886080 | bytes 1310720 | tf_op jit(solution)/shard_map/pallas_call | solution.py:367
  10.7 2.8 %all-to-all-done.after.got_ref = bf16[16,16,256]{2,1,0:T(8,128)(2,1)S(1)} async-done(((bf16[16,16,256]{2,1,0:T(8,128)(2,1)}), bf16[16,16,256]{2,1,0:T(8,128)(2,1)S(1)}, u32[]{:S(2)}, u32[]{:S(2)}) %all-to-all-start) | async-done | bytes 131104 | tf_op jit(solution)/shard_map/all_to_all | solution.py:366
  13.5 4.5 %shard_map.78 = (bf16[256,1536]{1,0:T(8,128)(2,1)}, bf16[256,1536]{1,0:T(8,128)(2,1)}, bf16[256,1536]{1,0:T(8,128)(2,1)}) custom-call(bf16[16,16,256]{2,1,0:T(8,128)(2,1)S(1)} %all-to-all-done.after.got_ref, bf16[256,1536]{1,0:T(8,128)(2,1)} %q_hbm.7, bf16[256,1536]{1,0:T(8,128)(2,1)} %k_hbm.7, bf16[256,1536]{1,0:T(8,128)(2,1)} %v_hbm.7, bf16[256,1536]{1,0:T(8,128)(2,1)} %g_hbm.7), custom_call_target="tpu_custom_call" | custom-call | flops 335544320 | bytes 1835008 | tf_op jit(solution)/shard_map/pallas_call | solution.py:175
  18.0 0.6 shard_map.79
  18.6 22.0 %all_to_all.15.after.own_ref = bf16[8,128,256]{2,1,0:T(8,128)(2,1)S(1)} all-to-all(bf16[8,128,256]{2,1,0:T(8,128)(2,1)S(1)} %shard_map.79), channel_id=1, replica_groups={{0,2,4,6,8,10,12,14},{1,3,5,7,9,11,13,15},{16,18,20,22,24,26,28,30},{17..., dimensions={0} | all-to-all | bytes 1048576 | tf_op jit(solution)/shard_map/all_to_all | solution.py:396
  40.7 3.0 %collective-permute-start = (bf16[8,64,256]{2,1,0:T(8,128)(2,1)S(1)}, bf16[8,64,256]{2,1,0:T(8,128)(2,1)S(1)}, u32[]{:S(2)}, u32[]{:S(2)}) collective-permute-start(bf16[8,64,256]{2,1,0:T(8,128)(2,1)S(1)} %get-tuple-element.26), channel_id=1, source_target_pairs={{0,1},{1,0},{2,3},{3,2},{4,5},{5,4},{6,7},{7,6},{8,9},{9,8},{10,11... | collective-permute-start | bytes 786440 | tf_op jit(solution)/shard_map/ppermute | solution.py:397
  43.7 0.6 collective-permute-start.1
  44.3 0.3 shard_map.80
  44.6 4.1 %collective-permute-done.other_ref = bf16[8,64,256]{2,1,0:T(8,128)(2,1)S(1)} collective-permute-done((bf16[8,64,256]{2,1,0:T(8,128)(2,1)S(1)}, bf16[8,64,256]{2,1,0:T(8,128)(2,1)S(1)}, u32[]{:S(2)}, u32[]{:S(2)}) %collective-permute-start) | collective-permute-done | bytes 262176 | tf_op jit(solution)/shard_map/ppermute | solution.py:397
  48.6 2.2 %shard_map.81 = (bf16[8,64,128]{2,1,0:T(8,128)(2,1)S(1)}, f32[512,256]{1,0:T(8,128)S(1)}, bf16[8,16,128]{2,1,0:T(8,128)(2,1)S(1)}) custom-call(bf16[8,128,256]{2,1,0:T(8,128)(2,1)S(1)} %all_to_all.15.after.own_ref, bf16[8,64,256]{2,1,0:T(8,128)(2,1)S(1)} %collective-permute-done.other_ref, bf16[256,1536]{1,0:T(8,128)(2,1)} %get-tuple-element.19.after.nq), custom_call_target="tpu_custom_call" | custom-call | flops 671088640 | tf_op jit(solution)/shard_map/pallas_call | solution.py:400
  50.9 0.6 collective-permute-done.1.query_ref
  51.5 1.7 %shard_map.82 = bf16[8,192,128]{2,1,0:T(8,128)(2,1)S(1)} custom-call(bf16[8,128,256]{2,1,0:T(8,128)(2,1)S(1)} %all_to_all.15.after.own_ref, bf16[8,64,256]{2,1,0:T(8,128)(2,1)S(1)} %collective-permute-done.other_ref, bf16[8,64,256]{2,1,0:T(8,128)(2,1)S(1)} %collective-permute-done.1.query_ref, bf16[8,64,128]{2,1,0:T(8,128)(2,1)S(1)} %get-tuple-element.20.dq_ref, ...), custom_call_target="tpu_custom_call" | custom-call | flops 536870912 | tf_op jit(solution)/shard_map/pallas_call | solution.py:412
  53.3 14.3 %all_to_all.16.got_ref = bf16[8,192,128]{2,1,0:T(8,128)(2,1)S(1)} all-to-all(bf16[8,192,128]{2,1,0:T(8,128)(2,1)S(1)} %shard_map.82), channel_id=1, replica_groups={{0,2,4,6,8,10,12,14},{1,3,5,7,9,11,13,15},{16,18,20,22,24,26,28,30},{17..., dimensions={0} | all-to-all | bytes 786432 | tf_op jit(solution)/shard_map/all_to_all | solution.py:421
  67.5 1.5 %shard_map.83 = (bf16[256,1536]{1,0:T(8,128)(2,1)}, bf16[256,1536]{1,0:T(8,128)(2,1)}, bf16[256,1536]{1,0:T(8,128)(2,1)}) custom-call(s32[8,256]{1,0:T(8,128)S(1)} %get-tuple-element.14.off_ref, bf16[8,192,128]{2,1,0:T(8,128)(2,1)S(1)} %all_to_all.16.got_ref, ...), custom_call_target="tpu_custom_call", output_to_operand_aliasing={{0}: (2, {}), {1}: (3, {}), {2}: (4, {})} | custom-call | tf_op jit(solution)/shard_map/pallas_call | solution.py:423
  (1 shorter events, 0.0 us)
Async XLA Ops:
  2.8 10.7 %all-to-all-start = ((bf16[16,16,256]{2,1,0:T(8,128)(2,1)}), bf16[16,16,256]{2,1,0:T(8,128)(2,1)S(1)}, u32[]{:S(2)}, u32[]{:S(2)}) async-start(bf16[16,16,256]{2,1,0:T(8,128)(2,1)} %get-tuple-element.15), calls=%async_computation | async-start | bytes 262144 | tf_op jit(solution)/shard_map/all_to_all | solution.py:366
  40.7 8.0 %collective-permute-start = (bf16[8,64,256]{2,1,0:T(8,128)(2,1)S(1)}, bf16[8,64,256]{2,1,0:T(8,128)(2,1)S(1)}, u32[]{:S(2)}, u32[]{:S(2)}) collective-permute-start(bf16[8,64,256]{2,1,0:T(8,128)(2,1)S(1)} %get-tuple-element.26), channel_id=1, source_target_pairs={{0,1},{1,0},{2,3},{3,2},{4,5},{5,4},{6,7},{7,6},{8,9},{9,8},{10,11... | collective-permute-start | bytes 786440 | tf_op jit(solution)/shard_map/ppermute | solution.py:397
  43.7 7.9 %collective-permute-start.1 = (bf16[8,64,256]{2,1,0:T(8,128)(2,1)S(1)}, bf16[8,64,256]{2,1,0:T(8,128)(2,1)S(1)}, u32[]{:S(2)}, u32[]{:S(2)}) collective-permute-start(bf16[8,64,256]{2,1,0:T(8,128)(2,1)S(1)} %get-tuple-element.25), channel_id=1, source_target_pairs={{0,1},{1,0},{2,3},{3,2},{4,5},{5,4},{6,7},{7,6},{8,9},{9,8},{10,11... | collective-permute-start | bytes 786440 | tf_op jit(solution)/shard_map/ppermute | solution.py:398

commit v7 on v6

--- a/solution.py
+++ b/solution.py
@@ -103,14 +103,28 @@
     off_copy.wait()
     for head in range(H_MID + H_WIDE):
         off_out[head : head + 1, :] = jnp.full((1, TOK), off_ref[head], jnp.int32)
-    row, column = iota2(16, TOK)
-    rows = 0.0
+    row, unused = iota2(16, HEAD_DIM)
+    row_pair, unused = iota2(16, 2 * HEAD_DIM)
+    rows = jnp.zeros((16, 2 * HEAD_DIM), F32)
     for at, head in enumerate(heads):
-        kv, qg = pairs(copies, held, head, at)
         offset = off_ref[head]
-        for start, block in ((2 * at, kv), (6 + 2 * at, qg)):
-            mine = (row >= start) & (row < start + 2)
-            rows += dot(one_hot(mine & (column == offset + R_WIDE * (row - start))), block)
+        base, place = lax.div(offset, 16) * 16, lax.rem(offset, 16)
+        for which in range(4):
+            copies[head, which].wait()
+        for again in range(2):
+            tile = pl.ds(pl.multiple_of(base + again * R_WIDE, 16), 16)
+            picked = [
+                jnp.sum(
+                    jnp.where(row == place, held[which, at, tile, :].astype(F32), 0.0),
+                    axis=0,
+                    keepdims=True,
+                )
+                for which in range(4)
+            ]
+            kv = jnp.concatenate([picked[1], picked[2]], axis=1)
+            qg = jnp.concatenate([picked[0], picked[3]], axis=1)
+            rows = jnp.where(row_pair == 2 * at + again, kv, rows)
+            rows = jnp.where(row_pair == 6 + 2 * at + again, qg, rows)
     rows = rows.astype(BF16)
     for target in range(OUTERS):
         out_ref[target] = rows
@@ -128,20 +142,13 @@
         out_ref[head, 64:128, :] = jnp.zeros((64, 2 * HEAD_DIM), BF16)
 
 
-def wide_pack_kernel(got_ref, packed, after, out, held, sems):
+def wide_pack_kernel(got_ref, packed, after, out_ref):
     rows = got_ref[...].reshape(OUTERS * 16, 2 * HEAD_DIM)
     row, column = iota2(64, OUTERS * 16)
     base = 16 * ((row % 32) // 2) + row % 2 + jnp.where(row < 32, 0, 6)
-    copies = []
     for head in range(H_WIDE):
-        held[head] = dot(one_hot(column == base + 2 * head), rows).astype(BF16)
-        copy = pltpu.make_async_copy(
-            held.at[head], out.at[H_MID + head, pl.ds(0, 64)], sems.at[head]
-        )
-        copy.start()
-        copies.append(copy)
-    for copy in copies:
-        copy.wait()
+        picked = dot(one_hot(column == base + 2 * head), rows)
+        out_ref[H_MID + head, 0:64, :] = picked.astype(BF16)
 
 
 def near_kernel(core, after, q_hbm, k_hbm, v_hbm, g_hbm, *rest):
@@ -282,14 +289,13 @@
             before = dkv_ref if start == 0 else sum_ref
             sum_ref[:, :HEAD_DIM] = before[:, :HEAD_DIM] + dot(score_gradients, query)
             sum_ref[:, HEAD_DIM:] = before[:, HEAD_DIM:] + dot(weights, gradient)
-        out_ref[:, 0:64, :] = dq_ref[...]
+        out_ref[:, :, :HEAD_DIM] = dq_ref[...]
         dkv = sum_ref[...].astype(BF16)
-        out_ref[:, 64:128, :] = dkv[:, :HEAD_DIM].reshape(SLOTS, MID_ROWS, HEAD_DIM)
-        out_ref[:, 128:192, :] = dkv[:, HEAD_DIM:].reshape(SLOTS, MID_ROWS, HEAD_DIM)
+        out_ref[:, :, HEAD_DIM:] = dkv.reshape(SLOTS, MID_ROWS, 2 * HEAD_DIM)
 
     @pl.when(slot() >= H_MID)
     def wide():
-        out_ref[:, 0:16, :] = wide_ref[...]
+        out_ref[:, 0:16, :HEAD_DIM] = wide_ref[...]
 
 
 def assemble_kernel(off_ref, got_ref, nq, nk, nv, dq_hbm, dk_hbm, dv_hbm, held, sems):
@@ -309,7 +315,7 @@
     row, unused = iota2(TOK, HEAD_DIM)
     for head in range(H_MID, H_MID + H_WIDE):
         offset = off_ref[head : head + 1, :HEAD_DIM]
-        rows = got_ref[head, 0:16, :].astype(F32)
+        rows = got_ref[head, 0:16, :HEAD_DIM].astype(F32)
         first, second = row == offset, row == offset + R_WIDE
         for which in range(3):
             spread = jnp.where(first, rows[2 * which : 2 * which + 1], 0.0)
@@ -317,8 +323,9 @@
     row, column = iota2(TOK, MID_ROWS)
     for head in range(H_MID):
         place = one_hot(row - R_MID * column == off_ref[head : head + 1, :1])
+        spread = dot(place, got_ref[head])
         for which in range(3):
-            send(which, head, dot(place, got_ref[head, 64 * which : 64 * which + 64, :]))
+            send(which, head, spread[:, which * HEAD_DIM : (which + 1) * HEAD_DIM])
     for copy in copies:
         copy.wait()
 
@@ -380,16 +387,12 @@
         ),
         compiler_params=params(8),
     )(offset_rows, *arrays)
-    near = near_heads(0, wide_got, arrays)
+    near = near_heads(0, offset_rows, arrays)
     packed = pl.pallas_call(
         wide_pack_kernel,
         out_shape=shape(SLOTS, 128, 256),
-        in_specs=[spec(pltpu.VMEM), spec(pl.ANY), spec(pl.ANY)],
-        out_specs=spec(pl.ANY),
-        scratch_shapes=[
-            pltpu.VMEM((H_WIDE, 64, 256), BF16),
-            pltpu.SemaphoreType.DMA((H_WIDE,)),
-        ],
+        in_specs=[spec(pltpu.VMEM), spec(pltpu.VMEM), spec(pl.ANY)],
+        out_specs=spec(pltpu.VMEM),
         input_output_aliases={1: 0},
         compiler_params=params(8),
     )(wide_got, packed, in_hbm(near[0]))
@@ -411,7 +414,7 @@
     )(own, other, in_hbm(near[0]))
     results = pl.pallas_call(
         other_work_kernel,
-        out_shape=shape(SLOTS, 192, HEAD_DIM),
+        out_shape=shape(SLOTS, MID_ROWS, 3 * HEAD_DIM),
         in_specs=[spec(pltpu.VMEM)] * 6,
         out_specs=spec(pltpu.VMEM),
         scratch_shapes=[pltpu.VMEM((HALF_KEYS, 256), F32)],

time: 70 us -> 73.2 us (1.046)
  the two profiles are of different devices: /device:TPU:2 before, /device:TPU:16 now
where the time goes in v7:
time: 73.2 us; the launch traced here: 72.8 us
  blocking collectives  41.4 us (57%)
  Pallas kernels  14.4 us (20%)
  starting transfers between devices  8.75 us (12%)
  waiting for transfers between devices  7.52 us (10%)
    all_to_all x1, blocking collectives, body(): own = lax.all_to_all(packed, 'inner', 0, 0, axis_index_groups=ALONG_Z)  25.9 us
    all_to_all x1, blocking collectives, body(): returned = lax.all_to_all(results, 'inner', 0, 0, axis_index_groups=ALONG_Z)  15.6 us
    ppermute x1, waiting for transfers between devices, body(): other = lax.ppermute(own[:, 0:64, :], 'inner', ACROSS_Y)  6.96 us
    all_to_all x1, starting transfers between devices, body(): wide_got = lax.all_to_all(wide_send, 'outer', 0, 0)  5.14 us
    pallas_call x2, Pallas kernels, near_heads(): pl.pallas_call(functools.partial(near_kernel, core), out_shape=[shape(TOK...  4.76 us
    ppermute x1, starting transfers between devices, body(): other_queries = lax.ppermute(own[:, 64:128, :], 'inner', ACROSS_Y)  2.9 us
    pallas_call x1, Pallas kernels, body(): pl.pallas_call(own_work_kernel, out_shape=[shape(SLOTS, MID_ROWS, HEAD_DI...  2.25 us
    pallas_call x1, Pallas kernels, body(): pl.pallas_call(mid_pack_kernel, out_shape=shape(SLOTS, 128, 256), in_spec...  2.02 us
  transfers between devices with their start and end apart: 3, of which 2 were waited for; matrix products, arithmetic and copies ran while one was open for 0% of the time, Pallas kernels for 12%

profile of v7, /device:TPU:16, one launch (start us, length us, event | category | flops | bytes accessed | tf_op | source)
XLA Modules:
  0.0 72.8 jit_solution(15014661396376880937)
XLA Ops:
  0.6 2.0 %shard_map.76 = (bf16[16,16,256]{2,1,0:T(8,128)(2,1)}, s32[8,256]{1,0:T(8,128)S(1)}) custom-call(s32[8]{0:T(128)} %off_hbm.1, bf16[256,1536]{1,0:T(8,128)(2,1)} %q_hbm.7, bf16[256,1536]{1,0:T(8,128)(2,1)} %k_hbm.7, bf16[256,1536]{1,0:T(8,128)(2,1)} %v_hbm.7, bf16[256,1536]{1,0:T(8,128)(2,1)} %g_hbm.7), custom_call_target="tpu_custom_call" | custom-call | tf_op jit(solution)/shard_map/pallas_call | solution.py:360
  2.6 5.1 %all-to-all-start = ((bf16[16,16,256]{2,1,0:T(8,128)(2,1)}), bf16[16,16,256]{2,1,0:T(8,128)(2,1)S(1)}, u32[]{:S(2)}, u32[]{:S(2)}) async-start(bf16[16,16,256]{2,1,0:T(8,128)(2,1)} %get-tuple-element.15), calls=%async_computation | async-start | bytes 262144 | tf_op jit(solution)/shard_map/all_to_all | solution.py:373
  7.8 2.0 %shard_map.77.packed = bf16[8,128,256]{2,1,0:T(8,128)(2,1)S(1)} custom-call(s32[8,256]{1,0:T(8,128)S(1)} %get-tuple-element.14.off_ref.after, bf16[256,1536]{1,0:T(8,128)(2,1)} %q_hbm.7, bf16[256,1536]{1,0:T(8,128)(2,1)} %k_hbm.7, bf16[256,1536]{1,0:T(8,128)(2,1)} %v_hbm.7, bf16[256,1536]{1,0:T(8,128)(2,1)} %g_hbm.7), custom_call_target="tpu_custom_call" | custom-call | flops 83886080 | bytes 1310720 | tf_op jit(solution)/shard_map/pallas_call | solution.py:374
  9.8 4.5 %shard_map.78 = (bf16[256,1536]{1,0:T(8,128)(2,1)}, bf16[256,1536]{1,0:T(8,128)(2,1)}, bf16[256,1536]{1,0:T(8,128)(2,1)}) custom-call(s32[8,256]{1,0:T(8,128)S(1)} %get-tuple-element.14.off_ref.after, bf16[256,1536]{1,0:T(8,128)(2,1)} %q_hbm.7, bf16[256,1536]{1,0:T(8,128)(2,1)} %k_hbm.7, bf16[256,1536]{1,0:T(8,128)(2,1)} %v_hbm.7, bf16[256,1536]{1,0:T(8,128)(2,1)} %g_hbm.7), custom_call_target="tpu_custom_call" | custom-call | flops 335544320 | bytes 1835008 | tf_op jit(solution)/shard_map/pallas_call | solution.py:182
  14.3 0.0 all-to-all-done.got_ref
  14.3 0.2 shard_map.79
  14.5 25.9 %all_to_all.15.after.own_ref = bf16[8,128,256]{2,1,0:T(8,128)(2,1)S(1)} all-to-all(bf16[8,128,256]{2,1,0:T(8,128)(2,1)S(1)} %shard_map.79), channel_id=1, replica_groups={{0,2,4,6,8,10,12,14},{1,3,5,7,9,11,13,15},{16,18,20,22,24,26,28,30},{17..., dimensions={0} | all-to-all | bytes 1048576 | tf_op jit(solution)/shard_map/all_to_all | solution.py:399
  40.4 0.7 collective-permute-start
  41.1 2.9 %collective-permute-start.1 = (bf16[8,64,256]{2,1,0:T(8,128)(2,1)S(1)}, bf16[8,64,256]{2,1,0:T(8,128)(2,1)S(1)}, u32[]{:S(2)}, u32[]{:S(2)}) collective-permute-start(bf16[8,64,256]{2,1,0:T(8,128)(2,1)S(1)} %get-tuple-element.25), channel_id=1, source_target_pairs={{0,1},{1,0},{2,3},{3,2},{4,5},{5,4},{6,7},{7,6},{8,9},{9,8},{10,11... | collective-permute-start | bytes 786440 | tf_op jit(solution)/shard_map/ppermute | solution.py:401
  44.0 0.3 shard_map.80
  44.3 7.0 %collective-permute-done.other_ref = bf16[8,64,256]{2,1,0:T(8,128)(2,1)S(1)} collective-permute-done((bf16[8,64,256]{2,1,0:T(8,128)(2,1)S(1)}, bf16[8,64,256]{2,1,0:T(8,128)(2,1)S(1)}, u32[]{:S(2)}, u32[]{:S(2)}) %collective-permute-start) | collective-permute-done | bytes 262176 | tf_op jit(solution)/shard_map/ppermute | solution.py:400
  51.2 2.2 %shard_map.81 = (bf16[8,64,128]{2,1,0:T(8,128)(2,1)S(1)}, f32[512,256]{1,0:T(8,128)S(1)}, bf16[8,16,128]{2,1,0:T(8,128)(2,1)S(1)}) custom-call(bf16[8,128,256]{2,1,0:T(8,128)(2,1)S(1)} %all_to_all.15.after.own_ref, bf16[8,64,256]{2,1,0:T(8,128)(2,1)S(1)} %collective-permute-done.other_ref, bf16[256,1536]{1,0:T(8,128)(2,1)} %get-tuple-element.19.after.nq), custom_call_target="tpu_custom_call" | custom-call | flops 671088640 | tf_op jit(solution)/shard_map/pallas_call | solution.py:403
  53.5 0.6 collective-permute-done.1.query_ref
  54.1 1.7 %shard_map.82 = bf16[8,64,384]{2,1,0:T(8,128)(2,1)S(1)} custom-call(bf16[8,128,256]{2,1,0:T(8,128)(2,1)S(1)} %all_to_all.15.after.own_ref, bf16[8,64,256]{2,1,0:T(8,128)(2,1)S(1)} %collective-permute-done.other_ref, bf16[8,64,256]{2,1,0:T(8,128)(2,1)S(1)} %collective-permute-done.1.query_ref, bf16[8,64,128]{2,1,0:T(8,128)(2,1)S(1)} %get-tuple-element.20.dq_ref, ...), custom_call_target="tpu_custom_call" | custom-call | flops 536870912 | tf_op jit(solution)/shard_map/pallas_call | solution.py:415
  55.8 15.6 %all_to_all.16.got_ref = bf16[8,64,384]{2,1,0:T(8,128)(2,1)S(1)} all-to-all(bf16[8,64,384]{2,1,0:T(8,128)(2,1)S(1)} %shard_map.82), channel_id=1, replica_groups={{0,2,4,6,8,10,12,14},{1,3,5,7,9,11,13,15},{16,18,20,22,24,26,28,30},{17..., dimensions={0} | all-to-all | bytes 786432 | tf_op jit(solution)/shard_map/all_to_all | solution.py:424
  71.3 1.5 %shard_map.83 = (bf16[256,1536]{1,0:T(8,128)(2,1)}, bf16[256,1536]{1,0:T(8,128)(2,1)}, bf16[256,1536]{1,0:T(8,128)(2,1)}) custom-call(s32[8,256]{1,0:T(8,128)S(1)} %get-tuple-element.14.off_ref.after, bf16[8,64,384]{2,1,0:T(8,128)(2,1)S(1)} %all_to_all.16.got_ref, ...), custom_call_target="tpu_custom_call", output_to_operand_aliasing={{0}: (2, {}), {1}: (3, {}), {2}: (4, {})} | custom-call | tf_op jit(solution)/shard_map/pallas_call | solution.py:426
  (1 shorter events, 0.0 us)
Async XLA Ops:
  2.6 11.7 %all-to-all-start = ((bf16[16,16,256]{2,1,0:T(8,128)(2,1)}), bf16[16,16,256]{2,1,0:T(8,128)(2,1)S(1)}, u32[]{:S(2)}, u32[]{:S(2)}) async-start(bf16[16,16,256]{2,1,0:T(8,128)(2,1)} %get-tuple-element.15), calls=%async_computation | async-start | bytes 262144 | tf_op jit(solution)/shard_map/all_to_all | solution.py:373
  40.4 10.8 %collective-permute-start = (bf16[8,64,256]{2,1,0:T(8,128)(2,1)S(1)}, bf16[8,64,256]{2,1,0:T(8,128)(2,1)S(1)}, u32[]{:S(2)}, u32[]{:S(2)}) collective-permute-start(bf16[8,64,256]{2,1,0:T(8,128)(2,1)S(1)} %get-tuple-element.26), channel_id=1, source_target_pairs={{0,1},{1,0},{2,3},{3,2},{4,5},{5,4},{6,7},{7,6},{8,9},{9,8},{10,11... | collective-permute-start | bytes 786440 | tf_op jit(solution)/shard_map/ppermute | solution.py:400
  41.1 12.9 %collective-permute-start.1 = (bf16[8,64,256]{2,1,0:T(8,128)(2,1)S(1)}, bf16[8,64,256]{2,1,0:T(8,128)(2,1)S(1)}, u32[]{:S(2)}, u32[]{:S(2)}) collective-permute-start(bf16[8,64,256]{2,1,0:T(8,128)(2,1)S(1)} %get-tuple-element.25), channel_id=1, source_target_pairs={{0,1},{1,0},{2,3},{3,2},{4,5},{5,4},{6,7},{7,6},{8,9},{9,8},{10,11... | collective-permute-start | bytes 786440 | tf_op jit(solution)/shard_map/ppermute | solution.py:401

commit v8 on v7

--- a/solution.py
+++ b/solution.py
@@ -23,10 +23,11 @@
 SLOTS = 8
 HALVES = 2
 HALF_KEYS = SLOTS * MID_ROWS
-QUERY_BLOCK = 256
 ALONG_Z = [[HALVES * z + half for z in range(SLOTS)] for half in range(HALVES)]
 ACROSS_Y = [(member, member ^ 1) for member in range(HALVES * SLOTS)]
 SCALE = 1.0 / math.sqrt(HEAD_DIM)
+EARLY_NEAR = (range(3), range(0))
+LATE_NEAR = tuple(range(len(early), H_NEAR) for early in EARLY_NEAR)
 EXP2_SCALE = SCALE * math.log2(math.e)
 BF16 = jnp.bfloat16
 F32 = jnp.float32
@@ -151,36 +152,43 @@
         out_ref[H_MID + head, 0:64, :] = picked.astype(BF16)
 
 
-def near_kernel(core, after, q_hbm, k_hbm, v_hbm, g_hbm, *rest):
+def near_some(sources, targets, held, results, sems, out_sems, heads):
+    copies = fetch(sources, held, sems, heads, 0)
+    sends = []
+    for at, head in enumerate(heads):
+        for which in range(4):
+            copies[head, which].wait()
+        query, key, value, gradient = (held[which, at] for which in range(4))
+        weights, score_gradients = attention_transposed(query, key, value, gradient)
+        results[0, at] = dot_tn(score_gradients, key).astype(BF16)
+        results[1, at] = dot(score_gradients, query).astype(BF16)
+        results[2, at] = dot(weights, gradient).astype(BF16)
+        for which, target in enumerate(targets):
+            send = pltpu.make_async_copy(
+                results.at[which, at],
+                target.at[:, pl.ds(head * HEAD_DIM, HEAD_DIM)],
+                out_sems.at[which, at],
+            )
+            send.start()
+            sends.append(send)
+    for send in sends:
+        send.wait()
+
+
+def near_kernel(heads_of_core, after, q_hbm, k_hbm, v_hbm, g_hbm, *rest):
     targets, (held, results, sems, out_sems) = rest[-7:-4], rest[-4:]
-
-    @pl.when(lax.rem(lax.axis_index("outer"), 2) == core)
-    def attend():
-        copies = fetch((q_hbm, k_hbm, v_hbm, g_hbm), held, sems, range(H_NEAR), 0)
-        sends = []
-        for head in range(H_NEAR):
-            for which in range(4):
-                copies[head, which].wait()
-            query, key, value, gradient = (held[which, head] for which in range(4))
-            weights, score_gradients = attention_transposed(query, key, value, gradient)
-            results[0, head] = dot_tn(score_gradients, key).astype(BF16)
-            results[1, head] = dot(score_gradients, query).astype(BF16)
-            results[2, head] = dot(weights, gradient).astype(BF16)
-            for which, target in enumerate(targets):
-                send = pltpu.make_async_copy(
-                    results.at[which, head],
-                    target.at[:, pl.ds(head * HEAD_DIM, HEAD_DIM)],
-                    out_sems.at[which, head],
-                )
-                send.start()
-                sends.append(send)
-        for send in sends:
-            send.wait()
-
-
-def near_heads(core, after, arrays, previous=()):
+    for core, heads in enumerate(heads_of_core):
+        if heads:
+
+            @pl.when(lax.rem(lax.axis_index("outer"), 2) == core)
+            def attend(heads=heads):
+                sources = (q_hbm, k_hbm, v_hbm, g_hbm)
+                near_some(sources, targets, held, results, sems, out_sems, heads)
+
+
+def near_heads(heads_of_core, after, arrays, previous=()):
     return pl.pallas_call(
-        functools.partial(near_kernel, core),
+        functools.partial(near_kernel, heads_of_core),
         out_shape=[shape(TOK, HIDDEN)] * 3,
         in_specs=[spec(pl.ANY)] + [spec(pltpu.HBM)] * (4 + len(previous)),
         out_specs=[spec(pltpu.HBM)] * 3,
@@ -255,43 +263,28 @@
 
     @pl.when(slot() < H_MID)
     def attend():
-        own_key, own_value = halves(own_ref, slice(0, 64))
-        other_key, other_value = halves(other_ref, slice(0, 64))
-        key = jnp.concatenate([own_key, other_key], axis=0)
-        value = jnp.concatenate([own_value, other_value], axis=0)
-        queries, gradients = halves(own_ref, slice(64, 128))
-        for start in range(0, HALF_KEYS, QUERY_BLOCK):
-            query = queries[start : start + QUERY_BLOCK]
-            gradient = gradients[start : start + QUERY_BLOCK]
-            weights, score_gradients = attention_transposed(query, key, value, gradient)
-            dk = dot(score_gradients[:HALF_KEYS], query)
-            dv = dot(weights[:HALF_KEYS], gradient)
-            if start == 0:
-                dkv_ref[:, :HEAD_DIM] = dk
-                dkv_ref[:, HEAD_DIM:] = dv
-            else:
-                dkv_ref[:, :HEAD_DIM] += dk
-                dkv_ref[:, HEAD_DIM:] += dv
-            dq = dot_tn(key, score_gradients).T.astype(BF16)
-            blocks = slice(start // MID_ROWS, (start + QUERY_BLOCK) // MID_ROWS)
-            dq_ref[blocks] = dq.reshape(QUERY_BLOCK // MID_ROWS, MID_ROWS, HEAD_DIM)
-
-
-def other_work_kernel(own_ref, other_ref, query_ref, dq_ref, dkv_ref, wide_ref, out_ref, sum_ref):
+        parts = [halves(own_ref, slice(0, 64)), halves(other_ref, slice(0, 64))]
+        key, value = (jnp.concatenate(pieces, axis=0) for pieces in zip(*parts))
+        query, gradient = halves(own_ref, slice(64, 128))
+        weights, score_gradients = attention_transposed(query, key, value, gradient)
+        dkv_ref[:, :HEAD_DIM] = dot(score_gradients[:HALF_KEYS], query)
+        dkv_ref[:, HEAD_DIM:] = dot(weights[:HALF_KEYS], gradient)
+        dq = dot_tn(key, score_gradients).T.astype(BF16)
+        dq_ref[...] = dq.reshape(SLOTS, MID_ROWS, HEAD_DIM)
+
+
+def other_work_kernel(own_ref, other_ref, query_ref, dq_ref, dkv_ref, wide_ref, out_ref):
     @pl.when(slot() < H_MID)
     def attend():
         parts = [halves(own_ref, slice(0, 64)), halves(other_ref, slice(0, 64))]
-        queries, gradients = halves(query_ref, slice(0, 64))
-        for start in range(0, HALF_KEYS, QUERY_BLOCK):
-            query = queries[start : start + QUERY_BLOCK]
-            gradient = gradients[start : start + QUERY_BLOCK]
-            weights, score_gradients = scaled_weights(parts, query, gradient)
-            before = dkv_ref if start == 0 else sum_ref
-            sum_ref[:, :HEAD_DIM] = before[:, :HEAD_DIM] + dot(score_gradients, query)
-            sum_ref[:, HEAD_DIM:] = before[:, HEAD_DIM:] + dot(weights, gradient)
+        query, gradient = halves(query_ref, slice(0, 64))
+        weights, score_gradients = scaled_weights(parts, query, gradient)
+        dk = dkv_ref[:, :HEAD_DIM] + dot(score_gradients, query)
+        dv = dkv_ref[:, HEAD_DIM:] + dot(weights, gradient)
         out_ref[:, :, :HEAD_DIM] = dq_ref[...]
-        dkv = sum_ref[...].astype(BF16)
-        out_ref[:, :, HEAD_DIM:] = dkv.reshape(SLOTS, MID_ROWS, 2 * HEAD_DIM)
+        for at, sums in ((HEAD_DIM, dk), (2 * HEAD_DIM, dv)):
+            sums = sums.astype(BF16).reshape(SLOTS, MID_ROWS, HEAD_DIM)
+            out_ref[:, :, at : at + HEAD_DIM] = sums
 
     @pl.when(slot() >= H_MID)
     def wide():
@@ -387,7 +380,7 @@
         ),
         compiler_params=params(8),
     )(offset_rows, *arrays)
-    near = near_heads(0, offset_rows, arrays)
+    near = near_heads(EARLY_NEAR, wide_got, arrays)
     packed = pl.pallas_call(
         wide_pack_kernel,
         out_shape=shape(SLOTS, 128, 256),
@@ -399,7 +392,7 @@
     own = lax.all_to_all(packed, "inner", 0, 0, axis_index_groups=ALONG_Z)
     other = lax.ppermute(own[:, 0:64, :], "inner", ACROSS_Y)
     other_queries = lax.ppermute(own[:, 64:128, :], "inner", ACROSS_Y)
-    near = near_heads(1, own, arrays, near)
+    near = near_heads(LATE_NEAR, own, arrays, near)
     dq, own_sums, wide_rows = pl.pallas_call(
         own_work_kernel,
         out_shape=[
@@ -417,7 +410,6 @@
         out_shape=shape(SLOTS, MID_ROWS, 3 * HEAD_DIM),
         in_specs=[spec(pltpu.VMEM)] * 6,
         out_specs=spec(pltpu.VMEM),
-        scratch_shapes=[pltpu.VMEM((HALF_KEYS, 256), F32)],
         cost_estimate=work_cost(4),
         compiler_params=params(24),
     )(own, other, other_queries, dq, own_sums, wide_rows)

time: 73.2 us -> 69.2 us (0.945)
  the two profiles are of different devices: /device:TPU:16 before, /device:TPU:2 now
where the time goes in v8:
time: 69.2 us; the launch traced here: 68.2 us
  blocking collectives  37 us (53%)
  Pallas kernels  15.4 us (22%)
  starting transfers between devices  9.49 us (14%)
  waiting for transfers between devices  5.63 us (8%)
    all_to_all x1, blocking collectives, body(): own = lax.all_to_all(packed, 'inner', 0, 0, axis_index_groups=ALONG_Z)  22.7 us
    all_to_all x1, blocking collectives, body(): returned = lax.all_to_all(results, 'inner', 0, 0, axis_index_groups=ALONG_Z)  14.3 us
    pallas_call x2, Pallas kernels, near_heads(): pl.pallas_call(functools.partial(near_kernel, heads_of_core), out_shape=[...  6.27 us
    all_to_all x1, starting transfers between devices, body(): wide_got = lax.all_to_all(wide_send, 'outer', 0, 0)  5.87 us
    ppermute x1, starting transfers between devices, body(): other = lax.ppermute(own[:, 0:64, :], 'inner', ACROSS_Y)  2.99 us
    all_to_all x1, waiting for transfers between devices, body(): wide_got = lax.all_to_all(wide_send, 'outer', 0, 0)  2.81 us
    pallas_call x1, Pallas kernels, body(): pl.pallas_call(mid_pack_kernel, out_shape=shape(SLOTS, 128, 256), in_spec...  2.02 us
    pallas_call x1, Pallas kernels, body(): pl.pallas_call(wide_kernel, out_shape=[shape(OUTERS, 16, 256), shape(head...  1.98 us
  transfers between devices with their start and end apart: 3, of which 3 were waited for; matrix products, arithmetic and copies ran while one was open for 0% of the time, Pallas kernels for 9%

profile of v8, /device:TPU:2, one launch (start us, length us, event | category | flops | bytes accessed | tf_op | source)
XLA Modules:
  0.0 68.2 jit_solution(5183544010386717560)
XLA Ops:
  0.6 2.0 %shard_map.76 = (bf16[16,16,256]{2,1,0:T(8,128)(2,1)}, s32[8,256]{1,0:T(8,128)S(1)}) custom-call(s32[8]{0:T(128)} %off_hbm.1, bf16[256,1536]{1,0:T(8,128)(2,1)} %q_hbm.7, bf16[256,1536]{1,0:T(8,128)(2,1)} %k_hbm.7, bf16[256,1536]{1,0:T(8,128)(2,1)} %v_hbm.7, bf16[256,1536]{1,0:T(8,128)(2,1)} %g_hbm.7), custom_call_target="tpu_custom_call" | custom-call | tf_op jit(solution)/shard_map/pallas_call | solution.py:353
  2.6 5.9 %all-to-all-start = ((bf16[16,16,256]{2,1,0:T(8,128)(2,1)}), bf16[16,16,256]{2,1,0:T(8,128)(2,1)S(1)}, u32[]{:S(2)}, u32[]{:S(2)}) async-start(bf16[16,16,256]{2,1,0:T(8,128)(2,1)} %get-tuple-element.15), calls=%async_computation | async-start | bytes 262144 | tf_op jit(solution)/shard_map/all_to_all | solution.py:366
  8.5 2.0 %shard_map.77.packed = bf16[8,128,256]{2,1,0:T(8,128)(2,1)S(1)} custom-call(s32[8,256]{1,0:T(8,128)S(1)} %get-tuple-element.14.off_ref, bf16[256,1536]{1,0:T(8,128)(2,1)} %q_hbm.7, bf16[256,1536]{1,0:T(8,128)(2,1)} %k_hbm.7, bf16[256,1536]{1,0:T(8,128)(2,1)} %v_hbm.7, bf16[256,1536]{1,0:T(8,128)(2,1)} %g_hbm.7), custom_call_target="tpu_custom_call" | custom-call | flops 83886080 | bytes 1310720 | tf_op jit(solution)/shard_map/pallas_call | solution.py:367
  10.5 2.8 %all-to-all-done.after.got_ref = bf16[16,16,256]{2,1,0:T(8,128)(2,1)S(1)} async-done(((bf16[16,16,256]{2,1,0:T(8,128)(2,1)}), bf16[16,16,256]{2,1,0:T(8,128)(2,1)S(1)}, u32[]{:S(2)}, u32[]{:S(2)}) %all-to-all-start) | async-done | bytes 131104 | tf_op jit(solution)/shard_map/all_to_all | solution.py:366
  13.3 3.8 %shard_map.78 = (bf16[256,1536]{1,0:T(8,128)(2,1)}, bf16[256,1536]{1,0:T(8,128)(2,1)}, bf16[256,1536]{1,0:T(8,128)(2,1)}) custom-call(bf16[16,16,256]{2,1,0:T(8,128)(2,1)S(1)} %all-to-all-done.after.got_ref, bf16[256,1536]{1,0:T(8,128)(2,1)} %q_hbm.7, bf16[256,1536]{1,0:T(8,128)(2,1)} %k_hbm.7, bf16[256,1536]{1,0:T(8,128)(2,1)} %v_hbm.7, bf16[256,1536]{1,0:T(8,128)(2,1)} %g_hbm.7), custom_call_target="tpu_custom_call" | custom-call | flops 335544320 | bytes 1835008 | tf_op jit(solution)/shard_map/pallas_call | solution.py:190
  17.1 0.2 shard_map.79
  17.3 22.7 %all_to_all.15.after.own_ref = bf16[8,128,256]{2,1,0:T(8,128)(2,1)S(1)} all-to-all(bf16[8,128,256]{2,1,0:T(8,128)(2,1)S(1)} %shard_map.79), channel_id=1, replica_groups={{0,2,4,6,8,10,12,14},{1,3,5,7,9,11,13,15},{16,18,20,22,24,26,28,30},{17..., dimensions={0} | all-to-all | bytes 1048576 | tf_op jit(solution)/shard_map/all_to_all | solution.py:392
  40.0 3.0 %collective-permute-start = (bf16[8,64,256]{2,1,0:T(8,128)(2,1)S(1)}, bf16[8,64,256]{2,1,0:T(8,128)(2,1)S(1)}, u32[]{:S(2)}, u32[]{:S(2)}) collective-permute-start(bf16[8,64,256]{2,1,0:T(8,128)(2,1)S(1)} %get-tuple-element.26), channel_id=1, source_target_pairs={{0,1},{1,0},{2,3},{3,2},{4,5},{5,4},{6,7},{7,6},{8,9},{9,8},{10,11... | collective-permute-start | bytes 786440 | tf_op jit(solution)/shard_map/ppermute | solution.py:393
  43.0 0.6 collective-permute-start.1
  43.7 2.5 %shard_map.80 = (bf16[256,1536]{1,0:T(8,128)(2,1)}, bf16[256,1536]{1,0:T(8,128)(2,1)}, bf16[256,1536]{1,0:T(8,128)(2,1)}) custom-call(bf16[8,128,256]{2,1,0:T(8,128)(2,1)S(1)} %all_to_all.15.after.own_ref, bf16[256,1536]{1,0:T(8,128)(2,1)} %q_hbm.7, bf16[256,1536]{1,0:T(8,128)(2,1)} %k_hbm.7, ...), custom_call_target="tpu_custom_call", output_to_operand_aliasing={{0}: (5, {}), {1}: (6, {}), {2}: (7, {})} | custom-call | flops 335544320 | bytes 1835008 | tf_op jit(solution)/shard_map/pallas_call | solution.py:190
  46.1 1.9 %collective-permute-done.other_ref = bf16[8,64,256]{2,1,0:T(8,128)(2,1)S(1)} collective-permute-done((bf16[8,64,256]{2,1,0:T(8,128)(2,1)S(1)}, bf16[8,64,256]{2,1,0:T(8,128)(2,1)S(1)}, u32[]{:S(2)}, u32[]{:S(2)}) %collective-permute-start) | collective-permute-done | bytes 262176 | tf_op jit(solution)/shard_map/ppermute | solution.py:393
  48.0 1.9 %shard_map.81 = (bf16[8,64,128]{2,1,0:T(8,128)(2,1)S(1)}, f32[512,256]{1,0:T(8,128)S(1)}, bf16[8,16,128]{2,1,0:T(8,128)(2,1)S(1)}) custom-call(bf16[8,128,256]{2,1,0:T(8,128)(2,1)S(1)} %all_to_all.15.after.own_ref, bf16[8,64,256]{2,1,0:T(8,128)(2,1)S(1)} %collective-permute-done.other_ref, bf16[256,1536]{1,0:T(8,128)(2,1)} %get-tuple-element.19.after.nq), custom_call_target="tpu_custom_call" | custom-call | flops 671088640 | tf_op jit(solution)/shard_map/pallas_call | solution.py:396
  49.9 1.0 %collective-permute-done.1.query_ref = bf16[8,64,256]{2,1,0:T(8,128)(2,1)S(1)} collective-permute-done((bf16[8,64,256]{2,1,0:T(8,128)(2,1)S(1)}, bf16[8,64,256]{2,1,0:T(8,128)(2,1)S(1)}, u32[]{:S(2)}, u32[]{:S(2)}) %collective-permute-start.1) | collective-permute-done | bytes 262176 | tf_op jit(solution)/shard_map/ppermute | solution.py:394
  50.9 1.5 %shard_map.82 = bf16[8,64,384]{2,1,0:T(8,128)(2,1)S(1)} custom-call(bf16[8,128,256]{2,1,0:T(8,128)(2,1)S(1)} %all_to_all.15.after.own_ref, bf16[8,64,256]{2,1,0:T(8,128)(2,1)S(1)} %collective-permute-done.other_ref, bf16[8,64,256]{2,1,0:T(8,128)(2,1)S(1)} %collective-permute-done.1.query_ref, bf16[8,64,128]{2,1,0:T(8,128)(2,1)S(1)} %get-tuple-element.20.dq_ref, ...), custom_call_target="tpu_custom_call" | custom-call | flops 536870912 | tf_op jit(solution)/shard_map/pallas_call | solution.py:408
  52.4 14.3 %all_to_all.16.got_ref = bf16[8,64,384]{2,1,0:T(8,128)(2,1)S(1)} all-to-all(bf16[8,64,384]{2,1,0:T(8,128)(2,1)S(1)} %shard_map.82), channel_id=1, replica_groups={{0,2,4,6,8,10,12,14},{1,3,5,7,9,11,13,15},{16,18,20,22,24,26,28,30},{17..., dimensions={0} | all-to-all | bytes 786432 | tf_op jit(solution)/shard_map/all_to_all | solution.py:416
  66.7 1.5 %shard_map.83 = (bf16[256,1536]{1,0:T(8,128)(2,1)}, bf16[256,1536]{1,0:T(8,128)(2,1)}, bf16[256,1536]{1,0:T(8,128)(2,1)}) custom-call(s32[8,256]{1,0:T(8,128)S(1)} %get-tuple-element.14.off_ref, bf16[8,64,384]{2,1,0:T(8,128)(2,1)S(1)} %all_to_all.16.got_ref, ...), custom_call_target="tpu_custom_call", output_to_operand_aliasing={{0}: (2, {}), {1}: (3, {}), {2}: (4, {})} | custom-call | tf_op jit(solution)/shard_map/pallas_call | solution.py:418
  (1 shorter events, 0.0 us)
Async XLA Ops:
  2.6 10.7 %all-to-all-start = ((bf16[16,16,256]{2,1,0:T(8,128)(2,1)}), bf16[16,16,256]{2,1,0:T(8,128)(2,1)S(1)}, u32[]{:S(2)}, u32[]{:S(2)}) async-start(bf16[16,16,256]{2,1,0:T(8,128)(2,1)} %get-tuple-element.15), calls=%async_computation | async-start | bytes 262144 | tf_op jit(solution)/shard_map/all_to_all | solution.py:366
  40.0 8.0 %collective-permute-start = (bf16[8,64,256]{2,1,0:T(8,128)(2,1)S(1)}, bf16[8,64,256]{2,1,0:T(8,128)(2,1)S(1)}, u32[]{:S(2)}, u32[]{:S(2)}) collective-permute-start(bf16[8,64,256]{2,1,0:T(8,128)(2,1)S(1)} %get-tuple-element.26), channel_id=1, source_target_pairs={{0,1},{1,0},{2,3},{3,2},{4,5},{5,4},{6,7},{7,6},{8,9},{9,8},{10,11... | collective-permute-start | bytes 786440 | tf_op jit(solution)/shard_map/ppermute | solution.py:393
  43.0 7.9 %collective-permute-start.1 = (bf16[8,64,256]{2,1,0:T(8,128)(2,1)S(1)}, bf16[8,64,256]{2,1,0:T(8,128)(2,1)S(1)}, u32[]{:S(2)}, u32[]{:S(2)}) collective-permute-start(bf16[8,64,256]{2,1,0:T(8,128)(2,1)S(1)} %get-tuple-element.25), channel_id=1, source_target_pairs={{0,1},{1,0},{2,3},{3,2},{4,5},{5,4},{6,7},{7,6},{8,9},{9,8},{10,11... | collective-permute-start | bytes 786440 | tf_op jit(solution)/shard_map/ppermute | solution.py:394

commit v9 on v8

--- a/solution.py
+++ b/solution.py
@@ -23,7 +23,8 @@
 SLOTS = 8
 HALVES = 2
 HALF_KEYS = SLOTS * MID_ROWS
-ALONG_Z = [[HALVES * z + half for z in range(SLOTS)] for half in range(HALVES)]
+Z_ORDER = (5, 6, 7, 3, 4, 1, 2, 0)
+ALONG_Z = [[HALVES * z + half for z in Z_ORDER] for half in range(HALVES)]
 ACROSS_Y = [(member, member ^ 1) for member in range(HALVES * SLOTS)]
 SCALE = 1.0 / math.sqrt(HEAD_DIM)
 EARLY_NEAR = (range(3), range(0))
@@ -209,7 +210,8 @@
 
 
 def slot():
-    return lax.div(lax.axis_index("inner"), HALVES)
+    z = lax.div(lax.axis_index("inner"), HALVES)
+    return sum(jnp.where(z == place, at, 0) for at, place in enumerate(Z_ORDER))
 
 
 def attend_wide(own_ref, other_ref, out_ref):

time: 69.2 us -> 65.1 us (0.941)
  blocking collectives: 37 us -> 34.2 us
  Pallas kernels: 15.4 us -> 13.3 us
  waiting for transfers between devices: 5.63 us -> 6.8 us
    all_to_all x1, blocking collectives: 22.7 us -> 19.4 us  [body(): own = lax.all_to_all(packed, 'inner', 0, 0, axis_index_groups=ALONG_Z)]
    pallas_call x1, Pallas kernels: 1.52 us -> 0.01 us  [body(): pl.pallas_call(other_work_kernel, out_shape=shape(SLOTS, MID_ROWS, 3 * HE...]
    ppermute x1, waiting for transfers between devices: 1.86 us -> 2.59 us  [body(): other = lax.ppermute(own[:, 0:64, :], 'inner', ACROSS_Y)]
where the time goes in v9:
time: 65.1 us; the launch traced here: 64.5 us
  blocking collectives  34.2 us (53%)
  Pallas kernels  13.3 us (20%)
  starting transfers between devices  9.49 us (15%)
  waiting for transfers between devices  6.8 us (10%)
  between operations  0.68 us (1%)
    all_to_all x1, blocking collectives, body(): own = lax.all_to_all(packed, 'inner', 0, 0, axis_index_groups=ALONG_Z)  19.4 us
    all_to_all x1, blocking collectives, body(): returned = lax.all_to_all(results, 'inner', 0, 0, axis_index_groups=ALONG_Z)  14.8 us
    pallas_call x2, Pallas kernels, near_heads(): pl.pallas_call(functools.partial(near_kernel, heads_of_core), out_shape=[...  6.27 us
    all_to_all x1, starting transfers between devices, body(): wide_got = lax.all_to_all(wide_send, 'outer', 0, 0)  5.87 us
    ppermute x1, starting transfers between devices, body(): other = lax.ppermute(own[:, 0:64, :], 'inner', ACROSS_Y)  2.99 us
    all_to_all x1, waiting for transfers between devices, body(): wide_got = lax.all_to_all(wide_send, 'outer', 0, 0)  2.81 us
    ppermute x1, waiting for transfers between devices, body(): other = lax.ppermute(own[:, 0:64, :], 'inner', ACROSS_Y)  2.59 us
    pallas_call x1, Pallas kernels, body(): pl.pallas_call(mid_pack_kernel, out_shape=shape(SLOTS, 128, 256), in_spec...  2.02 us
  transfers between devices with their start and end apart: 3, of which 3 were waited for; matrix products, arithmetic and copies ran while one was open for 0% of the time, Pallas kernels for 9%

profile of v9, /device:TPU:2, one launch (start us, length us, event | category | flops | bytes accessed | tf_op | source)
XLA Modules:
  0.0 64.5 jit_solution(10509608653082637889)
XLA Ops:
  0.6 2.0 %shard_map.76 = (bf16[16,16,256]{2,1,0:T(8,128)(2,1)}, s32[8,256]{1,0:T(8,128)S(1)}) custom-call(s32[8]{0:T(128)} %off_hbm.1, bf16[256,1536]{1,0:T(8,128)(2,1)} %q_hbm.7, bf16[256,1536]{1,0:T(8,128)(2,1)} %k_hbm.7, bf16[256,1536]{1,0:T(8,128)(2,1)} %v_hbm.7, bf16[256,1536]{1,0:T(8,128)(2,1)} %g_hbm.7), custom_call_target="tpu_custom_call" | custom-call | tf_op jit(solution)/shard_map/pallas_call | solution.py:355
  2.6 5.9 %all-to-all-start = ((bf16[16,16,256]{2,1,0:T(8,128)(2,1)}), bf16[16,16,256]{2,1,0:T(8,128)(2,1)S(1)}, u32[]{:S(2)}, u32[]{:S(2)}) async-start(bf16[16,16,256]{2,1,0:T(8,128)(2,1)} %get-tuple-element.15), calls=%async_computation | async-start | bytes 262144 | tf_op jit(solution)/shard_map/all_to_all | solution.py:368
  8.5 2.0 %shard_map.77.packed = bf16[8,128,256]{2,1,0:T(8,128)(2,1)S(1)} custom-call(s32[8,256]{1,0:T(8,128)S(1)} %get-tuple-element.14.off_ref, bf16[256,1536]{1,0:T(8,128)(2,1)} %q_hbm.7, bf16[256,1536]{1,0:T(8,128)(2,1)} %k_hbm.7, bf16[256,1536]{1,0:T(8,128)(2,1)} %v_hbm.7, bf16[256,1536]{1,0:T(8,128)(2,1)} %g_hbm.7), custom_call_target="tpu_custom_call" | custom-call | flops 83886080 | bytes 1310720 | tf_op jit(solution)/shard_map/pallas_call | solution.py:369
  10.5 2.8 %all-to-all-done.after.got_ref = bf16[16,16,256]{2,1,0:T(8,128)(2,1)S(1)} async-done(((bf16[16,16,256]{2,1,0:T(8,128)(2,1)}), bf16[16,16,256]{2,1,0:T(8,128)(2,1)S(1)}, u32[]{:S(2)}, u32[]{:S(2)}) %all-to-all-start) | async-done | bytes 131104 | tf_op jit(solution)/shard_map/all_to_all | solution.py:368
  13.3 3.8 %shard_map.78 = (bf16[256,1536]{1,0:T(8,128)(2,1)}, bf16[256,1536]{1,0:T(8,128)(2,1)}, bf16[256,1536]{1,0:T(8,128)(2,1)}) custom-call(bf16[16,16,256]{2,1,0:T(8,128)(2,1)S(1)} %all-to-all-done.after.got_ref, bf16[256,1536]{1,0:T(8,128)(2,1)} %q_hbm.7, bf16[256,1536]{1,0:T(8,128)(2,1)} %k_hbm.7, bf16[256,1536]{1,0:T(8,128)(2,1)} %v_hbm.7, bf16[256,1536]{1,0:T(8,128)(2,1)} %g_hbm.7), custom_call_target="tpu_custom_call" | custom-call | flops 335544320 | bytes 1835008 | tf_op jit(solution)/shard_map/pallas_call | solution.py:191
  17.1 0.2 shard_map.79
  17.3 19.4 %all_to_all.15.after.own_ref = bf16[8,128,256]{2,1,0:T(8,128)(2,1)S(1)} all-to-all(bf16[8,128,256]{2,1,0:T(8,128)(2,1)S(1)} %shard_map.79), channel_id=1, replica_groups={{10,12,14,6,8,2,4,0},{11,13,15,7,9,3,5,1},{26,28,30,22,24,18,20,16},{27..., dimensions={0} | all-to-all | bytes 1048576 | tf_op jit(solution)/shard_map/all_to_all | solution.py:394
  36.7 3.0 %collective-permute-start = (bf16[8,64,256]{2,1,0:T(8,128)(2,1)S(1)}, bf16[8,64,256]{2,1,0:T(8,128)(2,1)S(1)}, u32[]{:S(2)}, u32[]{:S(2)}) collective-permute-start(bf16[8,64,256]{2,1,0:T(8,128)(2,1)S(1)} %get-tuple-element.26), channel_id=1, source_target_pairs={{0,1},{1,0},{2,3},{3,2},{4,5},{5,4},{6,7},{7,6},{8,9},{9,8},{10,11... | collective-permute-start | bytes 786440 | tf_op jit(solution)/shard_map/ppermute | solution.py:395
  39.7 0.6 collective-permute-start.1
  40.4 2.5 %shard_map.80 = (bf16[256,1536]{1,0:T(8,128)(2,1)}, bf16[256,1536]{1,0:T(8,128)(2,1)}, bf16[256,1536]{1,0:T(8,128)(2,1)}) custom-call(bf16[8,128,256]{2,1,0:T(8,128)(2,1)S(1)} %all_to_all.15.after.own_ref, bf16[256,1536]{1,0:T(8,128)(2,1)} %q_hbm.7, bf16[256,1536]{1,0:T(8,128)(2,1)} %k_hbm.7, ...), custom_call_target="tpu_custom_call", output_to_operand_aliasing={{0}: (5, {}), {1}: (6, {}), {2}: (7, {})} | custom-call | flops 335544320 | bytes 1835008 | tf_op jit(solution)/shard_map/pallas_call | solution.py:191
  42.8 2.6 %collective-permute-done.other_ref = bf16[8,64,256]{2,1,0:T(8,128)(2,1)S(1)} collective-permute-done((bf16[8,64,256]{2,1,0:T(8,128)(2,1)S(1)}, bf16[8,64,256]{2,1,0:T(8,128)(2,1)S(1)}, u32[]{:S(2)}, u32[]{:S(2)}) %collective-permute-start) | collective-permute-done | bytes 262176 | tf_op jit(solution)/shard_map/ppermute | solution.py:395
  45.4 1.4 %shard_map.81 = (bf16[8,64,128]{2,1,0:T(8,128)(2,1)S(1)}, f32[512,256]{1,0:T(8,128)S(1)}, bf16[8,16,128]{2,1,0:T(8,128)(2,1)S(1)}) custom-call(bf16[8,128,256]{2,1,0:T(8,128)(2,1)S(1)} %all_to_all.15.after.own_ref, bf16[8,64,256]{2,1,0:T(8,128)(2,1)S(1)} %collective-permute-done.other_ref, bf16[256,1536]{1,0:T(8,128)(2,1)} %get-tuple-element.19.after.nq), custom_call_target="tpu_custom_call" | custom-call | flops 671088640 | tf_op jit(solution)/shard_map/pallas_call | solution.py:398
  46.8 1.4 %collective-permute-done.1.query_ref = bf16[8,64,256]{2,1,0:T(8,128)(2,1)S(1)} collective-permute-done((bf16[8,64,256]{2,1,0:T(8,128)(2,1)S(1)}, bf16[8,64,256]{2,1,0:T(8,128)(2,1)S(1)}, u32[]{:S(2)}, u32[]{:S(2)}) %collective-permute-start.1) | collective-permute-done | bytes 262176 | tf_op jit(solution)/shard_map/ppermute | solution.py:396
  48.2 14.8 %all_to_all.16.got_ref = bf16[8,64,384]{2,1,0:T(8,128)(2,1)S(1)} all-to-all(bf16[8,64,384]{2,1,0:T(8,128)(2,1)S(1)} %shard_map.82), channel_id=1, replica_groups={{10,12,14,6,8,2,4,0},{11,13,15,7,9,3,5,1},{26,28,30,22,24,18,20,16},{27..., dimensions={0} | all-to-all | bytes 786432 | tf_op jit(solution)/shard_map/all_to_all | solution.py:418
  63.0 1.5 %shard_map.83 = (bf16[256,1536]{1,0:T(8,128)(2,1)}, bf16[256,1536]{1,0:T(8,128)(2,1)}, bf16[256,1536]{1,0:T(8,128)(2,1)}) custom-call(s32[8,256]{1,0:T(8,128)S(1)} %get-tuple-element.14.off_ref, bf16[8,64,384]{2,1,0:T(8,128)(2,1)S(1)} %all_to_all.16.got_ref, ...), custom_call_target="tpu_custom_call", output_to_operand_aliasing={{0}: (2, {}), {1}: (3, {}), {2}: (4, {})} | custom-call | tf_op jit(solution)/shard_map/pallas_call | solution.py:420
  (2 shorter events, 0.0 us)
Async XLA Ops:
  2.6 10.7 %all-to-all-start = ((bf16[16,16,256]{2,1,0:T(8,128)(2,1)}), bf16[16,16,256]{2,1,0:T(8,128)(2,1)S(1)}, u32[]{:S(2)}, u32[]{:S(2)}) async-start(bf16[16,16,256]{2,1,0:T(8,128)(2,1)} %get-tuple-element.15), calls=%async_computation | async-start | bytes 262144 | tf_op jit(solution)/shard_map/all_to_all | solution.py:368
  36.7 8.7 %collective-permute-start = (bf16[8,64,256]{2,1,0:T(8,128)(2,1)S(1)}, bf16[8,64,256]{2,1,0:T(8,128)(2,1)S(1)}, u32[]{:S(2)}, u32[]{:S(2)}) collective-permute-start(bf16[8,64,256]{2,1,0:T(8,128)(2,1)S(1)} %get-tuple-element.26), channel_id=1, source_target_pairs={{0,1},{1,0},{2,3},{3,2},{4,5},{5,4},{6,7},{7,6},{8,9},{9,8},{10,11... | collective-permute-start | bytes 786440 | tf_op jit(solution)/shard_map/ppermute | solution.py:395
  39.7 8.5 %collective-permute-start.1 = (bf16[8,64,256]{2,1,0:T(8,128)(2,1)S(1)}, bf16[8,64,256]{2,1,0:T(8,128)(2,1)S(1)}, u32[]{:S(2)}, u32[]{:S(2)}) collective-permute-start(bf16[8,64,256]{2,1,0:T(8,128)(2,1)S(1)} %get-tuple-element.25), channel_id=1, source_target_pairs={{0,1},{1,0},{2,3},{3,2},{4,5},{5,4},{6,7},{7,6},{8,9},{9,8},{10,11... | collective-permute-start | bytes 786440 | tf_op jit(solution)/shard_map/ppermute | solution.py:396

commit v10 on v8

--- a/solution.py
+++ b/solution.py
@@ -23,7 +23,12 @@
 SLOTS = 8
 HALVES = 2
 HALF_KEYS = SLOTS * MID_ROWS
-ALONG_Z = [[HALVES * z + half for z in range(SLOTS)] for half in range(HALVES)]
+Z_IN = (5, 6, 7, 3, 4, 1, 2, 0)
+Z_OUT = (5, 6, 7, 3, 4, 1, 2, 0)
+OUTER_ORDER = tuple(range(OUTERS - 1, -1, -1))
+ALONG_Z_IN = [[HALVES * z + half for z in Z_IN] for half in range(HALVES)]
+ALONG_Z_OUT = [[HALVES * z + half for z in Z_OUT] for half in range(HALVES)]
+OUT_FROM_IN = [Z_IN.index(z) for z in Z_OUT]
 ACROSS_Y = [(member, member ^ 1) for member in range(HALVES * SLOTS)]
 SCALE = 1.0 / math.sqrt(HEAD_DIM)
 EARLY_NEAR = (range(3), range(0))
@@ -208,8 +213,12 @@
     )(after, *arrays, *previous)
 
 
+def place_in(order, index):
+    return sum(jnp.where(index == member, at, 0) for at, member in enumerate(order))
+
+
 def slot():
-    return lax.div(lax.axis_index("inner"), HALVES)
+    return place_in(Z_IN, lax.div(lax.axis_index("inner"), HALVES))
 
 
 def attend_wide(own_ref, other_ref, out_ref):
@@ -217,7 +226,7 @@
     kv = [ref[:, 0:32, :].reshape(wide_rows, 2 * HEAD_DIM) for ref in (own_ref, other_ref)]
     qg = [ref[:, 32:64, :].reshape(wide_rows, 2 * HEAD_DIM) for ref in (own_ref, other_ref)]
     row, column = iota2(16, wide_rows)
-    source = 32 * (row // 2) + 2 * lax.axis_index("outer") + row % 2
+    source = 32 * (row // 2) + 2 * place_in(OUTER_ORDER, lax.axis_index("outer")) + row % 2
     pick = one_hot(column == source)
     own_kv, own_qg = dot(pick, kv[0]).astype(BF16), dot(pick, qg[0]).astype(BF16)
     kv, qg = jnp.concatenate(kv, axis=0), jnp.concatenate(qg, axis=0)
@@ -281,14 +290,16 @@
         weights, score_gradients = scaled_weights(parts, query, gradient)
         dk = dkv_ref[:, :HEAD_DIM] + dot(score_gradients, query)
         dv = dkv_ref[:, HEAD_DIM:] + dot(weights, gradient)
-        out_ref[:, :, :HEAD_DIM] = dq_ref[...]
-        for at, sums in ((HEAD_DIM, dk), (2 * HEAD_DIM, dv)):
-            sums = sums.astype(BF16).reshape(SLOTS, MID_ROWS, HEAD_DIM)
-            out_ref[:, :, at : at + HEAD_DIM] = sums
+        dk, dv = (sums.astype(BF16).reshape(SLOTS, MID_ROWS, HEAD_DIM) for sums in (dk, dv))
+        for at, member in enumerate(OUT_FROM_IN):
+            out_ref[at, :, :HEAD_DIM] = dq_ref[member]
+            out_ref[at, :, HEAD_DIM : 2 * HEAD_DIM] = dk[member]
+            out_ref[at, :, 2 * HEAD_DIM :] = dv[member]
 
     @pl.when(slot() >= H_MID)
     def wide():
-        out_ref[:, 0:16, :HEAD_DIM] = wide_ref[...]
+        for at, member in enumerate(OUT_FROM_IN):
+            out_ref[at, 0:16, :HEAD_DIM] = wide_ref[member]
 
 
 def assemble_kernel(off_ref, got_ref, nq, nk, nv, dq_hbm, dk_hbm, dv_hbm, held, sems):
@@ -308,7 +319,7 @@
     row, unused = iota2(TOK, HEAD_DIM)
     for head in range(H_MID, H_MID + H_WIDE):
         offset = off_ref[head : head + 1, :HEAD_DIM]
-        rows = got_ref[head, 0:16, :HEAD_DIM].astype(F32)
+        rows = got_ref[OUT_FROM_IN.index(head), 0:16, :HEAD_DIM].astype(F32)
         first, second = row == offset, row == offset + R_WIDE
         for which in range(3):
             spread = jnp.where(first, rows[2 * which : 2 * which + 1], 0.0)
@@ -316,7 +327,7 @@
     row, column = iota2(TOK, MID_ROWS)
     for head in range(H_MID):
         place = one_hot(row - R_MID * column == off_ref[head : head + 1, :1])
-        spread = dot(place, got_ref[head])
+        spread = dot(place, got_ref[OUT_FROM_IN.index(head)])
         for which in range(3):
             send(which, head, spread[:, which * HEAD_DIM : (which + 1) * HEAD_DIM])
     for copy in copies:
@@ -363,7 +374,7 @@
         ],
         compiler_params=params(8),
     )(in_hbm(offsets), *arrays)
-    wide_got = lax.all_to_all(wide_send, "outer", 0, 0)
+    wide_got = lax.all_to_all(wide_send, "outer", 0, 0, axis_index_groups=[list(OUTER_ORDER)])
     packed = pl.pallas_call(
         mid_pack_kernel,
         out_shape=shape(SLOTS, 128, 256),
@@ -389,7 +400,7 @@
         input_output_aliases={1: 0},
         compiler_params=params(8),
     )(wide_got, packed, in_hbm(near[0]))
-    own = lax.all_to_all(packed, "inner", 0, 0, axis_index_groups=ALONG_Z)
+    own = lax.all_to_all(packed, "inner", 0, 0, axis_index_groups=ALONG_Z_IN)
     other = lax.ppermute(own[:, 0:64, :], "inner", ACROSS_Y)
     other_queries = lax.ppermute(own[:, 64:128, :], "inner", ACROSS_Y)
     near = near_heads(LATE_NEAR, own, arrays, near)
@@ -413,7 +424,7 @@
         cost_estimate=work_cost(4),
         compiler_params=params(24),
     )(own, other, other_queries, dq, own_sums, wide_rows)
-    returned = lax.all_to_all(results, "inner", 0, 0, axis_index_groups=ALONG_Z)
+    returned = lax.all_to_all(results, "inner", 0, 0, axis_index_groups=ALONG_Z_OUT)
     return tuple(
         pl.pallas_call(
             assemble_kernel,

time: 69.2 us -> 63.6 us (0.919)
  blocking collectives: 37 us -> 33.3 us
  Pallas kernels: 15.4 us -> 13.3 us
    all_to_all x2, blocking collectives: 37 us -> 33.3 us  [the longest x1 19 us: body(): own = lax.all_to_all(packed, 'inner', 0, 0, axis_index_groups=ALONG_Z_IN)]
    pallas_call x1, Pallas kernels: 1.52 us -> 0.01 us  [body(): pl.pallas_call(other_work_kernel, out_shape=shape(SLOTS, MID_ROWS, 3 * HE...]
    all_to_all x1, waiting for transfers between devices: 2.81 us -> 1.33 us  [body(): lax.all_to_all(wide_send, 'outer', 0, 0, axis_index_groups=[list(OUTER_OR...]
    ppermute x1, waiting for transfers between devices: 1.86 us -> 2.59 us  [body(): other = lax.ppermute(own[:, 0:64, :], 'inner', ACROSS_Y)]
where the time goes in v10:
time: 63.6 us; the launch traced here: 62.6 us
  blocking collectives  33.3 us (52%)
  Pallas kernels  13.3 us (21%)
  starting transfers between devices  9.91 us (16%)
  waiting for transfers between devices  5.33 us (8%)
  between operations  0.68 us (1%)
    all_to_all x1, blocking collectives, body(): own = lax.all_to_all(packed, 'inner', 0, 0, axis_index_groups=ALONG_Z_IN)  19 us
    all_to_all x1, blocking collectives, body(): lax.all_to_all(results, 'inner', 0, 0, axis_index_groups=ALONG_Z_OUT)  14.3 us
    all_to_all x1, starting transfers between devices, body(): lax.all_to_all(wide_send, 'outer', 0, 0, axis_index_groups=[list(OUTER_OR...  6.3 us
    pallas_call x2, Pallas kernels, near_heads(): pl.pallas_call(functools.partial(near_kernel, heads_of_core), out_shape=[...  6.26 us
    ppermute x1, starting transfers between devices, body(): other = lax.ppermute(own[:, 0:64, :], 'inner', ACROSS_Y)  2.99 us
    ppermute x1, waiting for transfers between devices, body(): other = lax.ppermute(own[:, 0:64, :], 'inner', ACROSS_Y)  2.59 us
    pallas_call x1, Pallas kernels, body(): pl.pallas_call(mid_pack_kernel, out_shape=shape(SLOTS, 128, 256), in_spec...  2.02 us
    pallas_call x1, Pallas kernels, body(): pl.pallas_call(wide_kernel, out_shape=[shape(OUTERS, 16, 256), shape(head...  1.98 us
  transfers between devices with their start and end apart: 3, of which 3 were waited for; matrix products, arithmetic and copies ran while one was open for 0% of the time, Pallas kernels for 9%

profile of v10, /device:TPU:2, one launch (start us, length us, event | category | flops | bytes accessed | tf_op | source)
XLA Modules:
  0.0 62.6 jit_solution(7924588422786635415)
XLA Ops:
  0.6 2.0 %shard_map.76 = (bf16[16,16,256]{2,1,0:T(8,128)(2,1)}, s32[8,256]{1,0:T(8,128)S(1)}) custom-call(s32[8]{0:T(128)} %off_hbm.1, bf16[256,1536]{1,0:T(8,128)(2,1)} %q_hbm.7, bf16[256,1536]{1,0:T(8,128)(2,1)} %k_hbm.7, bf16[256,1536]{1,0:T(8,128)(2,1)} %v_hbm.7, bf16[256,1536]{1,0:T(8,128)(2,1)} %g_hbm.7), custom_call_target="tpu_custom_call" | custom-call | tf_op jit(solution)/shard_map/pallas_call | solution.py:364
  2.6 6.3 %all-to-all-start = ((bf16[16,16,256]{2,1,0:T(8,128)(2,1)}), bf16[16,16,256]{2,1,0:T(8,128)(2,1)S(1)}, u32[]{:S(2)}, u32[]{:S(2)}) async-start(bf16[16,16,256]{2,1,0:T(8,128)(2,1)} %get-tuple-element.15), calls=%async_computation | async-start | bytes 262144 | tf_op jit(solution)/shard_map/all_to_all | solution.py:377
  8.9 2.0 %shard_map.77.packed = bf16[8,128,256]{2,1,0:T(8,128)(2,1)S(1)} custom-call(s32[8,256]{1,0:T(8,128)S(1)} %get-tuple-element.14.off_ref, bf16[256,1536]{1,0:T(8,128)(2,1)} %q_hbm.7, bf16[256,1536]{1,0:T(8,128)(2,1)} %k_hbm.7, bf16[256,1536]{1,0:T(8,128)(2,1)} %v_hbm.7, bf16[256,1536]{1,0:T(8,128)(2,1)} %g_hbm.7), custom_call_target="tpu_custom_call" | custom-call | flops 83886080 | bytes 1310720 | tf_op jit(solution)/shard_map/pallas_call | solution.py:378
  10.9 1.3 %all-to-all-done.after.got_ref = bf16[16,16,256]{2,1,0:T(8,128)(2,1)S(1)} async-done(((bf16[16,16,256]{2,1,0:T(8,128)(2,1)}), bf16[16,16,256]{2,1,0:T(8,128)(2,1)S(1)}, u32[]{:S(2)}, u32[]{:S(2)}) %all-to-all-start) | async-done | bytes 131104 | tf_op jit(solution)/shard_map/all_to_all | solution.py:377
  12.3 3.8 %shard_map.78 = (bf16[256,1536]{1,0:T(8,128)(2,1)}, bf16[256,1536]{1,0:T(8,128)(2,1)}, bf16[256,1536]{1,0:T(8,128)(2,1)}) custom-call(bf16[16,16,256]{2,1,0:T(8,128)(2,1)S(1)} %all-to-all-done.after.got_ref, bf16[256,1536]{1,0:T(8,128)(2,1)} %q_hbm.7, bf16[256,1536]{1,0:T(8,128)(2,1)} %k_hbm.7, bf16[256,1536]{1,0:T(8,128)(2,1)} %v_hbm.7, bf16[256,1536]{1,0:T(8,128)(2,1)} %g_hbm.7), custom_call_target="tpu_custom_call" | custom-call | flops 335544320 | bytes 1835008 | tf_op jit(solution)/shard_map/pallas_call | solution.py:195
  16.1 0.2 shard_map.79
  16.3 19.0 %all_to_all.15.after.own_ref = bf16[8,128,256]{2,1,0:T(8,128)(2,1)S(1)} all-to-all(bf16[8,128,256]{2,1,0:T(8,128)(2,1)S(1)} %shard_map.79), channel_id=1, replica_groups={{10,12,14,6,8,2,4,0},{11,13,15,7,9,3,5,1},{26,28,30,22,24,18,20,16},{27..., dimensions={0} | all-to-all | bytes 1048576 | tf_op jit(solution)/shard_map/all_to_all | solution.py:403
  35.3 3.0 %collective-permute-start = (bf16[8,64,256]{2,1,0:T(8,128)(2,1)S(1)}, bf16[8,64,256]{2,1,0:T(8,128)(2,1)S(1)}, u32[]{:S(2)}, u32[]{:S(2)}) collective-permute-start(bf16[8,64,256]{2,1,0:T(8,128)(2,1)S(1)} %get-tuple-element.26), channel_id=1, source_target_pairs={{0,1},{1,0},{2,3},{3,2},{4,5},{5,4},{6,7},{7,6},{8,9},{9,8},{10,11... | collective-permute-start | bytes 786440 | tf_op jit(solution)/shard_map/ppermute | solution.py:404
  38.3 0.6 %collective-permute-start.1 = (bf16[8,64,256]{2,1,0:T(8,128)(2,1)S(1)}, bf16[8,64,256]{2,1,0:T(8,128)(2,1)S(1)}, u32[]{:S(2)}, u32[]{:S(2)}) collective-permute-start(bf16[8,64,256]{2,1,0:T(8,128)(2,1)S(1)} %get-tuple-element.25), channel_id=1, source_target_pairs={{0,1},{1,0},{2,3},{3,2},{4,5},{5,4},{6,7},{7,6},{8,9},{9,8},{10,11... | collective-permute-start | bytes 786440 | tf_op jit(solution)/shard_map/ppermute | solution.py:405
  38.9 2.5 %shard_map.80 = (bf16[256,1536]{1,0:T(8,128)(2,1)}, bf16[256,1536]{1,0:T(8,128)(2,1)}, bf16[256,1536]{1,0:T(8,128)(2,1)}) custom-call(bf16[8,128,256]{2,1,0:T(8,128)(2,1)S(1)} %all_to_all.15.after.own_ref, bf16[256,1536]{1,0:T(8,128)(2,1)} %q_hbm.7, bf16[256,1536]{1,0:T(8,128)(2,1)} %k_hbm.7, ...), custom_call_target="tpu_custom_call", output_to_operand_aliasing={{0}: (5, {}), {1}: (6, {}), {2}: (7, {})} | custom-call | flops 335544320 | bytes 1835008 | tf_op jit(solution)/shard_map/pallas_call | solution.py:195
  41.4 2.6 %collective-permute-done.other_ref = bf16[8,64,256]{2,1,0:T(8,128)(2,1)S(1)} collective-permute-done((bf16[8,64,256]{2,1,0:T(8,128)(2,1)S(1)}, bf16[8,64,256]{2,1,0:T(8,128)(2,1)S(1)}, u32[]{:S(2)}, u32[]{:S(2)}) %collective-permute-start) | collective-permute-done | bytes 262176 | tf_op jit(solution)/shard_map/ppermute | solution.py:404
  44.0 1.4 %shard_map.81 = (bf16[8,64,128]{2,1,0:T(8,128)(2,1)S(1)}, f32[512,256]{1,0:T(8,128)S(1)}, bf16[8,16,128]{2,1,0:T(8,128)(2,1)S(1)}) custom-call(bf16[8,128,256]{2,1,0:T(8,128)(2,1)S(1)} %all_to_all.15.after.own_ref, bf16[8,64,256]{2,1,0:T(8,128)(2,1)S(1)} %collective-permute-done.other_ref, bf16[256,1536]{1,0:T(8,128)(2,1)} %get-tuple-element.19.after.nq), custom_call_target="tpu_custom_call" | custom-call | flops 671088640 | tf_op jit(solution)/shard_map/pallas_call | solution.py:407
  45.4 1.4 %collective-permute-done.1.query_ref = bf16[8,64,256]{2,1,0:T(8,128)(2,1)S(1)} collective-permute-done((bf16[8,64,256]{2,1,0:T(8,128)(2,1)S(1)}, bf16[8,64,256]{2,1,0:T(8,128)(2,1)S(1)}, u32[]{:S(2)}, u32[]{:S(2)}) %collective-permute-start.1) | collective-permute-done | bytes 262176 | tf_op jit(solution)/shard_map/ppermute | solution.py:405
  46.8 14.3 %all_to_all.16.got_ref = bf16[8,64,384]{2,1,0:T(8,128)(2,1)S(1)} all-to-all(bf16[8,64,384]{2,1,0:T(8,128)(2,1)S(1)} %shard_map.82), channel_id=1, replica_groups={{10,12,14,6,8,2,4,0},{11,13,15,7,9,3,5,1},{26,28,30,22,24,18,20,16},{27..., dimensions={0} | all-to-all | bytes 786432 | tf_op jit(solution)/shard_map/all_to_all | solution.py:427
  61.1 1.5 %shard_map.83 = (bf16[256,1536]{1,0:T(8,128)(2,1)}, bf16[256,1536]{1,0:T(8,128)(2,1)}, bf16[256,1536]{1,0:T(8,128)(2,1)}) custom-call(s32[8,256]{1,0:T(8,128)S(1)} %get-tuple-element.14.off_ref, bf16[8,64,384]{2,1,0:T(8,128)(2,1)S(1)} %all_to_all.16.got_ref, ...), custom_call_target="tpu_custom_call", output_to_operand_aliasing={{0}: (2, {}), {1}: (3, {}), {2}: (4, {})} | custom-call | tf_op jit(solution)/shard_map/pallas_call | solution.py:429
  (2 shorter events, 0.0 us)
Async XLA Ops:
  2.6 9.7 %all-to-all-start = ((bf16[16,16,256]{2,1,0:T(8,128)(2,1)}), bf16[16,16,256]{2,1,0:T(8,128)(2,1)S(1)}, u32[]{:S(2)}, u32[]{:S(2)}) async-start(bf16[16,16,256]{2,1,0:T(8,128)(2,1)} %get-tuple-element.15), calls=%async_computation | async-start | bytes 262144 | tf_op jit(solution)/shard_map/all_to_all | solution.py:377
  35.3 8.7 %collective-permute-start = (bf16[8,64,256]{2,1,0:T(8,128)(2,1)S(1)}, bf16[8,64,256]{2,1,0:T(8,128)(2,1)S(1)}, u32[]{:S(2)}, u32[]{:S(2)}) collective-permute-start(bf16[8,64,256]{2,1,0:T(8,128)(2,1)S(1)} %get-tuple-element.26), channel_id=1, source_target_pairs={{0,1},{1,0},{2,3},{3,2},{4,5},{5,4},{6,7},{7,6},{8,9},{9,8},{10,11... | collective-permute-start | bytes 786440 | tf_op jit(solution)/shard_map/ppermute | solution.py:404
  38.3 8.5 %collective-permute-start.1 = (bf16[8,64,256]{2,1,0:T(8,128)(2,1)S(1)}, bf16[8,64,256]{2,1,0:T(8,128)(2,1)S(1)}, u32[]{:S(2)}, u32[]{:S(2)}) collective-permute-start(bf16[8,64,256]{2,1,0:T(8,128)(2,1)S(1)} %get-tuple-element.25), channel_id=1, source_target_pairs={{0,1},{1,0},{2,3},{3,2},{4,5},{5,4},{6,7},{7,6},{8,9},{9,8},{10,11... | collective-permute-start | bytes 786440 | tf_op jit(solution)/shard_map/ppermute | solution.py:405

commit v11 on v10

--- a/solution.py
+++ b/solution.py
@@ -23,8 +23,8 @@
 SLOTS = 8
 HALVES = 2
 HALF_KEYS = SLOTS * MID_ROWS
-Z_IN = (5, 6, 7, 3, 4, 1, 2, 0)
-Z_OUT = (5, 6, 7, 3, 4, 1, 2, 0)
+Z_IN = (4, 5, 6, 2, 3, 0, 1, 7)
+Z_OUT = (4, 5, 6, 2, 3, 0, 1, 7)
 OUTER_ORDER = tuple(range(OUTERS - 1, -1, -1))
 ALONG_Z_IN = [[HALVES * z + half for z in Z_IN] for half in range(HALVES)]
 ALONG_Z_OUT = [[HALVES * z + half for z in Z_OUT] for half in range(HALVES)]

time: 63.6 us -> 63.4 us (level)
    all_to_all x1, blocking collectives: 19 us -> 18.1 us  [body(): own = lax.all_to_all(packed, 'inner', 0, 0, axis_index_groups=ALONG_Z_IN)]
where the time goes in v11:
time: 63.4 us; the launch traced here: 62.4 us
  blocking collectives  32.8 us (52%)
  Pallas kernels  13.3 us (21%)
  starting transfers between devices  9.91 us (16%)
  waiting for transfers between devices  5.6 us (9%)
  between operations  0.68 us (1%)
    all_to_all x1, blocking collectives, body(): own = lax.all_to_all(packed, 'inner', 0, 0, axis_index_groups=ALONG_Z_IN)  18.1 us
    all_to_all x1, blocking collectives, body(): lax.all_to_all(results, 'inner', 0, 0, axis_index_groups=ALONG_Z_OUT)  14.7 us
    all_to_all x1, starting transfers between devices, body(): lax.all_to_all(wide_send, 'outer', 0, 0, axis_index_groups=[list(OUTER_OR...  6.3 us
    pallas_call x2, Pallas kernels, near_heads(): pl.pallas_call(functools.partial(near_kernel, heads_of_core), out_shape=[...  6.27 us
    ppermute x1, starting transfers between devices, body(): other = lax.ppermute(own[:, 0:64, :], 'inner', ACROSS_Y)  2.99 us
    ppermute x1, waiting for transfers between devices, body(): other = lax.ppermute(own[:, 0:64, :], 'inner', ACROSS_Y)  2.87 us
    pallas_call x1, Pallas kernels, body(): pl.pallas_call(mid_pack_kernel, out_shape=shape(SLOTS, 128, 256), in_spec...  2.02 us
    pallas_call x1, Pallas kernels, body(): pl.pallas_call(wide_kernel, out_shape=[shape(OUTERS, 16, 256), shape(head...  1.98 us
  transfers between devices with their start and end apart: 3, of which 3 were waited for; matrix products, arithmetic and copies ran while one was open for 0% of the time, Pallas kernels for 9%

profile of v11, /device:TPU:2, one launch (start us, length us, event | category | flops | bytes accessed | tf_op | source)
XLA Modules:
  0.0 62.4 jit_solution(13245476376747531137)
XLA Ops:
  0.6 2.0 %shard_map.76 = (bf16[16,16,256]{2,1,0:T(8,128)(2,1)}, s32[8,256]{1,0:T(8,128)S(1)}) custom-call(s32[8]{0:T(128)} %off_hbm.1, bf16[256,1536]{1,0:T(8,128)(2,1)} %q_hbm.7, bf16[256,1536]{1,0:T(8,128)(2,1)} %k_hbm.7, bf16[256,1536]{1,0:T(8,128)(2,1)} %v_hbm.7, bf16[256,1536]{1,0:T(8,128)(2,1)} %g_hbm.7), custom_call_target="tpu_custom_call" | custom-call | tf_op jit(solution)/shard_map/pallas_call | solution.py:364
  2.6 6.3 %all-to-all-start = ((bf16[16,16,256]{2,1,0:T(8,128)(2,1)}), bf16[16,16,256]{2,1,0:T(8,128)(2,1)S(1)}, u32[]{:S(2)}, u32[]{:S(2)}) async-start(bf16[16,16,256]{2,1,0:T(8,128)(2,1)} %get-tuple-element.15), calls=%async_computation | async-start | bytes 262144 | tf_op jit(solution)/shard_map/all_to_all | solution.py:377
  8.9 2.0 %shard_map.77.packed = bf16[8,128,256]{2,1,0:T(8,128)(2,1)S(1)} custom-call(s32[8,256]{1,0:T(8,128)S(1)} %get-tuple-element.14.off_ref, bf16[256,1536]{1,0:T(8,128)(2,1)} %q_hbm.7, bf16[256,1536]{1,0:T(8,128)(2,1)} %k_hbm.7, bf16[256,1536]{1,0:T(8,128)(2,1)} %v_hbm.7, bf16[256,1536]{1,0:T(8,128)(2,1)} %g_hbm.7), custom_call_target="tpu_custom_call" | custom-call | flops 83886080 | bytes 1310720 | tf_op jit(solution)/shard_map/pallas_call | solution.py:378
  10.9 1.3 %all-to-all-done.after.got_ref = bf16[16,16,256]{2,1,0:T(8,128)(2,1)S(1)} async-done(((bf16[16,16,256]{2,1,0:T(8,128)(2,1)}), bf16[16,16,256]{2,1,0:T(8,128)(2,1)S(1)}, u32[]{:S(2)}, u32[]{:S(2)}) %all-to-all-start) | async-done | bytes 131104 | tf_op jit(solution)/shard_map/all_to_all | solution.py:377
  12.3 3.8 %shard_map.78 = (bf16[256,1536]{1,0:T(8,128)(2,1)}, bf16[256,1536]{1,0:T(8,128)(2,1)}, bf16[256,1536]{1,0:T(8,128)(2,1)}) custom-call(bf16[16,16,256]{2,1,0:T(8,128)(2,1)S(1)} %all-to-all-done.after.got_ref, bf16[256,1536]{1,0:T(8,128)(2,1)} %q_hbm.7, bf16[256,1536]{1,0:T(8,128)(2,1)} %k_hbm.7, bf16[256,1536]{1,0:T(8,128)(2,1)} %v_hbm.7, bf16[256,1536]{1,0:T(8,128)(2,1)} %g_hbm.7), custom_call_target="tpu_custom_call" | custom-call | flops 335544320 | bytes 1835008 | tf_op jit(solution)/shard_map/pallas_call | solution.py:195
  16.1 0.2 shard_map.79
  16.3 18.1 %all_to_all.15.after.own_ref = bf16[8,128,256]{2,1,0:T(8,128)(2,1)S(1)} all-to-all(bf16[8,128,256]{2,1,0:T(8,128)(2,1)S(1)} %shard_map.79), channel_id=1, replica_groups={{8,10,12,4,6,0,2,14},{9,11,13,5,7,1,3,15},{24,26,28,20,22,16,18,30},{25..., dimensions={0} | all-to-all | bytes 1048576 | tf_op jit(solution)/shard_map/all_to_all | solution.py:403
  34.4 3.0 %collective-permute-start = (bf16[8,64,256]{2,1,0:T(8,128)(2,1)S(1)}, bf16[8,64,256]{2,1,0:T(8,128)(2,1)S(1)}, u32[]{:S(2)}, u32[]{:S(2)}) collective-permute-start(bf16[8,64,256]{2,1,0:T(8,128)(2,1)S(1)} %get-tuple-element.26), channel_id=1, source_target_pairs={{0,1},{1,0},{2,3},{3,2},{4,5},{5,4},{6,7},{7,6},{8,9},{9,8},{10,11... | collective-permute-start | bytes 786440 | tf_op jit(solution)/shard_map/ppermute | solution.py:404
  37.4 0.6 %collective-permute-start.1 = (bf16[8,64,256]{2,1,0:T(8,128)(2,1)S(1)}, bf16[8,64,256]{2,1,0:T(8,128)(2,1)S(1)}, u32[]{:S(2)}, u32[]{:S(2)}) collective-permute-start(bf16[8,64,256]{2,1,0:T(8,128)(2,1)S(1)} %get-tuple-element.25), channel_id=1, source_target_pairs={{0,1},{1,0},{2,3},{3,2},{4,5},{5,4},{6,7},{7,6},{8,9},{9,8},{10,11... | collective-permute-start | bytes 786440 | tf_op jit(solution)/shard_map/ppermute | solution.py:405
  38.1 2.5 %shard_map.80 = (bf16[256,1536]{1,0:T(8,128)(2,1)}, bf16[256,1536]{1,0:T(8,128)(2,1)}, bf16[256,1536]{1,0:T(8,128)(2,1)}) custom-call(bf16[8,128,256]{2,1,0:T(8,128)(2,1)S(1)} %all_to_all.15.after.own_ref, bf16[256,1536]{1,0:T(8,128)(2,1)} %q_hbm.7, bf16[256,1536]{1,0:T(8,128)(2,1)} %k_hbm.7, ...), custom_call_target="tpu_custom_call", output_to_operand_aliasing={{0}: (5, {}), {1}: (6, {}), {2}: (7, {})} | custom-call | flops 335544320 | bytes 1835008 | tf_op jit(solution)/shard_map/pallas_call | solution.py:195
  40.5 2.9 %collective-permute-done.other_ref = bf16[8,64,256]{2,1,0:T(8,128)(2,1)S(1)} collective-permute-done((bf16[8,64,256]{2,1,0:T(8,128)(2,1)S(1)}, bf16[8,64,256]{2,1,0:T(8,128)(2,1)S(1)}, u32[]{:S(2)}, u32[]{:S(2)}) %collective-permute-start) | collective-permute-done | bytes 262176 | tf_op jit(solution)/shard_map/ppermute | solution.py:404
  43.4 1.4 %shard_map.81 = (bf16[8,64,128]{2,1,0:T(8,128)(2,1)S(1)}, f32[512,256]{1,0:T(8,128)S(1)}, bf16[8,16,128]{2,1,0:T(8,128)(2,1)S(1)}) custom-call(bf16[8,128,256]{2,1,0:T(8,128)(2,1)S(1)} %all_to_all.15.after.own_ref, bf16[8,64,256]{2,1,0:T(8,128)(2,1)S(1)} %collective-permute-done.other_ref, bf16[256,1536]{1,0:T(8,128)(2,1)} %get-tuple-element.19.after.nq), custom_call_target="tpu_custom_call" | custom-call | flops 671088640 | tf_op jit(solution)/shard_map/pallas_call | solution.py:407
  44.8 1.4 %collective-permute-done.1.query_ref = bf16[8,64,256]{2,1,0:T(8,128)(2,1)S(1)} collective-permute-done((bf16[8,64,256]{2,1,0:T(8,128)(2,1)S(1)}, bf16[8,64,256]{2,1,0:T(8,128)(2,1)S(1)}, u32[]{:S(2)}, u32[]{:S(2)}) %collective-permute-start.1) | collective-permute-done | bytes 262176 | tf_op jit(solution)/shard_map/ppermute | solution.py:405
  46.2 14.7 %all_to_all.16.got_ref = bf16[8,64,384]{2,1,0:T(8,128)(2,1)S(1)} all-to-all(bf16[8,64,384]{2,1,0:T(8,128)(2,1)S(1)} %shard_map.82), channel_id=1, replica_groups={{8,10,12,4,6,0,2,14},{9,11,13,5,7,1,3,15},{24,26,28,20,22,16,18,30},{25..., dimensions={0} | all-to-all | bytes 786432 | tf_op jit(solution)/shard_map/all_to_all | solution.py:427
  60.9 1.5 %shard_map.83 = (bf16[256,1536]{1,0:T(8,128)(2,1)}, bf16[256,1536]{1,0:T(8,128)(2,1)}, bf16[256,1536]{1,0:T(8,128)(2,1)}) custom-call(s32[8,256]{1,0:T(8,128)S(1)} %get-tuple-element.14.off_ref, bf16[8,64,384]{2,1,0:T(8,128)(2,1)S(1)} %all_to_all.16.got_ref, ...), custom_call_target="tpu_custom_call", output_to_operand_aliasing={{0}: (2, {}), {1}: (3, {}), {2}: (4, {})} | custom-call | tf_op jit(solution)/shard_map/pallas_call | solution.py:429
  (2 shorter events, 0.0 us)
Async XLA Ops:
  2.6 9.7 %all-to-all-start = ((bf16[16,16,256]{2,1,0:T(8,128)(2,1)}), bf16[16,16,256]{2,1,0:T(8,128)(2,1)S(1)}, u32[]{:S(2)}, u32[]{:S(2)}) async-start(bf16[16,16,256]{2,1,0:T(8,128)(2,1)} %get-tuple-element.15), calls=%async_computation | async-start | bytes 262144 | tf_op jit(solution)/shard_map/all_to_all | solution.py:377
  34.4 9.0 %collective-permute-start = (bf16[8,64,256]{2,1,0:T(8,128)(2,1)S(1)}, bf16[8,64,256]{2,1,0:T(8,128)(2,1)S(1)}, u32[]{:S(2)}, u32[]{:S(2)}) collective-permute-start(bf16[8,64,256]{2,1,0:T(8,128)(2,1)S(1)} %get-tuple-element.26), channel_id=1, source_target_pairs={{0,1},{1,0},{2,3},{3,2},{4,5},{5,4},{6,7},{7,6},{8,9},{9,8},{10,11... | collective-permute-start | bytes 786440 | tf_op jit(solution)/shard_map/ppermute | solution.py:404
  37.4 8.8 %collective-permute-start.1 = (bf16[8,64,256]{2,1,0:T(8,128)(2,1)S(1)}, bf16[8,64,256]{2,1,0:T(8,128)(2,1)S(1)}, u32[]{:S(2)}, u32[]{:S(2)}) collective-permute-start(bf16[8,64,256]{2,1,0:T(8,128)(2,1)S(1)} %get-tuple-element.25), channel_id=1, source_target_pairs={{0,1},{1,0},{2,3},{3,2},{4,5},{5,4},{6,7},{7,6},{8,9},{9,8},{10,11... | collective-permute-start | bytes 786440 | tf_op jit(solution)/shard_map/ppermute | solution.py:405
